TPU v7x, 32 devices: a whole 2x2x4 slice. The times are simulated.
32 devices in a mesh: dp: 8 (over y, x, core), head: 4 (over z).
Axes of the slice: x: 2, y: 2, z: 4, core: 2. Of those that a mesh axis runs over, the one named last changes fastest.
Arguments:
- tokens: bfloat16 [8, 2048, 2048], P('dp', 'head'), may hold values from -6 to 6
- lengths: int32 [8], P('dp'), may hold values from 1024 to 2048, as said below
- gain_attn: float32 [2048], replicated, may hold values from 0.5 to 1.5
- w_query: bfloat16 [2048, 2048], P('dp', 'head'), may hold values from -0.125 to 0.125
- w_key: bfloat16 [2048, 2048], P('dp', 'head'), may hold values from -0.125 to 0.125
- w_value: bfloat16 [2048, 4096], P('dp', 'head'), may hold values from -0.125 to 0.125
- w_decay: bfloat16 [2048, 16], P('dp', 'head'), may hold values from -0.125 to 0.125
- w_beta: bfloat16 [2048, 16], P('dp', 'head'), may hold values from -0.125 to 0.125
- w_gate_out: bfloat16 [2048, 4096], P('dp', 'head'), may hold values from -0.125 to 0.125
- conv_query: float32 [4, 2048], replicated, may hold values from -3 to 3
- conv_key: float32 [4, 2048], replicated, may hold values from -3 to 3
- conv_value: float32 [4, 4096], replicated, may hold values from -3 to 3
- decay_log: float32 [16], replicated, may hold values from -6.9 to -3
- decay_bias: float32 [16], replicated, may hold values from -2 to 1
- gain_head: float32 [256], replicated, may hold values from 0.5 to 1.5
- w_out: bfloat16 [2048, 4096], P('dp', 'head'), may hold values from -0.1875 to 0.1875
- gain_mlp: float32 [2048], replicated, may hold values from 0.5 to 1.5
- w_gate: bfloat16 [2048, 5632], P('dp', 'head'), may hold values from -0.125 to 0.125
- w_up: bfloat16 [2048, 5632], P('dp', 'head'), may hold values from -0.125 to 0.125
- w_down: bfloat16 [2048, 5632], P('dp', 'head'), may hold values from -0.078125 to 0.078125
- cotangent: bfloat16 [8, 2048, 2048], P('dp', 'head'), may hold values from -6 to 6
Outputs:
- mixed_rows: bfloat16 [8, 2048, 2048], P('dp', 'head')
- tokens_grad: bfloat16 [8, 2048, 2048], P('dp', 'head')
- grad_gain_attn: float32 [2048], replicated
- grad_w_query: float32 [2048, 2048], P('dp', 'head')
- grad_w_key: float32 [2048, 2048], P('dp', 'head')
- grad_w_value: float32 [2048, 4096], P('dp', 'head')
- grad_w_decay: float32 [2048, 16], P('dp', 'head')
- grad_w_beta: float32 [2048, 16], P('dp', 'head')
- grad_w_gate_out: float32 [2048, 4096], P('dp', 'head')
- grad_conv_query: float32 [4, 2048], replicated
- grad_conv_key: float32 [4, 2048], replicated
- grad_conv_value: float32 [4, 4096], replicated
- grad_decay_log: float32 [16], replicated
- grad_decay_bias: float32 [16], replicated
- grad_gain_head: float32 [256], replicated
- grad_w_out: float32 [2048, 4096], P('dp', 'head')
- grad_gain_mlp: float32 [2048], replicated
- grad_w_gate: float32 [2048, 5632], P('dp', 'head')
- grad_w_up: float32 [2048, 5632], P('dp', 'head')
- grad_w_down: float32 [2048, 5632], P('dp', 'head')
Inputs may be any that keep to these rules, and one draw needn't show every extreme that they name: `lengths`: in every aligned pair of rows (rows 0 and 1, 2 and 3, and so on) one row has all 2048 positions valid.
All inputs are finite; a program needn't handle non-finite values.
Results may differ from a plain program's by a relative error of at most 0.02.
Values may be sent and summed in bfloat16 or wider, within the bound.
No kernel may reach another device: no remote copies, remote signals or barrier semaphores. Data moves between devices by JAX's collectives and lax.ppermute only.
A program may use at most 448 MiB of HBM per device.

v0:
```python
import jax
import jax.numpy as jnp
from jax import lax
from jax.sharding import PartitionSpec as P

DK = 128
DV = 256
SPAN = 64


NORM_EPS = 1e-06


def rms_norm(values_in, gain_vec):
    return (
        values_in
        * lax.rsqrt(jnp.mean(values_in * values_in, axis=-1, keepdims=True) + NORM_EPS)
        * gain_vec
    )


def causal_conv(signal, kernel):
    tap_count = kernel.shape[0]
    length = signal.shape[1]
    padded = jnp.pad(signal, ((0, 0), (tap_count - 1, 0), (0, 0)))
    result = jnp.zeros_like(signal)
    for offset in range(tap_count):
        result = result + kernel[offset] * padded[:, offset : offset + length]
    return result


def unit_lower_inverse(system):
    highest = lax.Precision.HIGHEST
    lead = system.shape[:-2]
    order = system.shape[-1]
    blocks = jnp.ones(lead + (order, 1, 1), jnp.float32)
    size = 1
    while size < order:
        count = order // (2 * size)
        tiles = system.reshape(lead + (count, 2 * size, count, 2 * size))
        tiles = jnp.moveaxis(jnp.diagonal(tiles, axis1=-4, axis2=-2), -1, -3)
        lower_left = tiles[..., size:, :size]
        upper = blocks[..., 0::2, :, :]
        bottom = blocks[..., 1::2, :, :]
        corner = -jnp.matmul(
            jnp.matmul(bottom, lower_left, precision=highest), upper, precision=highest
        )
        zeros = jnp.zeros_like(corner)
        top_row = jnp.concatenate([upper, zeros], axis=-1)
        bottom_row = jnp.concatenate([corner, bottom], axis=-1)
        blocks = jnp.concatenate([top_row, bottom_row], axis=-2)
        size = size * 2
    return blocks.reshape(lead + (order, order))


def span_step(states, block_in):
    queries, keys_in, values, decays, betas = block_in
    highest = lax.Precision.HIGHEST
    cumulative = jnp.cumsum(decays, axis=0)
    cum_heads = cumulative.T
    positions = jnp.arange(SPAN)
    inclusive = positions[:, None] >= positions[None, :]
    strictly = positions[:, None] > positions[None, :]
    spread = cum_heads[:, :, None] - cum_heads[:, None, :]
    within = jnp.where(inclusive, jnp.exp(jnp.where(inclusive, spread, 0.0)), 0.0)
    below = jnp.where(strictly, within, 0.0)
    key_gram = jnp.einsum("ihd,jhd->hij", keys_in, keys_in, precision=highest)
    system = jnp.eye(SPAN, dtype=jnp.float32) + betas.T[:, :, None] * key_gram * below
    leading = jnp.exp(cumulative)
    inverse = unit_lower_inverse(system)
    w_part = jnp.einsum(
        "hij,jhd->ihd", inverse, (betas * leading)[:, :, None] * keys_in, precision=highest
    )
    u_part = jnp.einsum("hij,jhe->ihe", inverse, betas[:, :, None] * values, precision=highest)
    fresh = u_part - jnp.einsum("chd,hde->che", w_part, states, precision=highest)
    scores = jnp.einsum("ihd,jhd->hij", queries, keys_in, precision=highest) * within
    outputs = jnp.einsum("chd,hde->che", queries * leading[:, :, None], states, precision=highest)
    outputs = outputs + jnp.einsum("hij,jhe->ihe", scores, fresh, precision=highest)
    outputs = outputs * DK ** (-0.5)
    remaining = jnp.exp(cumulative[-1:] - cumulative)
    states = leading[-1][:, None, None] * states + jnp.einsum(
        "chd,che->hde", keys_in * remaining[:, :, None], fresh, precision=highest
    )
    return (states, outputs)


def gdn_row(queries, keys_in, values, decays, betas):
    length = queries.shape[0]
    head_count = queries.shape[1]
    block_count = length // SPAN
    blocks_all = (
        queries.reshape(block_count, SPAN, head_count, DK),
        keys_in.reshape(block_count, SPAN, head_count, DK),
        values.reshape(block_count, SPAN, head_count, DV),
        decays.reshape(block_count, SPAN, head_count),
        betas.reshape(block_count, SPAN, head_count),
    )
    states = jnp.zeros((head_count, DK, DV), jnp.float32)
    _, outputs = lax.scan(jax.checkpoint(span_step), states, blocks_all)
    return outputs.reshape(length, head_count, DV)


def mixer(
    pre_query,
    pre_key,
    pre_value,
    pre_decay,
    pre_beta,
    pre_gate,
    conv_q,
    conv_k,
    conv_v,
    log_rates,
    rate_bias,
    gain_vec,
):
    row_count, length, head_count = pre_decay.shape
    queries = jax.nn.silu(causal_conv(pre_query, conv_q)).reshape(row_count, length, head_count, DK)
    queries = queries * lax.rsqrt(jnp.sum(queries * queries, axis=-1, keepdims=True) + NORM_EPS)
    keys_in = jax.nn.silu(causal_conv(pre_key, conv_k)).reshape(row_count, length, head_count, DK)
    keys_in = keys_in * lax.rsqrt(jnp.sum(keys_in * keys_in, axis=-1, keepdims=True) + NORM_EPS)
    values = jax.nn.silu(causal_conv(pre_value, conv_v)).reshape(row_count, length, head_count, DV)
    betas = jax.nn.sigmoid(pre_beta)
    decays = -jnp.exp(log_rates) * jax.nn.softplus(pre_decay + rate_bias)
    recurrent = jax.vmap(gdn_row)(queries, keys_in, values, decays, betas)
    gated = rms_norm(recurrent, gain_vec) * jax.nn.silu(
        pre_gate.reshape(row_count, length, head_count, DV)
    )
    return gated.reshape(row_count, length, head_count * DV)


def place_slice(whole_like, part_in, start_at, axis_dim):
    return lax.dynamic_update_slice_in_dim(jnp.zeros_like(whole_like), part_in, start_at, axis_dim)


def per_device(
    tokens,
    lengths,
    gain_attn,
    w_query,
    w_key,
    w_value,
    w_decay,
    w_beta,
    w_gate_out,
    conv_query,
    conv_key,
    conv_value,
    decay_log,
    decay_bias,
    gain_head,
    w_out,
    gain_mlp,
    w_gate,
    w_up,
    w_down,
    cotangent,
):
    row_count, piece_len, model_width = tokens.shape
    head_devices = lax.axis_size("head")
    head_index = lax.axis_index("head")
    length = piece_len * head_devices
    local_heads = w_decay.shape[1]
    tokens_all = row_count * length
    positions = head_index * piece_len + jnp.arange(piece_len, dtype=jnp.int32)
    mask_piece = (positions[None, :] < lengths[:, None]).astype(jnp.float32)[:, :, None]
    contract_rows = (((0,), (0,)), ((), ()))
    contract_cols = (((1,), (1,)), ((), ()))
    gathered = (
        lax.all_gather(w_query, "dp", axis=0, tiled=True),
        lax.all_gather(w_key, "dp", axis=0, tiled=True),
        lax.all_gather(w_value, "dp", axis=0, tiled=True),
        lax.all_gather(w_decay, "dp", axis=0, tiled=True),
        lax.all_gather(w_beta, "dp", axis=0, tiled=True),
        lax.all_gather(w_gate_out, "dp", axis=0, tiled=True),
        lax.all_gather(w_out, "dp", axis=0, tiled=True),
        lax.all_gather(w_gate, "dp", axis=0, tiled=True),
        lax.all_gather(w_up, "dp", axis=0, tiled=True),
        lax.all_gather(w_down, "dp", axis=0, tiled=True),
    )
    (
        wq_full,
        wk_full,
        wv_full,
        wa_full,
        wb_full,
        wg_full,
        wo_full,
        wgate_full,
        wup_full,
        wdown_full,
    ) = gathered
    project_weights = (wq_full, wk_full, wv_full, wa_full, wb_full, wg_full)
    inputs32 = tokens.astype(jnp.float32)
    normed, norm_back = jax.vjp(rms_norm, inputs32, gain_attn)
    normed_all = lax.all_gather(normed.astype(jnp.bfloat16), "head", axis=1, tiled=True).reshape(
        tokens_all, model_width
    )
    projected = tuple(
        (
            jnp.dot(normed_all, weight, preferred_element_type=jnp.float32).reshape(
                row_count, length, weight.shape[1]
            )
            for weight in project_weights
        )
    )
    key_start = head_index * local_heads * DK
    value_start = head_index * local_heads * DV
    head_start = head_index * local_heads
    conv_q_local = lax.dynamic_slice_in_dim(conv_query, key_start, local_heads * DK, 1)
    conv_k_local = lax.dynamic_slice_in_dim(conv_key, key_start, local_heads * DK, 1)
    conv_v_local = lax.dynamic_slice_in_dim(conv_value, value_start, local_heads * DV, 1)
    log_local = lax.dynamic_slice_in_dim(decay_log, head_start, local_heads, 0)
    bias_local = lax.dynamic_slice_in_dim(decay_bias, head_start, local_heads, 0)
    mixed, mixer_back = jax.vjp(
        mixer,
        projected[0],
        projected[1],
        projected[2],
        projected[3],
        projected[4],
        projected[5],
        conv_q_local,
        conv_k_local,
        conv_v_local,
        log_local,
        bias_local,
        gain_head,
    )
    mixed_low = mixed.reshape(tokens_all, local_heads * DV).astype(jnp.bfloat16)
    partial_attn = lax.dot_general(
        mixed_low, wo_full, contract_cols, preferred_element_type=jnp.float32
    )
    attended = lax.psum_scatter(
        partial_attn.reshape(row_count, length, model_width).astype(jnp.bfloat16),
        "head",
        scatter_dimension=1,
        tiled=True,
    ).astype(jnp.float32)
    middle = inputs32 + mask_piece * attended
    normed_two, norm_two_back = jax.vjp(rms_norm, middle, gain_mlp)
    second_all = lax.all_gather(
        normed_two.astype(jnp.bfloat16), "head", axis=1, tiled=True
    ).reshape(tokens_all, model_width)
    gate_vals = jnp.dot(second_all, wgate_full, preferred_element_type=jnp.float32)
    up_vals = jnp.dot(second_all, wup_full, preferred_element_type=jnp.float32)
    sigmoid_gate = jax.nn.sigmoid(gate_vals)
    activated = gate_vals * sigmoid_gate
    hidden_low = (activated * up_vals).astype(jnp.bfloat16)
    partial_mlp = lax.dot_general(
        hidden_low, wdown_full, contract_cols, preferred_element_type=jnp.float32
    )
    mlp_out = lax.psum_scatter(
        partial_mlp.reshape(row_count, length, model_width).astype(jnp.bfloat16),
        "head",
        scatter_dimension=1,
        tiled=True,
    ).astype(jnp.float32)
    mixed_rows = (middle + mask_piece * mlp_out).astype(jnp.bfloat16)
    cot32 = cotangent.astype(jnp.float32)
    grad_mlp = (mask_piece * cot32).astype(jnp.bfloat16)
    grad_mlp_all = lax.all_gather(grad_mlp, "head", axis=1, tiled=True).reshape(
        tokens_all, model_width
    )
    grad_hidden = jnp.dot(grad_mlp_all, wdown_full, preferred_element_type=jnp.float32)
    grad_wdown = lax.dot_general(
        grad_mlp_all, hidden_low, contract_rows, preferred_element_type=jnp.float32
    )
    grad_gate = (
        grad_hidden * up_vals * sigmoid_gate * (1.0 + gate_vals * (1.0 - sigmoid_gate))
    ).astype(jnp.bfloat16)
    grad_up = (grad_hidden * activated).astype(jnp.bfloat16)
    grad_wgate = lax.dot_general(
        second_all, grad_gate, contract_rows, preferred_element_type=jnp.float32
    )
    grad_wup = lax.dot_general(
        second_all, grad_up, contract_rows, preferred_element_type=jnp.float32
    )
    part_two = lax.dot_general(
        grad_gate, wgate_full, contract_cols, preferred_element_type=jnp.float32
    )
    part_two = part_two + lax.dot_general(
        grad_up, wup_full, contract_cols, preferred_element_type=jnp.float32
    )
    grad_normed_two = lax.psum_scatter(
        part_two.reshape(row_count, length, model_width).astype(jnp.bfloat16),
        "head",
        scatter_dimension=1,
        tiled=True,
    ).astype(jnp.float32)
    grad_middle_norm, grad_gain_mlp = norm_two_back(grad_normed_two)
    grad_middle = cot32 + grad_middle_norm
    grad_attn = (mask_piece * grad_middle).astype(jnp.bfloat16)
    grad_attn_all = lax.all_gather(grad_attn, "head", axis=1, tiled=True).reshape(
        tokens_all, model_width
    )
    grad_mixed = jnp.dot(grad_attn_all, wo_full, preferred_element_type=jnp.float32).reshape(
        row_count, length, local_heads * DV
    )
    grad_wout = lax.dot_general(
        grad_attn_all, mixed_low, contract_rows, preferred_element_type=jnp.float32
    )
    mixer_grads = mixer_back(grad_mixed)
    grad_pre = tuple(
        (item.reshape(tokens_all, item.shape[2]).astype(jnp.bfloat16) for item in mixer_grads[:6])
    )
    part_one = jnp.zeros((tokens_all, model_width), jnp.float32)
    for grad_item, weight in zip(grad_pre, project_weights):
        part_one = part_one + lax.dot_general(
            grad_item, weight, contract_cols, preferred_element_type=jnp.float32
        )
    mixer_wgrads = tuple(
        (
            lax.dot_general(
                normed_all, grad_item, contract_rows, preferred_element_type=jnp.float32
            )
            for grad_item in grad_pre
        )
    )
    grad_normed = lax.psum_scatter(
        part_one.reshape(row_count, length, model_width).astype(jnp.bfloat16),
        "head",
        scatter_dimension=1,
        tiled=True,
    ).astype(jnp.float32)
    grad_inputs_norm, grad_gain_attn = norm_back(grad_normed)
    tokens_grad = (grad_middle + grad_inputs_norm).astype(jnp.bfloat16)
    small_sums = lax.psum(
        (
            grad_gain_attn,
            grad_gain_mlp,
            mixer_grads[11],
            place_slice(conv_query, mixer_grads[6], key_start, 1),
            place_slice(conv_key, mixer_grads[7], key_start, 1),
            place_slice(conv_value, mixer_grads[8], value_start, 1),
            place_slice(decay_log, mixer_grads[9], head_start, 0),
            place_slice(decay_bias, mixer_grads[10], head_start, 0),
        ),
        ("dp", "head"),
    )
    shards_all = (
        lax.psum_scatter(
            mixer_wgrads[0].astype(jnp.bfloat16), "dp", scatter_dimension=0, tiled=True
        ).astype(jnp.float32),
        lax.psum_scatter(
            mixer_wgrads[1].astype(jnp.bfloat16), "dp", scatter_dimension=0, tiled=True
        ).astype(jnp.float32),
        lax.psum_scatter(
            mixer_wgrads[2].astype(jnp.bfloat16), "dp", scatter_dimension=0, tiled=True
        ).astype(jnp.float32),
        lax.psum_scatter(
            mixer_wgrads[3].astype(jnp.bfloat16), "dp", scatter_dimension=0, tiled=True
        ).astype(jnp.float32),
        lax.psum_scatter(
            mixer_wgrads[4].astype(jnp.bfloat16), "dp", scatter_dimension=0, tiled=True
        ).astype(jnp.float32),
        lax.psum_scatter(
            mixer_wgrads[5].astype(jnp.bfloat16), "dp", scatter_dimension=0, tiled=True
        ).astype(jnp.float32),
        lax.psum_scatter(
            grad_wout.astype(jnp.bfloat16), "dp", scatter_dimension=0, tiled=True
        ).astype(jnp.float32),
        lax.psum_scatter(
            grad_wgate.astype(jnp.bfloat16), "dp", scatter_dimension=0, tiled=True
        ).astype(jnp.float32),
        lax.psum_scatter(
            grad_wup.astype(jnp.bfloat16), "dp", scatter_dimension=0, tiled=True
        ).astype(jnp.float32),
        lax.psum_scatter(
            grad_wdown.astype(jnp.bfloat16), "dp", scatter_dimension=0, tiled=True
        ).astype(jnp.float32),
    )
    return (
        mixed_rows,
        tokens_grad,
        small_sums[0],
        shards_all[0],
        shards_all[1],
        shards_all[2],
        shards_all[3],
        shards_all[4],
        shards_all[5],
        small_sums[3],
        small_sums[4],
        small_sums[5],
        small_sums[6],
        small_sums[7],
        small_sums[2],
        shards_all[6],
        small_sums[1],
        shards_all[7],
        shards_all[8],
        shards_all[9],
    )


def solution(mesh):
    placed = (
        P("dp", "head", None),
        P("dp"),
        P(),
        P("dp", "head"),
        P("dp", "head"),
        P("dp", "head"),
        P("dp", "head"),
        P("dp", "head"),
        P("dp", "head"),
        P(),
        P(),
        P(),
        P(),
        P(),
        P(),
        P("dp", "head"),
        P(),
        P("dp", "head"),
        P("dp", "head"),
        P("dp", "head"),
        P("dp", "head", None),
    )
    return jax.shard_map(
        per_device,
        mesh=mesh,
        in_specs=placed,
        out_specs=(
            P("dp", "head", None),
            P("dp", "head", None),
            P(),
            P("dp", "head"),
            P("dp", "head"),
            P("dp", "head"),
            P("dp", "head"),
            P("dp", "head"),
            P("dp", "head"),
            P(),
            P(),
            P(),
            P(),
            P(),
            P(),
            P("dp", "head"),
            P(),
            P("dp", "head"),
            P("dp", "head"),
            P("dp", "head"),
        ),
        check_vma=False,
    )
```

profile of v0, /device:TPU:0, one launch (start us, length us, event | category | flops | bytes accessed | tf_op | source)
XLA Modules:
  0.0 6670.1 jit_solution(14950002575733610310)
XLA Ops:
  40.6 151.8 %all-gather.13.cloned.1.call-done = bf16[1,2048,2048]{2,1,0:T(8,128)(2,1)} async-done(((bf16[1,512,2048]{2,1,0:T(8,128)(2,1)}), bf16[1,2048,2048]{2,1,0:T(8,128)(2,1)}) %all-gather.13.cloned.1.call-update) | async-done | bytes 8388624 | tf_op jit(solution)/shard_map/all_gather | solution.py:196
  259.6 14.4 fusion.366
  274.1 20.1 fusion.374
  335.9 987.5 %while.45 = (s32[]{:T(128)}, f32[1,4,128,256]{3,2,1,0:T(8,128)S(1)}, f32[32,1,64,4,256]{4,2,3,1,0:T(8,128)}, f32[32,1,4,128,256]{4,3,2,1,0:T(8,128)}, f32[32,1,6...) while((s32[]{:T(128)}, ...), condition=%wide.region_5.6_spmd.clone.clone, body=%wide.region_3.5_spmd.clone.clone.sunk | while | flops 483895232 | bytes 10137082 | solution.py:99
  1356.3 19.7 multiply_convert_fusion.3
  1375.9 14.5 convert_bitcast_fusion.2
  1391.9 143.2 %reduce-scatter.19.cloned.1.call-done = bf16[1,512,2048]{2,1,0:T(8,128)(2,1)} async-done(((bf16[1,2048,2048]{2,1,0:T(8,128)(2,1)}), bf16[1,512,2048]{2,1,0:T(8,128)(2,1)}) %reduce-scatter.19.cloned.1.call-update) | async-done | bytes 2097168 | tf_op jit(solution)/shard_map/reduce_scatter | solution.py:234
  1543.5 37.6 all-gather.29.cloned.1.call-done
  1581.1 151.8 %all-gather.25.cloned.1.call-done = bf16[1,2048,2048]{2,1,0:T(8,128)(2,1)} async-done(((bf16[1,512,2048]{2,1,0:T(8,128)(2,1)}), bf16[1,2048,2048]{2,1,0:T(8,128)(2,1)}) %all-gather.25.cloned.1.call-update) | async-done | bytes 8388624 | tf_op jit(solution)/shard_map/all_gather | solution.py:242
  1732.9 18.7 fusion.346
  1751.5 24.7 all-gather.27.cloned.1.call-done
  1776.2 18.6 fusion.348
  1794.8 26.6 all-gather.31.cloned.1.call-done
  1821.4 151.7 %all-gather.33.cloned.1.call-done = bf16[1,2048,2048]{2,1,0:T(8,128)(2,1)} async-done(((bf16[1,512,2048]{2,1,0:T(8,128)(2,1)}), bf16[1,2048,2048]{2,1,0:T(8,128)(2,1)}) %all-gather.33.cloned.1.call-update) | async-done | bytes 8388624 | tf_op jit(solution)/shard_map/all_gather | solution.py:262
  1973.1 29.4 multiply_convert_fusion
  2002.5 19.5 fusion.485
  2022.0 21.5 fusion.332
  2043.6 142.8 %reduce-scatter.23.cloned.1.call-done = bf16[1,512,2048]{2,1,0:T(8,128)(2,1)} async-done(((bf16[1,2048,2048]{2,1,0:T(8,128)(2,1)}), bf16[1,512,2048]{2,1,0:T(8,128)(2,1)}) %reduce-scatter.23.cloned.1.call-update) | async-done | bytes 2097168 | tf_op jit(solution)/shard_map/reduce_scatter | solution.py:285
  2195.1 19.5 fusion.375
  2214.6 19.1 fusion.378
  2264.6 19.0 fusion.381
  2283.8 61.8 all-gather.35.cloned.1.call-done
  2345.5 22.8 fusion.331
  2411.5 3307.8 %while.44 = (s32[]{:T(128)}, f32[1,4,128,256]{2,3,1,0:T(8,128)S(1)}, f32[32,1,64,4,128]{4,2,3,1,0:T(8,128)}, f32[32,1,64,4,128]{4,2,3,1,0:T(8,128)}, f32[32,1,64...) while((s32[]{:T(128)}, ...), condition=%wide.region_30.31_spmd.clone, body=%wide.region_13.30_spmd.clone.sunk | while | flops 1198955008 | bytes 38982372 | solution.py:99
  5889.9 23.5 multiply_reduce_fusion.10
  5913.5 14.6 broadcast_multiply_fusion
  6021.1 30.5 fusion.384
  6051.6 18.8 convert_bitcast_fusion.1
  6103.8 144.7 %reduce-scatter.25.cloned.1.call-done = bf16[1,512,2048]{2,1,0:T(8,128)(2,1)} async-done(((bf16[1,2048,2048]{2,1,0:T(8,128)(2,1)}), bf16[1,512,2048]{2,1,0:T(8,128)(2,1)}) %reduce-scatter.25.cloned.1.call-update) | async-done | bytes 2097168 | tf_op jit(solution)/shard_map/reduce_scatter | solution.py:320
  6252.5 143.4 %reduce-scatter.21.cloned.1.call-done = bf16[1,512,2048]{2,1,0:T(8,128)(2,1)} async-done(((bf16[1,2048,2048]{2,1,0:T(8,128)(2,1)}), bf16[1,512,2048]{2,1,0:T(8,128)(2,1)}) %reduce-scatter.21.cloned.1.call-update) | async-done | bytes 2097168 | tf_op jit(solution)/shard_map/reduce_scatter | solution.py:253
  6403.5 116.7 %all-reduce.61.cloned.1.call-done = f32[4,4096]{1,0:T(4,128)} async-done(((f32[4,4096]{1,0:T(4,128)}), f32[4,4096]{1,0:T(4,128)}) %all-reduce.61.cloned.1.call-update) | async-done | bytes 65552 | tf_op jit(solution)/shard_map/psum | solution.py:328
  6520.2 132.5 %all-reduce.63.cloned.1.call-done = (f32[2048]{0:T(1024)}, f32[4,2048]{1,0:T(4,128)}, f32[4,2048]{1,0:T(4,128)}, f32[16]{0:T(128)}, f32[16]{0:T(128)}, /*index=5*/f32[256]{0:T(256)}, f32[2048]{0:T(1024)}) async-done(((f32[2048]{0:T(1024)}, f32[4,2048]{1,0:T(4,128)}, f32[4,2048]{1,0:T(4,128)}, f32[16]{0:T(128)}, f32[16]{0:T(128)}, /*index=5*/f32[256]{0:T(256)}, f32[2048]{0:T(1024)}), (f32[2048]{0:T(1024)}, ...) | async-done | bytes 83088 | tf_op jit(solution)/shard_map/psum | solution.py:328
  (10128 shorter events, 4801.1 us)
Async XLA Ops:
  7.2 33.4 all-gather.19.cloned.1.call-start
  7.9 184.5 %all-gather.13.cloned.1.call-start = ((), (), s32[]{:S(2)}) async-start(), calls=%async_computation.14 | async-start | bytes 10485760 | tf_op jit(solution)/shard_map/all_gather | solution.py:196
  14.7 205.7 %all-gather.15.cloned.1.call-start = ((), (), s32[]{:S(2)}) async-start(), calls=%async_computation.15 | async-start | bytes 2359296 | tf_op jit(solution)/shard_map/all_gather | solution.py:171
  15.5 244.1 %all-gather.17.cloned.1.call-start = ((), (), s32[]{:S(2)}) async-start(), calls=%async_computation.16 | async-start | bytes 4718592 | tf_op jit(solution)/shard_map/all_gather | solution.py:172
  16.1 1340.2 %all-gather.21.cloned.1.call-start = ((), (), s32[]{:S(2)}) async-start(), calls=%async_computation.18 | async-start | bytes 4718592 | tf_op jit(solution)/shard_map/all_gather | solution.py:175
  16.6 1359.3 %all-gather.23.cloned.1.call-start = ((), (), s32[]{:S(2)}) async-start(), calls=%async_computation.19 | async-start | bytes 4718592 | tf_op jit(solution)/shard_map/all_gather | solution.py:176
  17.2 1517.9 %reduce-scatter.19.cloned.1.call-start = ((), (), s32[]{:S(2)}) async-start(), calls=%async_computation.20 | async-start | bytes 10485760 | tf_op jit(solution)/shard_map/reduce_scatter | solution.py:234
  1390.4 190.6 %all-gather.29.cloned.1.call-start = ((), (), s32[]{:S(2)}) async-start(), calls=%async_computation.23 | async-start | bytes 6488064 | tf_op jit(solution)/shard_map/all_gather | solution.py:178
  1391.2 341.7 %all-gather.25.cloned.1.call-start = ((), (), s32[]{:S(2)}) async-start(), calls=%async_computation.21 | async-start | bytes 10485760 | tf_op jit(solution)/shard_map/all_gather | solution.py:242
  1541.6 234.6 %all-gather.27.cloned.1.call-start = ((), (), s32[]{:S(2)}) async-start(), calls=%async_computation.22 | async-start | bytes 6488064 | tf_op jit(solution)/shard_map/all_gather | solution.py:177
  1542.1 279.3 %all-gather.31.cloned.1.call-start = ((), (), s32[]{:S(2)}) async-start(), calls=%async_computation.24 | async-start | bytes 6488064 | tf_op jit(solution)/shard_map/all_gather | solution.py:179
  1542.9 430.2 %all-gather.33.cloned.1.call-start = ((), (), s32[]{:S(2)}) async-start(), calls=%async_computation.26 | async-start | bytes 10485760 | tf_op jit(solution)/shard_map/all_gather | solution.py:262
  1543.5 643.0 %reduce-scatter.23.cloned.1.call-start = ((), (), s32[]{:S(2)}) async-start(), calls=%async_computation.27 | async-start | bytes 10485760 | tf_op jit(solution)/shard_map/reduce_scatter | solution.py:285
  2043.6 302.0 %all-gather.35.cloned.1.call-start = ((), (), s32[]{:S(2)}) async-start(), calls=%async_computation.28 | async-start | bytes 10485760 | tf_op jit(solution)/shard_map/all_gather | solution.py:294
  2195.0 3875.7 %reduce-scatter.37.cloned.1.call-start = ((), (), s32[]{:S(2)}) async-start(), calls=%async_computation.36 | async-start | bytes 6488064 | tf_op jit(solution)/shard_map/reduce_scatter | solution.py:363
  2214.6 3858.4 %reduce-scatter.39.cloned.1.call-start = ((), (), s32[]{:S(2)}) async-start(), calls=%async_computation.37 | async-start | bytes 6488064 | tf_op jit(solution)/shard_map/reduce_scatter | solution.py:366
  2233.8 3841.6 %reduce-scatter.41.cloned.1.call-start = ((), (), s32[]{:S(2)}) async-start(), calls=%async_computation.38 | async-start | bytes 6488064 | tf_op jit(solution)/shard_map/reduce_scatter | solution.py:369
  2283.7 3795.5 %reduce-scatter.43.cloned.1.call-start = ((), (), s32[]{:S(2)}) async-start(), calls=%async_computation.39 | async-start | bytes 589824
  5777.7 303.1 %reduce-scatter.45.cloned.1.call-start = ((), (), s32[]{:S(2)}) async-start(), calls=%async_computation.40 | async-start | bytes 589824
  5785.9 296.4 %reduce-scatter.29.cloned.1.call-start = ((), (), s32[]{:S(2)}) async-start(), calls=%async_computation.31 | async-start | bytes 2359296 | tf_op jit(solution)/shard_map/reduce_scatter | solution.py:345
  5828.4 255.7 %reduce-scatter.27.cloned.1.call-start = ((), (), s32[]{:S(2)}) async-start(), calls=%async_computation.30 | async-start | bytes 2359296 | tf_op jit(solution)/shard_map/reduce_scatter | solution.py:342
  5864.7 221.3 %reduce-scatter.35.cloned.1.call-start = ((), (), s32[]{:S(2)}) async-start(), calls=%async_computation.35 | async-start | bytes 4718592 | tf_op jit(solution)/shard_map/reduce_scatter | solution.py:360
  5889.8 198.3 %reduce-scatter.31.cloned.1.call-start = ((), (), s32[]{:S(2)}) async-start(), calls=%async_computation.32 | async-start | bytes 4718592 | tf_op jit(solution)/shard_map/reduce_scatter | solution.py:348
  5953.8 147.9 %reduce-scatter.33.cloned.1.call-start = ((), (), s32[]{:S(2)}) async-start(), calls=%async_computation.33 | async-start | bytes 4718592 | tf_op jit(solution)/shard_map/reduce_scatter | solution.py:357
  5968.1 280.4 %reduce-scatter.25.cloned.1.call-start = ((), (), s32[]{:S(2)}) async-start(), calls=%async_computation.29 | async-start | bytes 10485760 | tf_op jit(solution)/shard_map/reduce_scatter | solution.py:320
  6051.6 344.3 %reduce-scatter.21.cloned.1.call-start = ((), (), s32[]{:S(2)}) async-start(), calls=%async_computation.25 | async-start | bytes 10485760 | tf_op jit(solution)/shard_map/reduce_scatter | solution.py:253
  6070.6 449.6 %all-reduce.61.cloned.1.call-start = ((), (), s32[]{:S(2)}) async-start(), calls=%async_computation.34 | async-start | bytes 131072 | tf_op jit(solution)/shard_map/psum | solution.py:328
  6078.5 574.2 %all-reduce.63.cloned.1.call-start = ((), (), s32[]{:S(2)}) async-start(), calls=%async_computation.41 | async-start | bytes 167936 | tf_op jit(solution)/shard_map/psum | solution.py:328
  6085.9 310.0 %copy-start.91 = (f32[2048]{0:T(1024)S(1)}, f32[2048]{0:T(1024)}, u32[]{:S(2)}) copy-start(f32[2048]{0:T(1024)} %param.43) | copy-start | bytes 24580
  6085.9 310.0 %copy-start.95 = (f32[512]{0:T(512)S(1)}, f32[512]{0:T(512)}, u32[]{:S(2)}) copy-start(f32[512]{0:T(512)} %copy-done.93) | copy-start | bytes 6148
  6085.9 310.0 %copy-start.100 = (f32[512]{0:T(512)S(1)}, f32[512]{0:T(512)}, u32[]{:S(2)}) copy-start(f32[512]{0:T(512)} %copy-done.98) | copy-start | bytes 6148
  6086.0 310.0 %copy-start.114 = (f32[512]{0:T(512)S(1)}, f32[512]{0:T(512)}, u32[]{:S(2)}) copy-start(f32[512]{0:T(512)} %copy-done.113) | copy-start | bytes 6148
  (1439 other events, 14225.4 us)
Sparse Core Ops, SparseCore 0:
  9.9 30.6 all-gather.18
  42.8 149.6 all-gather.12
  194.3 26.1 all-gather.14
  222.2 36.7 all-gather.16
  260.7 36.7 all-gather.20
  299.2 36.7 all-gather.22
  1390.5 144.5 reduce-scatter.18
  1537.0 44.0 all-gather.28
  1583.2 149.6 all-gather.24
  1734.6 41.5 all-gather.26
  1778.1 43.3 all-gather.30
  1823.4 149.6 all-gather.32
  2043.7 142.6 reduce-scatter.22
  2195.1 150.3 all-gather.34
  2348.8 57.2 reduce-scatter.36
  2409.8 59.0 reduce-scatter.38
  2472.2 59.0 reduce-scatter.40
  5777.8 31.9 reduce-scatter.42
  5813.5 34.1 reduce-scatter.44
  5851.1 41.2 reduce-scatter.28
  5895.7 41.1 reduce-scatter.26
  5940.6 51.3 reduce-scatter.34
  5995.4 51.2 reduce-scatter.30
  6050.3 51.3 reduce-scatter.32
  6104.0 144.4 reduce-scatter.24
  6250.7 145.1 reduce-scatter.20
  6401.9 118.2 all-reduce.60
  6528.4 124.3 all-reduce.62
where the time goes:
time: 6730 us; the launch traced here: 6670 us
  local copies, waits for them, and re-layouts  2270 us (34%)
  matrix products  1970 us (29%)
  waiting for transfers between devices  1450 us (22%)
  other arithmetic  865 us (13%)
  loops' own time  78.7 us (1%)
    reshape x736, local copies, waits for them, and re-layouts, unit_lower_inverse(): tiles = system.reshape(lead + (count, 2 * size, count, 2 * size))  733 us
    gather x640, local copies, waits for them, and re-layouts, unit_lower_inverse(): tiles = jnp.moveaxis(jnp.diagonal(tiles, axis1=-4, axis2=-2), -1, -3)  476 us
    dot_general x640, matrix products, unit_lower_inverse(): jnp.matmul(jnp.matmul(bottom, lower_left, precision=highest), upper, prec...  386 us
    dot_general x640, matrix products, unit_lower_inverse(): jnp.matmul(bottom, lower_left, precision=highest)  357 us
    scatter-add x160, other arithmetic, unit_lower_inverse(): tiles = jnp.moveaxis(jnp.diagonal(tiles, axis1=-4, axis2=-2), -1, -3)  262 us
    psum x2, waiting for transfers between devices, per_device(): lax.psum((grad_gain_attn, grad_gain_mlp, mixer_grads[11], place_slice(con...  249 us
    transpose x480, local copies, waits for them, and re-layouts, unit_lower_inverse(): tiles = jnp.moveaxis(jnp.diagonal(tiles, axis1=-4, axis2=-2), -1, -3)  211 us
    all_gather x1, waiting for transfers between devices, per_device(): lax.all_gather(normed_two.astype(jnp.bfloat16), 'head', axis=1, tiled=True)  152 us

commit v1 on v0

v1 whole, which is shorter than its diff:
```python
import functools

import jax
import jax.numpy as jnp
from jax import lax
from jax.experimental import pallas as pl
from jax.experimental.pallas import tpu as pltpu
from jax.sharding import PartitionSpec as P

DK = 128
DV = 256
CHUNK = 128
NORM_EPS = 1e-06
BF = jnp.bfloat16
F32 = jnp.float32
NN = (((1,), (0,)), ((), ()))
NT = (((1,), (1,)), ((), ()))
TN = (((0,), (0,)), ((), ()))


def mm(a, b, dims=NN):
    return lax.dot_general(a.astype(BF), b.astype(BF), dims, preferred_element_type=F32)


def split(a):
    high = a.astype(BF)
    return high, (a - high.astype(F32)).astype(BF)


def mm3(a, b, dims=NN):
    ah, al = split(a)
    bh, bl = split(b)
    return mm(ah, bh, dims) + mm(ah, bl, dims) + mm(al, bh, dims)


def exact(a, b, dims=NN):
    return lax.dot_general(a, b, dims, precision=lax.Precision.HIGHEST, preferred_element_type=F32)


def iotas(n):
    return (
        lax.broadcasted_iota(jnp.int32, (n, n), 0),
        lax.broadcasted_iota(jnp.int32, (n, n), 1),
    )


def lower_inverses(lowers):
    n = lowers[0].shape[0]
    row, col = iotas(n)
    eye = (row == col).astype(F32)
    pair = (row // 2 == col // 2).astype(F32)
    inverses = [eye - low * pair for low in lowers]
    size = 2
    while size < n:
        corner = ((row // (2 * size)) == (col // (2 * size))) & ((row // size) != (col // size))
        corner = corner.astype(F32)
        half = [x.astype(BF) for x in inverses]
        inner = [mm(x, low * corner) for x, low in zip(half, lowers)]
        inverses = [x - mm(i, h) for x, i, h in zip(inverses, inner, half)]
        size = size * 2
    residual = [eye - x - mm3(low, x) for low, x in zip(lowers, inverses)]
    return [x + mm(x, r) for x, r in zip(inverses, residual)]


def sigmoid(x):
    return 1.0 / (1.0 + jnp.exp(-x))


def conv_of(buf, taps, sl):
    total = taps[0:1, sl] * buf[5 : 5 + CHUNK, sl]
    for i in range(1, 4):
        total = total + taps[i : i + 1, sl] * buf[5 + i : 5 + i + CHUNK, sl]
    return total


def softplus(x):
    return jnp.maximum(x, 0.0) + jnp.log1p(jnp.exp(-jnp.abs(x)))


def unit(a):
    r = lax.rsqrt(jnp.sum(a * a, axis=-1, keepdims=True) + NORM_EPS)
    return a * r, r


def mixer_forward_kernel(
    heads, pq, pk, pv, pg, ps, cq, ck, cv, rates, bias, gain,
    mixed, t_out, s_out, f_out, bq, bk, bv, state,
):
    step = pl.program_id(1)

    @pl.when(step == 0)
    def _():
        state[...] = jnp.zeros_like(state)
        for b in (bq, bk, bv):
            b[0:8, :] = jnp.zeros((8, b.shape[1]), F32)

    @pl.when(step > 0)
    def _():
        for b in (bq, bk, bv):
            b[0:8, :] = b[CHUNK : CHUNK + 8, :]

    for b, p in ((bq, pq), (bk, pk), (bv, pv)):
        b[8 : CHUNK + 8, :] = p[0].astype(F32)
    row, col = iotas(CHUNK)
    small = ps[0]
    g = rates[...] * softplus(small + bias[...])
    beta_all = sigmoid(small)
    cum = exact((row >= col).astype(F32), g)
    cum_t = cum.T
    hs = range(heads)
    ks = [slice(h * DK, (h + 1) * DK) for h in hs]
    vs = [slice(h * DV, (h + 1) * DV) for h in hs]
    q, k, v, within, kbeta, gamma, rem, last = [], [], [], [], [], [], [], []
    for h in hs:
        a = conv_of(bq, cq, ks[h])
        q.append(unit(a * sigmoid(a))[0])
        a = conv_of(bk, ck, ks[h])
        k.append(unit(a * sigmoid(a))[0])
        a = conv_of(bv, cv, vs[h])
        v.append(a * sigmoid(a))
        gc = cum[:, h : h + 1]
        within.append(jnp.exp(jnp.where(row >= col, gc - cum_t[h : h + 1, :], -1e30)))
        kbeta.append(beta_all[:, heads + h : heads + h + 1])
        gamma.append(jnp.exp(gc))
        tail = cum[CHUNK - 1 : CHUNK, h : h + 1]
        rem.append(jnp.exp(tail - gc))
        last.append(jnp.exp(tail))
    kb = [x.astype(BF) for x in k]
    lowers = [
        jnp.where(row > col, kbeta[h] * (mm(kb[h], kb[h], NT) * within[h]), 0.0) for h in hs
    ]
    scores = [mm(q[h], kb[h], NT) * within[h] for h in hs]
    inv = lower_inverses(lowers)
    states = [state[h] for h in hs]
    sb = [s.astype(BF) for s in states]
    both = [
        mm(jnp.concatenate([gamma[h] * k[h], gamma[h] * q[h]], axis=0), sb[h]) for h in hs
    ]
    fresh = [mm(inv[h], kbeta[h] * (v[h] - both[h][:CHUNK])) for h in hs]
    fb = [x.astype(BF) for x in fresh]
    out = [(both[h][CHUNK:] + mm(scores[h], fb[h])) * DK**-0.5 for h in hs]
    for h in hs:
        state[h] = last[h] * states[h] + mm(rem[h] * k[h], fb[h], TN)
        t_out[0, 0, h] = inv[h].astype(t_out.dtype)
        s_out[0, 0, h] = sb[h]
        f_out[0, :, vs[h]] = fb[h]
        o = out[h]
        r = lax.rsqrt(jnp.mean(o * o, axis=-1, keepdims=True) + NORM_EPS)
        pgh = pg[0, :, vs[h]].astype(F32)
        mixed[0, :, vs[h]] = (o * r * gain[...] * (pgh * sigmoid(pgh))).astype(mixed.dtype)


def mixer_backward_kernel(
    heads, dm, pq, pk, pv, pg, ps, tq, tk, tv, cq, ck, cv, rates, bias, gain, t_in, s_in, f_in,
    gqks, gvg, dcq, dck, dcv, dsm, dgain,
    bq, bk, bv, eq, ek, ev, dstate,
):
    row_at = pl.program_id(0)
    step = pl.program_id(1)
    chunk = pl.num_programs(1) - 1 - step

    @pl.when((row_at == 0) & (step == 0))
    def _():
        for r in (dcq, dck, dcv, dsm, dgain):
            r[...] = jnp.zeros_like(r)

    @pl.when(step == 0)
    def _():
        dstate[...] = jnp.zeros_like(dstate)
        for b in (eq, ek, ev):
            b[CHUNK : CHUNK + 8, :] = jnp.zeros((8, b.shape[1]), F32)

    @pl.when(step > 0)
    def _():
        for b in (eq, ek, ev):
            b[CHUNK : CHUNK + 8, :] = b[0:8, :]

    has_before = (chunk > 0).astype(F32)
    for b, p, t in ((bq, pq, tq), (bk, pk, tk), (bv, pv, tv)):
        b[0:8, :] = t[0].astype(F32) * has_before
        b[8 : CHUNK + 8, :] = p[0].astype(F32)
    row, col = iotas(CHUNK)
    lane = col
    small = ps[0]
    shifted = small + bias[...]
    g = rates[...] * softplus(shifted)
    beta_all = sigmoid(small)
    cum = exact((row >= col).astype(F32), g)
    cum_t = cum.T
    hs = range(heads)
    ks = [slice(h * DK, (h + 1) * DK) for h in hs]
    vs = [slice(h * DV, (h + 1) * DV) for h in hs]
    scale = DK**-0.5
    dcum = jnp.zeros((CHUNK, CHUNK), F32)
    dcum_rows = jnp.zeros((CHUNK, CHUNK), F32)
    dbeta = jnp.zeros((CHUNK, CHUNK), F32)
    head_dgain = jnp.zeros((1, DV), F32)
    q, k, v, rq, rk, kbeta, gamma, rem, last, within = [], [], [], [], [], [], [], [], [], []
    for h in hs:
        a = conv_of(bq, cq, ks[h])
        x, r = unit(a * sigmoid(a))
        q.append(x)
        rq.append(r)
        a = conv_of(bk, ck, ks[h])
        x, r = unit(a * sigmoid(a))
        k.append(x)
        rk.append(r)
        a = conv_of(bv, cv, vs[h])
        v.append(a * sigmoid(a))
        gc = cum[:, h : h + 1]
        within.append(jnp.exp(jnp.where(row >= col, gc - cum_t[h : h + 1, :], -1e30)))
        kbeta.append(beta_all[:, heads + h : heads + h + 1])
        gamma.append(jnp.exp(gc))
        tail = cum[CHUNK - 1 : CHUNK, h : h + 1]
        rem.append(jnp.exp(tail - gc))
        last.append(jnp.exp(tail))
    qb = [x.astype(BF) for x in q]
    kb = [x.astype(BF) for x in k]
    sb = [s_in[0, 0, h] for h in hs]
    fb = [f_in[0, :, vs[h]] for h in hs]
    tb = [t_in[0, 0, h].astype(BF) for h in hs]
    gram = [mm(kb[h], kb[h], NT) * within[h] for h in hs]
    scores = [mm(qb[h], kb[h], NT) * within[h] for h in hs]
    gk_gq = [
        jnp.concatenate([gamma[h] * k[h], gamma[h] * q[h]], axis=0) for h in hs
    ]
    both = [mm(gk_gq[h], sb[h]) for h in hs]
    x_in = [v[h] - both[h][:CHUNK] for h in hs]
    out = [(both[h][CHUNK:] + mm(scores[h], fb[h])) * scale for h in hs]
    dout = []
    for h in hs:
        o = out[h]
        r = lax.rsqrt(jnp.mean(o * o, axis=-1, keepdims=True) + NORM_EPS)
        n = o * r
        p = pg[0, :, vs[h]].astype(F32)
        s = sigmoid(p)
        d = dm[0, :, vs[h]].astype(F32)
        y = n * gain[...]
        at = heads * DV + h * DV
        gvg[0, :, at : at + DV] = (d * y * (s * (1.0 + p * (1.0 - s)))).astype(BF)
        dy = d * (p * s)
        head_dgain = head_dgain + jnp.sum(dy * n, axis=0, keepdims=True)
        dn = dy * gain[...]
        dout.append(scale * r * (dn - n * jnp.mean(n * dn, axis=-1, keepdims=True)))
    dob = [x.astype(BF) for x in dout]
    ds_next = [dstate[h] for h in hs]
    dsb = [x.astype(BF) for x in ds_next]
    krem = [rem[h] * k[h] for h in hs]
    dfresh = [mm(scores[h], dob[h], TN) + mm(krem[h], dsb[h]) for h in hs]
    dr = [mm(tb[h], dfresh[h], TN) for h in hs]
    drb = [x.astype(BF) for x in dr]
    dx = [kbeta[h] * dr[h] for h in hs]
    dx_do = [jnp.concatenate([-dx[h], dout[h]], axis=0).astype(BF) for h in hs]
    for h in hs:
        dstate[h] = last[h] * ds_next[h] + mm(gk_gq[h], dx_do[h], TN)
    dgk_gq = [mm(dx_do[h], sb[h], NT) for h in hs]
    dkrem = [mm(fb[h], dsb[h], NT) for h in hs]
    dscore = [mm(dob[h], fb[h], NT) for h in hs]
    dlow = [jnp.where(row > col, -mm(drb[h], fb[h], NT), 0.0) for h in hs]
    for h in hs:
        m = dscore[h] * within[h]
        dgram = kbeta[h] * (dlow[h] * within[h])
        lg = dlow[h] * gram[h]
        e = dscore[h] * scores[h] + kbeta[h] * lg
        dq = gamma[h] * dgk_gq[h][CHUNK:] + mm(m, kb[h])
        mk = jnp.concatenate([m, dgram], axis=0)
        dk = (
            gamma[h] * dgk_gq[h][:CHUNK]
            + rem[h] * dkrem[h]
            + mm(mk, jnp.concatenate([qb[h], kb[h]], axis=0), TN)
            + mm(dgram, kb[h])
        )
        rem_part = jnp.sum(dkrem[h] * krem[h], axis=-1, keepdims=True)
        head_dcum = (
            jnp.sum(e, axis=-1, keepdims=True)
            + jnp.sum(
                dgk_gq[h][:CHUNK] * gk_gq[h][:CHUNK] + dgk_gq[h][CHUNK:] * gk_gq[h][CHUNK:],
                axis=-1, keepdims=True,
            )
            - rem_part
        )
        state_part = jnp.sum(
            jnp.sum(ds_next[h] * sb[h].astype(F32), axis=0, keepdims=True), axis=1, keepdims=True
        )
        end_part = jnp.sum(rem_part, axis=0, keepdims=True) + last[h] * state_part
        head_dcum = head_dcum + jnp.where(row[:, 0:1] == CHUNK - 1, end_part, 0.0)
        dcum = dcum + jnp.where(lane == h, head_dcum, 0.0)
        dcum_rows = dcum_rows + jnp.where(row == h, jnp.sum(e, axis=0, keepdims=True), 0.0)
        head_dbeta = jnp.sum(dr[h] * x_in[h], axis=-1, keepdims=True) + jnp.sum(
            lg, axis=-1, keepdims=True
        )
        dbeta = dbeta + jnp.where(lane == heads + h, head_dbeta, 0.0)
        a = conv_of(bq, cq, ks[h])
        s = sigmoid(a)
        da = rq[h] * (dq - q[h] * jnp.sum(q[h] * dq, axis=-1, keepdims=True))
        eq[0:CHUNK, ks[h]] = da * (s * (1.0 + a * (1.0 - s)))
        a = conv_of(bk, ck, ks[h])
        s = sigmoid(a)
        da = rk[h] * (dk - k[h] * jnp.sum(k[h] * dk, axis=-1, keepdims=True))
        ek[0:CHUNK, ks[h]] = da * (s * (1.0 + a * (1.0 - s)))
        a = conv_of(bv, cv, vs[h])
        s = sigmoid(a)
        ev[0:CHUNK, vs[h]] = dx[h] * (s * (1.0 + a * (1.0 - s)))
    dgain[0:1, :] += head_dgain
    dcum = dcum - dcum_rows.T
    dg = exact((row >= col).astype(F32), dcum, TN)
    dshift = dg * rates[...] * sigmoid(shifted)
    dsm[0:1, :] += jnp.sum(dg * g, axis=0, keepdims=True)
    dsm[1:2, :] += jnp.sum(dshift, axis=0, keepdims=True)
    gqks[0, :, 2 * heads * DK :] = (
        jnp.where(lane < heads, dshift, 0.0) + dbeta * beta_all * (1.0 - beta_all)
    ).astype(BF)
    for b, e, taps, dtaps, out_ref, start in (
        (bq, eq, cq, dcq, gqks, 0), (bk, ek, ck, dck, gqks, heads * DK), (bv, ev, cv, dcv, gvg, 0),
    ):
        for at in range(0, b.shape[1], DK):
            sl = slice(at, at + DK)
            own = e[0:CHUNK, sl]
            total = taps[3:4, sl] * own
            for i in range(3):
                total = total + taps[i : i + 1, sl] * e[3 - i : 3 - i + CHUNK, sl]
            out_ref[0, :, start + at : start + at + DK] = total.astype(BF)
            for i in range(4):
                dtaps[i : i + 1, sl] += jnp.sum(
                    own * b[5 + i : 5 + i + CHUNK, sl], axis=0, keepdims=True
                )


def whole_spec(shape):
    return pl.BlockSpec(shape, lambda r, c: (0,) * len(shape))


def lane_pad(vec, at):
    return jnp.zeros((1, 128), F32).at[0, at : at + vec.shape[0]].set(vec)


def mixer_forward(pqks, pvg, cq, ck, cv, log_rates, rate_bias, gain):
    rows, length, value_width = pvg.shape
    value_width = value_width // 2
    key_width = value_width * DK // DV
    heads = key_width // DK
    chunks = length // CHUNK
    seq = lambda width, at=0: pl.BlockSpec((1, CHUNK, width), lambda r, c: (r, c, at))
    per = lambda a, b: pl.BlockSpec((1, 1, heads, a, b), lambda r, c: (r, c, 0, 0, 0))
    return pl.pallas_call(
        functools.partial(mixer_forward_kernel, heads),
        grid=(rows, chunks),
        in_specs=[seq(key_width), seq(key_width, 1), seq(value_width), seq(value_width, 1),
                  seq(128, 2 * heads),
                  whole_spec((4, key_width)), whole_spec((4, key_width)), whole_spec((4, value_width)),
                  whole_spec((1, 128)), whole_spec((1, 128)), whole_spec((1, DV))],
        out_specs=[seq(value_width), per(CHUNK, CHUNK), per(DK, DV), seq(value_width)],
        out_shape=[
            jax.ShapeDtypeStruct((rows, length, value_width), BF),
            jax.ShapeDtypeStruct((rows, chunks, heads, CHUNK, CHUNK), BF),
            jax.ShapeDtypeStruct((rows, chunks, heads, DK, DV), BF),
            jax.ShapeDtypeStruct((rows, length, value_width), BF),
        ],
        scratch_shapes=[
            pltpu.VMEM((CHUNK + 8, key_width), F32),
            pltpu.VMEM((CHUNK + 8, key_width), F32),
            pltpu.VMEM((CHUNK + 8, value_width), F32),
            pltpu.VMEM((heads, DK, DV), F32),
        ],
        compiler_params=pltpu.CompilerParams(
            dimension_semantics=("arbitrary", "arbitrary"), vmem_limit_bytes=40 << 20
        ),
        name="mixer_forward",
    )(pqks, pqks, pvg, pvg, pqks, cq, ck, cv, lane_pad(-jnp.exp(log_rates), 0),
      lane_pad(rate_bias, 0), gain.reshape(1, DV))


def mixer_backward(dm, pqks, pvg, cq, ck, cv, log_rates, rate_bias, gain, t_in, s_in, f_in):
    rows, length, value_width = dm.shape
    key_width = value_width * DK // DV
    heads = key_width // DK
    chunks = length // CHUNK
    seq = lambda width, at=0: pl.BlockSpec(
        (1, CHUNK, width), lambda r, c: (r, chunks - 1 - c, at)
    )
    before = lambda width, at=0: pl.BlockSpec(
        (1, 8, width),
        lambda r, c: (r, jnp.maximum((chunks - 1 - c) * (CHUNK // 8) - 1, 0), at),
    )
    per = lambda a, b: pl.BlockSpec(
        (1, 1, heads, a, b), lambda r, c: (r, chunks - 1 - c, 0, 0, 0)
    )
    seq_shape = lambda width: jax.ShapeDtypeStruct((rows, length, width), BF)
    return pl.pallas_call(
        functools.partial(mixer_backward_kernel, heads),
        grid=(rows, chunks),
        in_specs=[seq(value_width), seq(key_width), seq(key_width, 1), seq(value_width),
                  seq(value_width, 1), seq(128, 2 * heads),
                  before(key_width), before(key_width, 1), before(value_width),
                  whole_spec((4, key_width)), whole_spec((4, key_width)), whole_spec((4, value_width)),
                  whole_spec((1, 128)), whole_spec((1, 128)), whole_spec((1, DV)),
                  per(CHUNK, CHUNK), per(DK, DV), seq(value_width)],
        out_specs=[seq(2 * key_width + 128), seq(2 * value_width),
                   whole_spec((8, key_width)), whole_spec((8, key_width)), whole_spec((8, value_width)),
                   whole_spec((8, 128)), whole_spec((8, DV))],
        out_shape=[seq_shape(2 * key_width + 128), seq_shape(2 * value_width),
                   jax.ShapeDtypeStruct((8, key_width), F32),
                   jax.ShapeDtypeStruct((8, key_width), F32),
                   jax.ShapeDtypeStruct((8, value_width), F32),
                   jax.ShapeDtypeStruct((8, 128), F32),
                   jax.ShapeDtypeStruct((8, DV), F32)],
        scratch_shapes=[
            pltpu.VMEM((CHUNK + 8, key_width), F32),
            pltpu.VMEM((CHUNK + 8, key_width), F32),
            pltpu.VMEM((CHUNK + 8, value_width), F32),
            pltpu.VMEM((CHUNK + 8, key_width), F32),
            pltpu.VMEM((CHUNK + 8, key_width), F32),
            pltpu.VMEM((CHUNK + 8, value_width), F32),
            pltpu.VMEM((heads, DK, DV), F32),
        ],
        compiler_params=pltpu.CompilerParams(
            dimension_semantics=("arbitrary", "arbitrary"), vmem_limit_bytes=48 << 20
        ),
        name="mixer_backward",
    )(dm, pqks, pqks, pvg, pvg, pqks, pqks, pqks, pvg, cq, ck, cv, lane_pad(-jnp.exp(log_rates), 0),
      lane_pad(rate_bias, 0), gain.reshape(1, DV), t_in, s_in, f_in)


GROUP = 0


def ring(size, group):
    return [(i, i // group * group + (i + 1) % group) for i in range(size)]


def swap(size, bit):
    return [(i, i ^ bit) for i in range(size)]


def matmul(a, b, dims=NN):
    return lax.dot_general(a, b, dims, preferred_element_type=F32)


def gather_ring(piece, size, group):
    pieces = [piece]
    for _ in range(group - 1):
        pieces.append(lax.ppermute(pieces[-1], "head", ring(size, group)))
    return pieces


def scatter_ring(part_of, size, group):
    total = part_of(1 % group)
    for s in range(2, group + 1):
        moved = lax.ppermute(total.astype(BF), "head", ring(size, group))
        total = part_of(s % group) + moved.astype(F32)
    return total


def norm_parts(x):
    r = lax.rsqrt(jnp.mean(x * x, axis=-1, keepdims=True) + NORM_EPS)
    return x * r, r


def norm_back(n, r, gain, grad):
    inner = gain * grad
    return r * (inner - n * jnp.mean(n * inner, axis=-1, keepdims=True))


def sum_small(flat, sizes):
    for axis in ("dp", "head"):
        bit = 1
        while bit < sizes[axis]:
            flat = flat + lax.ppermute(flat, axis, swap(sizes[axis], bit))
            bit = bit * 2
    return flat


def per_device(
    tokens,
    lengths,
    gain_attn,
    w_query,
    w_key,
    w_value,
    w_decay,
    w_beta,
    w_gate_out,
    conv_query,
    conv_key,
    conv_value,
    decay_log,
    decay_bias,
    gain_head,
    w_out,
    gain_mlp,
    w_gate,
    w_up,
    w_down,
    cotangent,
):
    rows, piece, width = tokens.shape
    size = lax.axis_size("head")
    me = lax.axis_index("head")
    length = piece * size
    heads = w_decay.shape[1]
    flat_piece = rows * piece
    positions = me * piece + jnp.arange(piece, dtype=jnp.int32)
    mask = (positions[None, :] < lengths[:, None]).astype(F32)[:, :, None]

    def owner(s):
        return lax.rem(me + size - s, size)

    def put(whole, part, s):
        return lax.dynamic_update_slice_in_dim(whole, part, owner(s) * piece, 1)

    def take(whole, s):
        return lax.dynamic_slice_in_dim(whole, owner(s) * piece, piece, 1)

    def gather_weight(w):
        return lax.all_gather(w, "dp", axis=0, tiled=True)

    small_pad = jnp.zeros((w_decay.shape[0], 128 - 2 * heads), BF)
    w_qks = gather_weight(jnp.concatenate([w_query, w_key, w_decay, w_beta, small_pad], axis=1))
    w_vg = gather_weight(jnp.concatenate([w_value, w_gate_out], axis=1))
    wo_full = gather_weight(w_out)
    wgate_full = gather_weight(w_gate)
    wup_full = gather_weight(w_up)
    wdown_full = gather_weight(w_down)

    inputs32 = tokens.astype(F32)
    n_one, r_one = norm_parts(inputs32)
    normed = (n_one * gain_attn).astype(BF)
    normed_pieces = gather_ring(normed, size, size)
    normed_all = jnp.zeros((rows, length, width), BF)
    pqks = jnp.zeros((rows, length, w_qks.shape[1]), F32)
    pvg = jnp.zeros((rows, length, w_vg.shape[1]), F32)
    batch_nn = (((2,), (0,)), ((), ()))
    batch_nt = (((2,), (1,)), ((), ()))
    for s, item in enumerate(normed_pieces):
        pqks = put(pqks, matmul(item, w_qks, batch_nn), s)
        pvg = put(pvg, matmul(item, w_vg, batch_nn), s)
        normed_all = put(normed_all, item, s)

    cq = lax.dynamic_slice_in_dim(conv_query, me * heads * DK, heads * DK, 1)
    ck = lax.dynamic_slice_in_dim(conv_key, me * heads * DK, heads * DK, 1)
    cv = lax.dynamic_slice_in_dim(conv_value, me * heads * DV, heads * DV, 1)
    log_local = lax.dynamic_slice_in_dim(decay_log, me * heads, heads, 0)
    bias_local = lax.dynamic_slice_in_dim(decay_bias, me * heads, heads, 0)
    mixed, t_kept, s_kept, f_kept = mixer_forward(
        pqks, pvg, cq, ck, cv, log_local, bias_local, gain_head
    )
    attended = scatter_ring(
        lambda s: matmul(take(mixed, s), wo_full, batch_nt), size, size
    )
    middle = inputs32 + mask * attended
    n_two, r_two = norm_parts(middle)
    normed_two = (n_two * gain_mlp).astype(BF)
    cot32 = cotangent.astype(F32)
    grad_mlp = (mask * cot32).astype(BF)

    group = GROUP or size
    second = [x.reshape(flat_piece, width) for x in gather_ring(normed_two, size, group)]
    grad_out = [x.reshape(flat_piece, width) for x in gather_ring(grad_mlp, size, group)]
    hidden, grad_gate, grad_up = [], [], []
    for x, g in zip(second, grad_out):
        gate = matmul(x, wgate_full)
        up = matmul(x, wup_full)
        sig = jax.nn.sigmoid(gate)
        act = gate * sig
        hidden.append((act * up).astype(BF))
        back = matmul(g, wdown_full)
        grad_gate.append((back * up * sig * (1.0 + gate * (1.0 - sig))).astype(BF))
        grad_up.append((back * act).astype(BF))
    shape3 = (rows, piece, width)
    grad_normed_two = scatter_ring(
        lambda s: matmul(grad_gate[s], wgate_full, NT) + matmul(grad_up[s], wup_full, NT),
        size, group,
    ).reshape(shape3)
    grad_gain_mlp = jnp.sum(grad_normed_two * n_two, axis=(0, 1))
    grad_middle = cot32 + norm_back(n_two, r_two, gain_mlp, grad_normed_two)
    grad_attn = (mask * grad_middle).astype(BF)
    grad_attn_pieces = gather_ring(grad_attn, size, size)
    grad_mixed = jnp.zeros((rows, length, heads * DV), F32)
    grad_attn_all = jnp.zeros((rows, length, width), BF)
    for s, item in enumerate(grad_attn_pieces):
        grad_mixed = put(grad_mixed, matmul(item, wo_full, batch_nn), s)
        grad_attn_all = put(grad_attn_all, item, s)

    mlp_out = scatter_ring(
        lambda s: matmul(hidden[s], wdown_full, NT), size, group
    ).reshape(shape3)
    mixed_rows = (middle + mask * mlp_out).astype(BF)
    second_all = jnp.concatenate(second, axis=0)
    grad_wdown = matmul(jnp.concatenate(grad_out, axis=0), jnp.concatenate(hidden, axis=0), TN)
    grad_wgate = matmul(second_all, jnp.concatenate(grad_gate, axis=0), TN)
    grad_wup = matmul(second_all, jnp.concatenate(grad_up, axis=0), TN)

    def scatter_weight(g):
        return lax.psum_scatter(g.astype(BF), "dp", scatter_dimension=0, tiled=True).astype(F32)

    out_wdown = scatter_weight(grad_wdown)
    out_wgate = scatter_weight(grad_wgate)
    out_wup = scatter_weight(grad_wup)
    flat = lambda x: x.reshape(rows * length, x.shape[2])
    out_wout = scatter_weight(matmul(flat(grad_attn_all), flat(mixed), TN))

    gqks, gvg, dcq, dck, dcv, dsm, dgain = mixer_backward(
        grad_mixed, pqks, pvg, cq, ck, cv, log_local, bias_local, gain_head,
        t_kept, s_kept, f_kept,
    )
    gain_sums = []

    def part_one(s):
        part = matmul(take(gqks, s), w_qks, batch_nt) + matmul(take(gvg, s), w_vg, batch_nt)
        gain_sums.append(jnp.sum(part * take(normed_all, s).astype(F32), axis=(0, 1)))
        return part

    grad_normed = scatter_ring(part_one, size, size)
    out_qks = scatter_weight(matmul(flat(normed_all), flat(gqks), TN))
    out_vg = scatter_weight(matmul(flat(normed_all), flat(gvg), TN))
    tokens_grad = (grad_middle + norm_back(n_one, r_one, gain_attn, grad_normed)).astype(BF)

    def spread(part, axis):
        shape = part.shape[:axis] + (size,) + part.shape[axis:]
        whole = jnp.zeros(shape, F32)
        whole = lax.dynamic_update_slice_in_dim(whole, jnp.expand_dims(part, axis), me, axis)
        return whole.reshape(part.shape[:axis] + (size * part.shape[axis],) + part.shape[axis + 1 :])

    small = (
        sum(gain_sums) / gain_attn,
        grad_gain_mlp,
        dgain[0],
        spread(dcq[:4], 1),
        spread(dck[:4], 1),
        spread(dcv[:4], 1),
        spread(dsm[0, :heads], 0),
        spread(dsm[1, :heads], 0),
    )
    lane_sizes = [x.size for x in small]
    total = sum(lane_sizes)
    padded = -(-total // 1024) * 1024
    packed = jnp.concatenate(
        [x.reshape(-1) for x in small] + [jnp.zeros((padded - total,), F32)]
    ).reshape(padded // 128, 128)
    packed = sum_small(packed, {"dp": lax.axis_size("dp"), "head": size}).reshape(-1)
    sums = []
    at = 0
    for x in small:
        sums.append(packed[at : at + x.size].reshape(x.shape))
        at = at + x.size
    key_width = heads * DK
    value_width = heads * DV
    return (
        mixed_rows,
        tokens_grad,
        sums[0],
        out_qks[:, :key_width],
        out_qks[:, key_width : 2 * key_width],
        out_vg[:, :value_width],
        out_qks[:, 2 * key_width : 2 * key_width + heads],
        out_qks[:, 2 * key_width + heads : 2 * key_width + 2 * heads],
        out_vg[:, value_width:],
        sums[3],
        sums[4],
        sums[5],
        sums[6],
        sums[7],
        sums[2],
        out_wout,
        sums[1],
        out_wgate,
        out_wup,
        out_wdown,
    )


def solution(mesh):
    rows = P("dp", "head", None)
    weight = P("dp", "head")
    same = P()
    return jax.shard_map(
        per_device,
        mesh=mesh,
        in_specs=(
            rows, P("dp"), same, weight, weight, weight, weight, weight, weight, same, same, same,
            same, same, same, weight, same, weight, weight, weight, rows,
        ),
        out_specs=(
            rows, rows, same, weight, weight, weight, weight, weight, weight, same, same, same,
            same, same, same, weight, same, weight, weight, weight,
        ),
        check_vma=False,
    )
```

time: 6730 us -> 1460 us (0.22)
  local copies, waits for them, and re-layouts: 2270 us -> 74.2 us
  matrix products: 1970 us -> 410 us
  other arithmetic: 865 us -> 49.5 us
  waiting for transfers between devices: 1450 us -> 738 us
  Pallas kernels: 0 us -> 162 us
  loops' own time: 78.7 us -> 0 us
    dot_general x2238 -> x54, matrix products: 1970 us -> 410 us  [matmul(): return lax.dot_general(a, b, dims, preferred_element_type=F32)]
    reshape x774 -> x6, local copies, waits for them, and re-layouts: 768 us -> 6.45 us  [the longest x1 4.36 us: per_device(): flat = lambda x: x.reshape(rows * length, x.shape[2])]
    ppermute x0 -> x29, waiting for transfers between devices: none -> 737 us  [the longest x12 429 us: gather_ring(): pieces.append(lax.ppermute(pieces[-1], 'head', ring(size, group)))]
    all_gather x12 -> x6, waiting for transfers between devices: 608 us -> 0.03 us  [gather_weight(): return lax.all_gather(w, 'dp', axis=0, tiled=True)]
    reduce_scatter x12 -> x6, waiting for transfers between devices: 586 us -> 0.03 us  [scatter_weight(): lax.psum_scatter(g.astype(BF), 'dp', scatter_dimension=0, tiled=True)]
    gather x640 -> x0, local copies, waits for them, and re-layouts: 476 us -> none  [unit_lower_inverse(): tiles = jnp.moveaxis(jnp.diagonal(tiles, axis1=-4, axis2=-2), -1, -3)]
    scatter-add x160 -> x0, other arithmetic: 262 us -> none  [unit_lower_inverse(): tiles = jnp.moveaxis(jnp.diagonal(tiles, axis1=-4, axis2=-2), -1, -3)]
    psum x2 -> x0, waiting for transfers between devices: 249 us -> none  [per_device(): lax.psum((grad_gain_attn, grad_gain_mlp, mixer_grads[11], place_slice(con...]
where the time goes in v1:
time: 1460 us
  waiting for transfers between devices  738 us (51%)
  matrix products  410 us (28%)
  Pallas kernels  162 us (11%)
  local copies, waits for them, and re-layouts  74.2 us (5%)
  other arithmetic  49.5 us (3%)
  between operations  16.5 us (1%)
    ppermute x12, waiting for transfers between devices, gather_ring(): pieces.append(lax.ppermute(pieces[-1], 'head', ring(size, group)))  429 us
    dot_general x54, matrix products, matmul(): return lax.dot_general(a, b, dims, preferred_element_type=F32)  410 us
    ppermute x12, waiting for transfers between devices, scatter_ring(): moved = lax.ppermute(total.astype(BF), 'head', ring(size, group))  296 us
    pallas_call x1, Pallas kernels, mixer_backward(): pl.pallas_call(functools.partial(mixer_backward_kernel, heads), grid=(row...  97.7 us
    pallas_call x1, Pallas kernels, mixer_forward(): pl.pallas_call(functools.partial(mixer_forward_kernel, heads), grid=(rows...  64.5 us
  transfers between devices with their start and end apart: 41, of which 25 were waited for; matrix products, arithmetic and copies ran while one was open for 33% of the time, Pallas kernels for 11%

profile of v1, /device:TPU:0, one launch (start us, length us, event | category | flops | bytes accessed | tf_op | source)
XLA Modules:
  0.0 1459.9 jit_solution(4901781722812232691)
XLA Ops:
  24.5 47.8 %collective-permute-done = bf16[1,512,2048]{2,1,0:T(8,128)(2,1)} collective-permute-done((bf16[1,512,2048]{2,1,0:T(8,128)(2,1)S(1)}, bf16[1,512,2048]{2,1,0:T(8,128)(2,1)}, u32[]{:S(2)}, u32[]{:S(2)}) %collective-permute-start) | collective-permute-done | bytes 2097184 | tf_op jit(solution)/shard_map/ppermute | solution.py:442
  74.6 46.7 %collective-permute-done.1 = bf16[1,512,2048]{2,1,0:T(8,128)(2,1)} collective-permute-done((bf16[1,512,2048]{2,1,0:T(8,128)(2,1)}, bf16[1,512,2048]{2,1,0:T(8,128)(2,1)}, u32[]{:S(2)}, u32[]{:S(2)}) %collective-permute-start.1) | collective-permute-done | bytes 2097184 | tf_op jit(solution)/shard_map/ppermute | solution.py:442
  142.2 27.2 %collective-permute-done.2 = bf16[1,512,2048]{2,1,0:T(8,128)(2,1)} collective-permute-done((bf16[1,512,2048]{2,1,0:T(8,128)(2,1)}, bf16[1,512,2048]{2,1,0:T(8,128)(2,1)}, u32[]{:S(2)}, u32[]{:S(2)}) %collective-permute-start.2) | collective-permute-done | bytes 2097184 | tf_op jit(solution)/shard_map/ppermute | solution.py:442
  208.9 64.5 %mixer_forward.1 = (bf16[1,2048,1024]{2,1,0:T(8,128)(2,1)S(1)}, bf16[1,16,4,128,128]{4,3,2,1,0:T(8,128)(2,1)S(1)}, bf16[1,16,4,128,256]{4,3,2,1,0:T(8,128)(2,1)S(1)}, bf16[1,2048,1024]{2,1,0:T(8,128)(2,1)}) custom-call(f32[1,2048,1152]{2,1,0:T(8,128)} %fusion.76.pq.pk.ps.tq.tk, f32[1,2048,1152]{2,1,0:T(8,128)} %fusion.76.pq.pk.ps.tq.tk, ...), custom_call_target="tpu_custom_call" | custom-call | tf_op jit(solution)/shard_map/mixer_forward/pallas_call | solution.py:345
  283.5 47.4 %collective-permute-done.3 = bf16[1,512,2048]{2,1,0:T(8,128)(2,1)} collective-permute-done((bf16[1,512,2048]{2,1,0:T(8,128)(2,1)}, bf16[1,512,2048]{2,1,0:T(8,128)(2,1)}, u32[]{:S(2)}, u32[]{:S(2)}) %collective-permute-start.3) | collective-permute-done | bytes 2097184 | tf_op jit(solution)/shard_map/ppermute | solution.py:449
  339.0 43.9 %collective-permute-done.4 = bf16[1,512,2048]{2,1,0:T(8,128)(2,1)S(1)} collective-permute-done((bf16[1,512,2048]{2,1,0:T(8,128)(2,1)S(1)}, bf16[1,512,2048]{2,1,0:T(8,128)(2,1)S(1)}, u32[]{:S(2)}, u32[]{:S(2)}) %collective-permute-start.4) | collective-permute-done | bytes 2097184 | tf_op jit(solution)/shard_map/ppermute | solution.py:449
  387.0 42.3 %collective-permute-done.5 = bf16[1,512,2048]{2,1,0:T(8,128)(2,1)S(1)} collective-permute-done((bf16[1,512,2048]{2,1,0:T(8,128)(2,1)S(1)}, bf16[1,512,2048]{2,1,0:T(8,128)(2,1)S(1)}, u32[]{:S(2)}, u32[]{:S(2)}) %collective-permute-start.5) | collective-permute-done | bytes 2097184 | tf_op jit(solution)/shard_map/ppermute | solution.py:449
  452.8 11.2 multiply_convert_fusion.8
  464.1 22.8 %collective-permute-done.6 = bf16[1,512,2048]{2,1,0:T(8,128)(2,1)} collective-permute-done((bf16[1,512,2048]{2,1,0:T(8,128)(2,1)}, bf16[1,512,2048]{2,1,0:T(8,128)(2,1)}, u32[]{:S(2)}, u32[]{:S(2)}) %collective-permute-start.6) | collective-permute-done | bytes 2097184 | tf_op jit(solution)/shard_map/ppermute | solution.py:442
  493.7 38.2 %collective-permute-done.12 = bf16[1,512,2048]{2,1,0:T(8,128)(2,1)} collective-permute-done((bf16[1,512,2048]{2,1,0:T(8,128)(2,1)}, bf16[1,512,2048]{2,1,0:T(8,128)(2,1)}, u32[]{:S(2)}, u32[]{:S(2)}) %collective-permute-start.12) | collective-permute-done | bytes 2097184 | tf_op jit(solution)/shard_map/ppermute | solution.py:442
  544.6 32.0 %collective-permute-done.7 = bf16[1,512,2048]{2,1,0:T(8,128)(2,1)S(1)} collective-permute-done((bf16[1,512,2048]{2,1,0:T(8,128)(2,1)}, bf16[1,512,2048]{2,1,0:T(8,128)(2,1)S(1)}, u32[]{:S(2)}, u32[]{:S(2)}) %collective-permute-start.7) | collective-permute-done | bytes 2097184 | tf_op jit(solution)/shard_map/ppermute | solution.py:442
  580.1 41.5 %collective-permute-done.13 = bf16[1,512,2048]{2,1,0:T(8,128)(2,1)S(1)} collective-permute-done((bf16[1,512,2048]{2,1,0:T(8,128)(2,1)}, bf16[1,512,2048]{2,1,0:T(8,128)(2,1)S(1)}, u32[]{:S(2)}, u32[]{:S(2)}) %collective-permute-start.13) | collective-permute-done | bytes 2097184 | tf_op jit(solution)/shard_map/ppermute | solution.py:442
  634.2 32.4 %collective-permute-done.8 = bf16[1,512,2048]{2,1,0:T(8,128)(2,1)S(1)} collective-permute-done((bf16[1,512,2048]{2,1,0:T(8,128)(2,1)S(1)}, bf16[1,512,2048]{2,1,0:T(8,128)(2,1)S(1)}, u32[]{:S(2)}, u32[]{:S(2)}) %collective-permute-start.8) | collective-permute-done | bytes 2097184 | tf_op jit(solution)/shard_map/ppermute | solution.py:442
  673.4 32.2 %collective-permute-done.14 = bf16[1,512,2048]{2,1,0:T(8,128)(2,1)S(1)} collective-permute-done((bf16[1,512,2048]{2,1,0:T(8,128)(2,1)S(1)}, bf16[1,512,2048]{2,1,0:T(8,128)(2,1)S(1)}, u32[]{:S(2)}, u32[]{:S(2)}) %collective-permute-start.14) | collective-permute-done | bytes 2097184 | tf_op jit(solution)/shard_map/ppermute | solution.py:442
  711.3 19.3 %fusion.21 = bf16[2048,1408]{1,0:T(8,128)(2,1)} fusion(bf16[512,2048]{1,0:T(8,128)(2,1)} %bitcast.371, bf16[512,2048]{1,0:T(8,128)(2,1)} %bitcast.370, bf16[512,2048]{1,0:T(8,128)(2,1)} %bitcast.32, bf16[512,2048]{1,0:T(8,128)(2,1)} %bitcast.29, bf16[512,1408]{1,0:T(8,128)(2,1)} %get-tuple-element.141, bf16[512,1408]{1,0:T(8,128)(2,1)} %get-tuple-element.144, ...), kind=kOutput, calls=%fused_computation.16 | convolution fusion | flops 11870666752 | bytes 19922944 | tf_op jit(solution)/shard_map/dot_general | solution.py:436
  749.5 37.4 %collective-permute-done.15 = bf16[512,2048]{1,0:T(8,128)(2,1)S(1)} collective-permute-done((bf16[512,2048]{1,0:T(8,128)(2,1)S(1)}, bf16[512,2048]{1,0:T(8,128)(2,1)S(1)}, u32[]{:S(2)}, u32[]{:S(2)}) %collective-permute-start.15) | collective-permute-done | bytes 2097184 | tf_op jit(solution)/shard_map/ppermute | solution.py:449
  791.8 19.0 %convolution_convert_fusion = bf16[2048,1408]{1,0:T(8,128)(2,1)} fusion(bf16[512,1408]{1,0:T(8,128)(2,1)} %get-tuple-element.139, bf16[512,1408]{1,0:T(8,128)(2,1)} %get-tuple-element.142, bf16[512,1408]{1,0:T(8,128)(2,1)} %get-tuple-element.145, bf16[512,1408]{1,0:T(8,128)(2,1)} %get-tuple-element.136, bf16[512,2048]{1,0:T(8,128)(2,1)} %bitcast.368, ...), kind=kOutput, calls=%fused_computation.17 | convolution fusion | flops 11870666752 | bytes 19922944 | tf_op jit(solution)/shard_map/dot_general | solution.py:436
  822.9 11.8 collective-permute-done.16
  851.5 27.3 %collective-permute-done.17 = bf16[512,2048]{1,0:T(8,128)(2,1)} collective-permute-done((bf16[512,2048]{1,0:T(8,128)(2,1)S(1)}, bf16[512,2048]{1,0:T(8,128)(2,1)}, u32[]{:S(2)}, u32[]{:S(2)}) %collective-permute-start.17) | collective-permute-done | bytes 2097184 | tf_op jit(solution)/shard_map/ppermute | solution.py:449
  891.7 19.0 %convolution_convert_fusion.1 = bf16[2048,1408]{1,0:T(8,128)(2,1)} fusion(bf16[512,1408]{1,0:T(8,128)(2,1)} %get-tuple-element.140, bf16[512,1408]{1,0:T(8,128)(2,1)} %get-tuple-element.143, bf16[512,1408]{1,0:T(8,128)(2,1)} %get-tuple-element.146, bf16[512,1408]{1,0:T(8,128)(2,1)} %get-tuple-element.137, bf16[512,2048]{1,0:T(8,128)(2,1)} %bitcast.369, ...), kind=kOutput, calls=%fused_computation.18 | convolution fusion | flops 11870666752 | bytes 19922944 | tf_op jit(solution)/shard_map/dot_general | solution.py:436
  910.8 26.7 %collective-permute-done.18 = bf16[1,512,2048]{2,1,0:T(8,128)(2,1)} collective-permute-done((bf16[1,512,2048]{2,1,0:T(8,128)(2,1)}, bf16[1,512,2048]{2,1,0:T(8,128)(2,1)}, u32[]{:S(2)}, u32[]{:S(2)}) %collective-permute-start.18) | collective-permute-done | bytes 2097184 | tf_op jit(solution)/shard_map/ppermute | solution.py:442
  937.5 45.6 %collective-permute-done.19 = bf16[1,512,2048]{2,1,0:T(8,128)(2,1)} collective-permute-done((bf16[1,512,2048]{2,1,0:T(8,128)(2,1)}, bf16[1,512,2048]{2,1,0:T(8,128)(2,1)}, u32[]{:S(2)}, u32[]{:S(2)}) %collective-permute-start.19) | collective-permute-done | bytes 2097184 | tf_op jit(solution)/shard_map/ppermute | solution.py:442
  997.6 36.4 %collective-permute-done.20 = bf16[1,512,2048]{2,1,0:T(8,128)(2,1)} collective-permute-done((bf16[1,512,2048]{2,1,0:T(8,128)(2,1)}, bf16[1,512,2048]{2,1,0:T(8,128)(2,1)}, u32[]{:S(2)}, u32[]{:S(2)}) %collective-permute-start.20) | collective-permute-done | bytes 2097184 | tf_op jit(solution)/shard_map/ppermute | solution.py:442
  1037.1 12.9 fusion.73
  1095.4 97.7 %mixer_backward.1 = (bf16[1,2048,1152]{2,1,0:T(8,128)(2,1)}, bf16[1,2048,2048]{2,1,0:T(8,128)(2,1)}, f32[8,512]{1,0:T(8,128)S(1)}, f32[8,512]{1,0:T(8,128)S(1)},...) custom-call(f32[1,2048,1024]{2,1,0:T(8,128)} %copy-done.17, ...), custom_call_target="tpu_custom_call" | custom-call | tf_op jit(solution)/shard_map/mixer_backward/pallas_call | solution.py:389
  1193.1 16.4 %fusion.13 = bf16[2048,1152]{1,0:T(8,128)(2,1)} fusion(bf16[1,2048,2048]{2,1,0:T(8,128)(2,1)} %constant_dynamic-update-slice_fusion, bf16[1,2048,1152]{2,1,0:T(8,128)(2,1)} %get-tuple-element.75), kind=kOutput, calls=%fused_computation.14 | convolution fusion | flops 9666035712 | bytes 17825792 | tf_op jit(solution)/shard_map/dot_general | solution.py:436
  1234.9 22.1 %fusion.16 = bf16[2048,2048]{1,0:T(8,128)(2,1)} fusion(bf16[1,2048,2048]{2,1,0:T(8,128)(2,1)} %get-tuple-element.76, bf16[1,2048,2048]{2,1,0:T(8,128)(2,1)S(1)} %bitcast.344), kind=kOutput, calls=%fused_computation.15 | convolution fusion | flops 17184063488 | bytes 25165824 | tf_op jit(solution)/shard_map/dot_general | solution.py:436
  1271.2 12.2 fusion.61
  1295.5 31.3 %collective-permute-done.22 = bf16[1,512,2048]{2,1,0:T(8,128)(2,1)S(1)} collective-permute-done((bf16[1,512,2048]{2,1,0:T(8,128)(2,1)S(1)}, bf16[1,512,2048]{2,1,0:T(8,128)(2,1)S(1)}, u32[]{:S(2)}, u32[]{:S(2)}) %collective-permute-start.22) | collective-permute-done | bytes 2097184 | tf_op jit(solution)/shard_map/ppermute | solution.py:449
  1341.2 38.4 %collective-permute-done.23 = bf16[1,512,2048]{2,1,0:T(8,128)(2,1)} collective-permute-done((bf16[1,512,2048]{2,1,0:T(8,128)(2,1)}, bf16[1,512,2048]{2,1,0:T(8,128)(2,1)}, u32[]{:S(2)}, u32[]{:S(2)}) %collective-permute-start.23) | collective-permute-done | bytes 2097184 | tf_op jit(solution)/shard_map/ppermute | solution.py:449
  1379.6 17.7 %fusion.62 = (f32[2048]{0:T(1024)S(1)}, f32[2048]{0:T(1024)S(1)}, f32[2048]{0:T(1024)S(1)}, f32[2048]{0:T(1024)S(1)}, f32[512]{0:T(512)S(1)}, /*index=5*/f32[512,2048]{1,0:T(8,128)}) fusion(f32[512,2048]{1,0:T(8,128)} %get-tuple-element.166, bf16[1,2048,2048]{2,1,0:T(8,128)(2,1)} %constant_dynamic-update-slice_fusion, s32[]{:T(128)S(6)} %select_n.18, ...), kind=kOutput, calls=%fused_computation.66 | convolution fusion | flops 4315930112 | bytes 44087808 | tf_op jit(solution)/shard_map/dot_general | solution.py:436
  1430.7 11.2 fusion.55
  (369 shorter events, 410.9 us)
Async XLA Ops:
  7.2 114.2 %all-gather.7.cloned.1.call-start = ((), (), s32[]{:S(2)}) async-start(), calls=%async_computation.6 | async-start | bytes 5308416 | tf_op jit(solution)/shard_map/all_gather | solution.py:515
  11.0 164.3 %all-gather.9.cloned.1.call-start = ((), (), s32[]{:S(2)}) async-start(), calls=%async_computation.7 | async-start | bytes 9437184 | tf_op jit(solution)/shard_map/all_gather | solution.py:515
  13.4 263.9 %all-gather.11.cloned.1.call-start = ((), (), s32[]{:S(2)}) async-start(), calls=%async_computation.8 | async-start | bytes 4718592 | tf_op jit(solution)/shard_map/all_gather | solution.py:515
  14.1 422.1 %all-gather.15.cloned.1.call-start = ((), (), s32[]{:S(2)}) async-start(), calls=%async_computation.10 | async-start | bytes 6488064 | tf_op jit(solution)/shard_map/all_gather | solution.py:515
  14.7 429.9 %all-gather.13.cloned.1.call-start = ((), (), s32[]{:S(2)}) async-start(), calls=%async_computation.9 | async-start | bytes 6488064 | tf_op jit(solution)/shard_map/all_gather | solution.py:515
  21.5 50.8 %collective-permute-start = (bf16[1,512,2048]{2,1,0:T(8,128)(2,1)S(1)}, bf16[1,512,2048]{2,1,0:T(8,128)(2,1)}, u32[]{:S(2)}, u32[]{:S(2)}) collective-permute-start(bf16[1,512,2048]{2,1,0:T(8,128)(2,1)S(1)} %get-tuple-element.132), channel_id=1, source_target_pairs={{0,1},{1,2},{2,3},{3,0},{4,5},{5,6},{6,7},{7,4},{8,9},{9,10},{10,1... | collective-permute-start | bytes 6291464 | tf_op jit(solution)/shard_map/ppermute | solution.py:442
  72.3 48.9 %collective-permute-start.1 = (bf16[1,512,2048]{2,1,0:T(8,128)(2,1)}, bf16[1,512,2048]{2,1,0:T(8,128)(2,1)}, u32[]{:S(2)}, u32[]{:S(2)}) collective-permute-start(bf16[1,512,2048]{2,1,0:T(8,128)(2,1)} %collective-permute-done), channel_id=1, source_target_pairs={{0,1},{1,2},{2,3},{3,0},{4,5},{5,6},{6,7},{7,4},{8,9},{9,10},{10,1... | collective-permute-start | bytes 6291464 | tf_op jit(solution)/shard_map/ppermute | solution.py:442
  72.3 380.5 %all-gather.17.cloned.1.call-start = ((), (), s32[]{:S(2)}) async-start(), calls=%async_computation.11 | async-start | bytes 6488064 | tf_op jit(solution)/shard_map/all_gather | solution.py:515
  121.2 48.2 %collective-permute-start.2 = (bf16[1,512,2048]{2,1,0:T(8,128)(2,1)}, bf16[1,512,2048]{2,1,0:T(8,128)(2,1)}, u32[]{:S(2)}, u32[]{:S(2)}) collective-permute-start(bf16[1,512,2048]{2,1,0:T(8,128)(2,1)} %collective-permute-done.1), channel_id=1, source_target_pairs={{0,1},{1,2},{2,3},{3,0},{4,5},{5,6},{6,7},{7,4},{8,9},{9,10},{10,1... | collective-permute-start | bytes 6291464 | tf_op jit(solution)/shard_map/ppermute | solution.py:442
  283.4 47.5 %collective-permute-start.3 = (bf16[1,512,2048]{2,1,0:T(8,128)(2,1)}, bf16[1,512,2048]{2,1,0:T(8,128)(2,1)}, u32[]{:S(2)}, u32[]{:S(2)}) collective-permute-start(bf16[1,512,2048]{2,1,0:T(8,128)(2,1)} %fusion.84), channel_id=1, source_target_pairs={{0,1},{1,2},{2,3},{3,0},{4,5},{5,6},{6,7},{7,4},{8,9},{9,10},{10,1... | collective-permute-start | bytes 6291464 | tf_op jit(solution)/shard_map/ppermute | solution.py:449
  283.5 1132.7 %reduce-scatter.17.cloned.1.call-start = ((), (), s32[]{:S(2)}) async-start(), calls=%async_computation.17 | async-start | bytes 6488064 | tf_op jit(solution)/shard_map/reduce_scatter | solution.py:594
  336.5 46.3 %collective-permute-start.4 = (bf16[1,512,2048]{2,1,0:T(8,128)(2,1)S(1)}, bf16[1,512,2048]{2,1,0:T(8,128)(2,1)S(1)}, u32[]{:S(2)}, u32[]{:S(2)}) collective-permute-start(bf16[1,512,2048]{2,1,0:T(8,128)(2,1)S(1)} %fusion.70), channel_id=1, source_target_pairs={{0,1},{1,2},{2,3},{3,0},{4,5},{5,6},{6,7},{7,4},{8,9},{9,10},{10,1... | collective-permute-start | bytes 6291464 | tf_op jit(solution)/shard_map/ppermute | solution.py:449
  383.7 45.6 %collective-permute-start.5 = (bf16[1,512,2048]{2,1,0:T(8,128)(2,1)S(1)}, bf16[1,512,2048]{2,1,0:T(8,128)(2,1)S(1)}, u32[]{:S(2)}, u32[]{:S(2)}) collective-permute-start(bf16[1,512,2048]{2,1,0:T(8,128)(2,1)S(1)} %fusion.71), channel_id=1, source_target_pairs={{0,1},{1,2},{2,3},{3,0},{4,5},{5,6},{6,7},{7,4},{8,9},{9,10},{10,1... | collective-permute-start | bytes 6291464 | tf_op jit(solution)/shard_map/ppermute | solution.py:449
  436.2 50.7 %collective-permute-start.6 = (bf16[1,512,2048]{2,1,0:T(8,128)(2,1)}, bf16[1,512,2048]{2,1,0:T(8,128)(2,1)}, u32[]{:S(2)}, u32[]{:S(2)}) collective-permute-start(bf16[1,512,2048]{2,1,0:T(8,128)(2,1)} %multiply_convert_fusion.1), channel_id=1, source_target_pairs={{0,1},{1,2},{2,3},{3,0},{4,5},{5,6},{6,7},{7,4},{8,9},{9,10},{10,1... | collective-permute-start | bytes 6291464 | tf_op jit(solution)/shard_map/ppermute | solution.py:442
  436.2 95.6 %collective-permute-start.12 = (bf16[1,512,2048]{2,1,0:T(8,128)(2,1)}, bf16[1,512,2048]{2,1,0:T(8,128)(2,1)}, u32[]{:S(2)}, u32[]{:S(2)}) collective-permute-start(bf16[1,512,2048]{2,1,0:T(8,128)(2,1)} %get-tuple-element.164), channel_id=1, source_target_pairs={{0,1},{1,2},{2,3},{3,0},{4,5},{5,6},{6,7},{7,4},{8,9},{9,10},{10,1... | collective-permute-start | bytes 6291464 | tf_op jit(solution)/shard_map/ppermute | solution.py:442
  486.9 89.8 %collective-permute-start.7 = (bf16[1,512,2048]{2,1,0:T(8,128)(2,1)}, bf16[1,512,2048]{2,1,0:T(8,128)(2,1)S(1)}, u32[]{:S(2)}, u32[]{:S(2)}) collective-permute-start(bf16[1,512,2048]{2,1,0:T(8,128)(2,1)} %collective-permute-done.6), channel_id=1, source_target_pairs={{0,1},{1,2},{2,3},{3,0},{4,5},{5,6},{6,7},{7,4},{8,9},{9,10},{10,1... | collective-permute-start | bytes 6291464 | tf_op jit(solution)/shard_map/ppermute | solution.py:442
  531.8 89.8 %collective-permute-start.13 = (bf16[1,512,2048]{2,1,0:T(8,128)(2,1)}, bf16[1,512,2048]{2,1,0:T(8,128)(2,1)S(1)}, u32[]{:S(2)}, u32[]{:S(2)}) collective-permute-start(bf16[1,512,2048]{2,1,0:T(8,128)(2,1)} %collective-permute-done.12), channel_id=1, source_target_pairs={{0,1},{1,2},{2,3},{3,0},{4,5},{5,6},{6,7},{7,4},{8,9},{9,10},{10,1... | collective-permute-start | bytes 6291464 | tf_op jit(solution)/shard_map/ppermute | solution.py:442
  576.7 89.9 %collective-permute-start.8 = (bf16[1,512,2048]{2,1,0:T(8,128)(2,1)S(1)}, bf16[1,512,2048]{2,1,0:T(8,128)(2,1)S(1)}, u32[]{:S(2)}, u32[]{:S(2)}) collective-permute-start(bf16[1,512,2048]{2,1,0:T(8,128)(2,1)S(1)} %collective-permute-done.7), channel_id=1, source_target_pairs={{0,1},{1,2},{2,3},{3,0},{4,5},{5,6},{6,7},{7,4},{8,9},{9,10},{10,1... | collective-permute-start | bytes 6291464 | tf_op jit(solution)/shard_map/ppermute | solution.py:442
  621.6 84.0 %collective-permute-start.14 = (bf16[1,512,2048]{2,1,0:T(8,128)(2,1)S(1)}, bf16[1,512,2048]{2,1,0:T(8,128)(2,1)S(1)}, u32[]{:S(2)}, u32[]{:S(2)}) collective-permute-start(bf16[1,512,2048]{2,1,0:T(8,128)(2,1)S(1)} %collective-permute-done.13), channel_id=1, source_target_pairs={{0,1},{1,2},{2,3},{3,0},{4,5},{5,6},{6,7},{7,4},{8,9},{9,10},{10,1... | collective-permute-start | bytes 6291464 | tf_op jit(solution)/shard_map/ppermute | solution.py:442
  730.6 687.8 %reduce-scatter.15.cloned.1.call-start = ((), (), s32[]{:S(2)}) async-start(), calls=%async_computation.16 | async-start | bytes 6488064 | tf_op jit(solution)/shard_map/reduce_scatter | solution.py:594
  810.9 609.9 %reduce-scatter.13.cloned.1.call-start = ((), (), s32[]{:S(2)}) async-start(), calls=%async_computation.15 | async-start | bytes 6488064 | tf_op jit(solution)/shard_map/reduce_scatter | solution.py:594
  891.7 45.8 %collective-permute-start.18 = (bf16[1,512,2048]{2,1,0:T(8,128)(2,1)}, bf16[1,512,2048]{2,1,0:T(8,128)(2,1)}, u32[]{:S(2)}, u32[]{:S(2)}) collective-permute-start(bf16[1,512,2048]{2,1,0:T(8,128)(2,1)} %get-tuple-element.130), channel_id=1, source_target_pairs={{0,1},{1,2},{2,3},{3,0},{4,5},{5,6},{6,7},{7,4},{8,9},{9,10},{10,1... | collective-permute-start | bytes 6291464 | tf_op jit(solution)/shard_map/ppermute | solution.py:442
  910.8 512.3 %reduce-scatter.11.cloned.1.call-start = ((), (), s32[]{:S(2)}) async-start(), calls=%async_computation.14 | async-start | bytes 4718592 | tf_op jit(solution)/shard_map/reduce_scatter | solution.py:594
  937.5 45.6 %collective-permute-start.19 = (bf16[1,512,2048]{2,1,0:T(8,128)(2,1)}, bf16[1,512,2048]{2,1,0:T(8,128)(2,1)}, u32[]{:S(2)}, u32[]{:S(2)}) collective-permute-start(bf16[1,512,2048]{2,1,0:T(8,128)(2,1)} %collective-permute-done.18), channel_id=1, source_target_pairs={{0,1},{1,2},{2,3},{3,0},{4,5},{5,6},{6,7},{7,4},{8,9},{9,10},{10,1... | collective-permute-start | bytes 6291464 | tf_op jit(solution)/shard_map/ppermute | solution.py:442
  983.1 50.8 %collective-permute-start.20 = (bf16[1,512,2048]{2,1,0:T(8,128)(2,1)}, bf16[1,512,2048]{2,1,0:T(8,128)(2,1)}, u32[]{:S(2)}, u32[]{:S(2)}) collective-permute-start(bf16[1,512,2048]{2,1,0:T(8,128)(2,1)} %collective-permute-done.19), channel_id=1, source_target_pairs={{0,1},{1,2},{2,3},{3,0},{4,5},{5,6},{6,7},{7,4},{8,9},{9,10},{10,1... | collective-permute-start | bytes 6291464 | tf_op jit(solution)/shard_map/ppermute | solution.py:442
  991.1 76.9 %collective-permute-start.9 = (bf16[512,2048]{1,0:T(8,128)(2,1)}, bf16[512,2048]{1,0:T(8,128)(2,1)}, u32[]{:S(2)}, u32[]{:S(2)}) collective-permute-start(bf16[512,2048]{1,0:T(8,128)(2,1)} %convolution_convert_fusion.3), channel_id=1, source_target_pairs={{0,1},{1,2},{2,3},{3,0},{4,5},{5,6},{6,7},{7,4},{8,9},{9,10},{10,1... | collective-permute-start | bytes 6291464 | tf_op jit(solution)/shard_map/ppermute | solution.py:449
  1050.0 395.6 %reduce-scatter.7.cloned.1.call-start = ((), (), s32[]{:S(2)}) async-start(), calls=%async_computation.12 | async-start | bytes 5308416 | tf_op jit(solution)/shard_map/reduce_scatter | solution.py:594
  1074.0 255.0 %collective-permute-start.10 = (bf16[512,2048]{1,0:T(8,128)(2,1)}, bf16[512,2048]{1,0:T(8,128)(2,1)}, u32[]{:S(2)}, u32[]{:S(2)}) collective-permute-start(bf16[512,2048]{1,0:T(8,128)(2,1)} %add_convert_fusion.4), channel_id=1, source_target_pairs={{0,1},{1,2},{2,3},{3,0},{4,5},{5,6},{6,7},{7,4},{8,9},{9,10},{10,1... | collective-permute-start | bytes 6291464 | tf_op jit(solution)/shard_map/ppermute | solution.py:449
  1209.5 240.5 %reduce-scatter.9.cloned.1.call-start = ((), (), s32[]{:S(2)}) async-start(), calls=%async_computation.13 | async-start | bytes 9437184 | tf_op jit(solution)/shard_map/reduce_scatter | solution.py:594
  1283.3 43.5 %collective-permute-start.22 = (bf16[1,512,2048]{2,1,0:T(8,128)(2,1)S(1)}, bf16[1,512,2048]{2,1,0:T(8,128)(2,1)S(1)}, u32[]{:S(2)}, u32[]{:S(2)}) collective-permute-start(bf16[1,512,2048]{2,1,0:T(8,128)(2,1)S(1)} %get-tuple-element.165), channel_id=1, source_target_pairs={{0,1},{1,2},{2,3},{3,0},{4,5},{5,6},{6,7},{7,4},{8,9},{9,10},{10,1... | collective-permute-start | bytes 6291464 | tf_op jit(solution)/shard_map/ppermute | solution.py:449
  1328.9 50.7 %collective-permute-start.23 = (bf16[1,512,2048]{2,1,0:T(8,128)(2,1)}, bf16[1,512,2048]{2,1,0:T(8,128)(2,1)}, u32[]{:S(2)}, u32[]{:S(2)}) collective-permute-start(bf16[1,512,2048]{2,1,0:T(8,128)(2,1)} %fusion.63), channel_id=1, source_target_pairs={{0,1},{1,2},{2,3},{3,0},{4,5},{5,6},{6,7},{7,4},{8,9},{9,10},{10,1... | collective-permute-start | bytes 6291464 | tf_op jit(solution)/shard_map/ppermute | solution.py:449
  1332.7 97.9 %collective-permute-start.11 = (bf16[512,2048]{1,0:T(8,128)(2,1)}, bf16[512,2048]{1,0:T(8,128)(2,1)}, u32[]{:S(2)}, u32[]{:S(2)}) collective-permute-start(bf16[512,2048]{1,0:T(8,128)(2,1)} %add_convert_fusion.3), channel_id=1, source_target_pairs={{0,1},{1,2},{2,3},{3,0},{4,5},{5,6},{6,7},{7,4},{8,9},{9,10},{10,1... | collective-permute-start | bytes 6291464 | tf_op jit(solution)/shard_map/ppermute | solution.py:449
  (87 other events, 2123.4 us)
Sparse Core Ops, SparseCore 0:
  11.1 41.6 all-gather.6
  55.2 54.3 all-gather.8
  111.6 36.7 all-gather.10
  150.1 43.3 all-gather.14
  195.1 43.3 all-gather.12
  283.6 44.3 all-gather.16
  730.8 57.5 reduce-scatter.16
  811.0 60.9 reduce-scatter.14
  910.9 61.1 reduce-scatter.12
  1050.1 50.1 reduce-scatter.10
  1209.7 54.9 reduce-scatter.6
  1268.3 71.2 reduce-scatter.8

commit v2 on v1

--- a/solution.py
+++ b/solution.py
@@ -365,6 +365,7 @@
         compiler_params=pltpu.CompilerParams(
             dimension_semantics=("arbitrary", "arbitrary"), vmem_limit_bytes=40 << 20
         ),
+        cost_estimate=pl.CostEstimate(flops=0, bytes_accessed=int(rows * chunks * heads * 3500000.0), transcendentals=0),
         name="mixer_forward",
     )(pqks, pqks, pvg, pvg, pqks, cq, ck, cv, lane_pad(-jnp.exp(log_rates), 0),
       lane_pad(rate_bias, 0), gain.reshape(1, DV))
@@ -416,49 +417,298 @@
         compiler_params=pltpu.CompilerParams(
             dimension_semantics=("arbitrary", "arbitrary"), vmem_limit_bytes=48 << 20
         ),
+        cost_estimate=pl.CostEstimate(flops=0, bytes_accessed=int(rows * chunks * heads * 5304687.5), transcendentals=0),
         name="mixer_backward",
     )(dm, pqks, pqks, pvg, pvg, pqks, pqks, pqks, pvg, cq, ck, cv, lane_pad(-jnp.exp(log_rates), 0),
       lane_pad(rate_bias, 0), gain.reshape(1, DV), t_in, s_in, f_in)
 
 
-GROUP = 0
+FREE = pl.CostEstimate(flops=0, bytes_accessed=0, transcendentals=0)
+VMEM_LIMIT = 44 << 20
+
+
+def rows_kernel(count, nt, has_weigh, at, *refs):
+    out = refs[-2] if has_weigh else refs[-1]
+    total = None
+    for i in range(count):
+        part = lax.dot_general(
+            refs[2 * i][0], refs[2 * i + 1][...], NT if nt else NN, preferred_element_type=F32
+        )
+        total = part if total is None else total + part
+    if has_weigh:
+        refs[-1][0, 0:1, :] = jnp.sum(
+            total * refs[2 * count][0].astype(F32), axis=0, keepdims=True
+        )
+    out[0] = total.astype(out.dtype)
+
+
+def rows_matmul(pairs, piece, nt=False, tile=512, take=0, weigh=None, into=None, put=0, dtype=BF):
+    rows = pairs[0][0].shape[0]
+    width = pairs[0][1].shape[0 if nt else 1]
+    tile = min(tile, width)
+    at = jnp.stack([jnp.int32(take), jnp.int32(put)])
+    specs, args = [], []
+    for a, w in pairs:
+        depth = a.shape[2]
+        specs.append(pl.BlockSpec((1, piece, depth), lambda r, n, at: (r, at[0], 0)))
+        if nt:
+            specs.append(pl.BlockSpec((tile, depth), lambda r, n, at: (n, 0)))
+        else:
+            specs.append(pl.BlockSpec((depth, tile), lambda r, n, at: (0, n)))
+        args.extend((a, w))
+    if weigh is not None:
+        specs.append(pl.BlockSpec((1, piece, tile), lambda r, n, at: (r, 0, n)))
+        args.append(weigh)
+    aliases = {}
+    shape = (rows, piece, width)
+    if into is not None:
+        shape = into.shape
+        dtype = into.dtype
+        if not isinstance(into, jax.ShapeDtypeStruct):
+            specs.append(pl.BlockSpec(memory_space=pl.ANY))
+            args.append(into)
+            aliases = {len(args): 0}
+    out_specs = [pl.BlockSpec((1, piece, tile), lambda r, n, at: (r, at[1], n))]
+    out_shape = [jax.ShapeDtypeStruct(shape, dtype)]
+    if weigh is not None:
+        out_specs.append(pl.BlockSpec((1, 8, tile), lambda r, n, at: (r, 0, n)))
+        out_shape.append(jax.ShapeDtypeStruct((rows, 8, width), F32))
+    out = pl.pallas_call(
+        functools.partial(rows_kernel, len(pairs), nt, weigh is not None),
+        grid_spec=pltpu.PrefetchScalarGridSpec(
+            num_scalar_prefetch=1,
+            grid=(rows, pl.cdiv(width, tile)),
+            in_specs=specs,
+            out_specs=out_specs,
+        ),
+        out_shape=out_shape,
+        input_output_aliases=aliases,
+        compiler_params=pltpu.CompilerParams(
+            dimension_semantics=("arbitrary", "arbitrary"), vmem_limit_bytes=VMEM_LIMIT
+        ),
+        cost_estimate=FREE,
+        name="rows_matmul",
+    )(at, *args)
+    return out[0] if weigh is None else (out[0], jnp.sum(out[1][:, 0], axis=0))
+
+
+def outer_kernel(count, blocks, at, *refs):
+    xs, gs = refs[:count], refs[count : 2 * count]
+    out, flipped = refs[-2:]
+    rows, piece, width = xs[0].shape
+    depth = rows * piece
+    block = flipped.shape[0] // blocks
+
+    @pl.when(pl.program_id(0) == 0)
+    def _():
+        for i, x in enumerate(xs):
+            for k in range(blocks):
+                start = pl.multiple_of((2 * k + at[0]) * block, block)
+                part = x[:, :, pl.ds(start, block)].reshape(depth, block)
+                flipped[k * block : (k + 1) * block, i * depth : (i + 1) * depth] = part.T
+
+    total = None
+    for i, g in enumerate(gs):
+        part = lax.dot_general(
+            flipped[:, i * depth : (i + 1) * depth],
+            g[...].reshape(depth, g.shape[2]),
+            NN,
+            preferred_element_type=F32,
+        )
+        total = part if total is None else total + part
+    for extra in refs[2 * count : -2]:
+        total = total + extra[...].astype(F32)
+    out[...] = total.astype(out.dtype)
+
+
+def outer_sum(xs, gs, places, core, data, tile=512, adds=(), dtype=BF):
+    rows, piece, width = xs[0].shape
+    columns = gs[0].shape[2]
+    tile = min(tile, columns)
+    at = jnp.stack([jnp.int32(core)] + [jnp.int32(x) for x in places])
+    specs = [pl.BlockSpec((rows, piece, width), lambda n, at: (0, 0, 0))] * len(xs)
+    for i in range(len(gs)):
+        specs.append(
+            pl.BlockSpec((rows, piece, tile), lambda n, at, i=i: (0, at[1 + i], n))
+        )
+    args = [*xs, *gs]
+    out_spec = pl.BlockSpec((width // 2, tile), lambda n, at: (0, n))
+    for extra in adds:
+        specs.append(out_spec)
+        args.append(extra)
+    return pl.pallas_call(
+        functools.partial(outer_kernel, len(xs), data // 2),
+        grid_spec=pltpu.PrefetchScalarGridSpec(
+            num_scalar_prefetch=1,
+            grid=(columns // tile,),
+            in_specs=specs,
+            out_specs=out_spec,
+            scratch_shapes=[pltpu.VMEM((width // 2, len(xs) * rows * piece), BF)],
+        ),
+        out_shape=jax.ShapeDtypeStruct((width // 2, columns), dtype),
+        compiler_params=pltpu.CompilerParams(
+            dimension_semantics=("arbitrary",), vmem_limit_bytes=VMEM_LIMIT
+        ),
+        cost_estimate=FREE,
+        name="outer_sum",
+    )(at, *args)
+
+
+UNITS = 256
+
+
+def lanes_of(units):
+    return 128 if units % 128 == 0 else 64
+
+
+def mlp_kernel(lanes, x, wgu, g, wd, hidden, grads):
+    mlp_finish(lanes, lax.dot_general(x[...], wgu[...], NN, preferred_element_type=F32), g, wd, hidden, grads)
+
+
+def mlp_finish(lanes, both, g, wd, hidden, grads):
+    back = lax.dot_general(g[...], wd[...], NN, preferred_element_type=F32)
+    for at in range(0, UNITS, lanes):
+        first, second = 2 * at, 2 * at + lanes
+        gate = both[:, first : first + lanes]
+        up = both[:, second : second + lanes]
+        own = back[:, at : at + lanes]
+        sig = sigmoid(gate)
+        act = gate * sig
+        hidden[:, at : at + lanes] = (act * up).astype(BF)
+        own_gate = own * up * (sig * (1.0 + gate * (1.0 - sig)))
+        grads[:, first : first + lanes] = own_gate.astype(BF)
+        grads[:, second : second + lanes] = (own * act).astype(BF)
+
+
+def mlp_block(g, wd, x=None, wgu=None, both=None):
+    piece, width = g.shape
+    units = wd.shape[1]
+    whole = pl.BlockSpec((piece, width), lambda n: (0, 0))
+    part = lambda depth, size: pl.BlockSpec((depth, size), lambda n: (0, n))
+    if both is None:
+        kernel, args = mlp_kernel, (x, wgu, g, wd)
+        specs = [whole, part(width, 2 * UNITS), whole, part(width, UNITS)]
+    else:
+        kernel, args = mlp_finish, (both, g, wd)
+        specs = [part(piece, 2 * UNITS), whole, part(width, UNITS)]
+    return pl.pallas_call(
+        functools.partial(kernel, lanes_of(units)),
+        grid=(pl.cdiv(units, UNITS),),
+        in_specs=specs,
+        out_specs=[part(piece, UNITS), part(piece, 2 * UNITS)],
+        out_shape=[
+            jax.ShapeDtypeStruct((piece, units), BF),
+            jax.ShapeDtypeStruct((piece, 2 * units), BF),
+        ],
+        compiler_params=pltpu.CompilerParams(
+            dimension_semantics=("arbitrary",), vmem_limit_bytes=VMEM_LIMIT
+        ),
+        cost_estimate=FREE,
+        name="mlp_block",
+    )(*args)
+
+
+NORM_ROWS = 128
+
+
+def row_stats(x):
+    r = lax.rsqrt(jnp.mean(x * x, axis=-1, keepdims=True) + NORM_EPS)
+    return x * r, r
+
+
+def norm_grad(n, r, inner):
+    return r * (inner - n * jnp.mean(n * inner, axis=-1, keepdims=True))
+
+
+def valid_rows(at):
+    start = at[0] + pl.program_id(1) * NORM_ROWS
+    positions = start + lax.broadcasted_iota(jnp.int32, (NORM_ROWS, 1), 0)
+    return (positions < at[1 + pl.program_id(0)]).astype(F32)
+
+
+def enter_kernel(at, tokens, gain, normed):
+    normed[0] = (row_stats(tokens[0].astype(F32))[0] * gain[...]).astype(BF)
+
+
+def middle_kernel(at, own, moved, tokens, gain, middle, normed):
+    total = own[0] + moved[0].astype(F32)
+    x = tokens[0].astype(F32) + valid_rows(at) * total
+    middle[0] = x
+    normed[0] = (row_stats(x)[0] * gain[...]).astype(BF)
+
+
+def middle_back_kernel(at, own, moved, middle, cot, gain, grad_middle, grad_attn, dgain):
+    @pl.when((pl.program_id(0) == 0) & (pl.program_id(1) == 0))
+    def _():
+        dgain[...] = jnp.zeros_like(dgain)
+
+    grad = own[0] + moved[0].astype(F32)
+    n, r = row_stats(middle[0])
+    dgain[0:1, :] += jnp.sum(grad * n, axis=0, keepdims=True)
+    total = cot[0].astype(F32) + norm_grad(n, r, gain[...] * grad)
+    grad_middle[0] = total
+    grad_attn[0] = (valid_rows(at) * total).astype(BF)
+
+
+def leave_kernel(at, own, moved, tokens, grad_middle, gain, out):
+    grad = own[0] + moved[0].astype(F32)
+    n, r = row_stats(tokens[0].astype(F32))
+    out[0] = (grad_middle[0] + norm_grad(n, r, gain[...] * grad)).astype(BF)
+
+
+def result_kernel(at, own, moved, middle, out):
+    total = own[0] + moved[0].astype(F32)
+    out[0] = (middle[0] + valid_rows(at) * total).astype(BF)
+
+
+def by_rows(kernel, at, arrays, gain, out_types, with_sum=False):
+    rows, piece, width = arrays[0].shape
+    block = pl.BlockSpec((1, NORM_ROWS, width), lambda r, t, at: (r, t, 0))
+    out_shape = [jax.ShapeDtypeStruct((rows, piece, width), x) for x in out_types]
+    out_specs = [block] * len(out_types)
+    specs = [block] * len(arrays)
+    args = list(arrays)
+    if gain is not None:
+        specs.append(pl.BlockSpec((1, width), lambda r, t, at: (0, 0)))
+        args.append(gain.reshape(1, width))
+    if with_sum:
+        out_shape.append(jax.ShapeDtypeStruct((8, width), F32))
+        out_specs.append(pl.BlockSpec((8, width), lambda r, t, at: (0, 0)))
+    return pl.pallas_call(
+        kernel,
+        grid_spec=pltpu.PrefetchScalarGridSpec(
+            num_scalar_prefetch=1,
+            grid=(rows, piece // NORM_ROWS),
+            in_specs=specs,
+            out_specs=out_specs,
+        ),
+        out_shape=out_shape,
+        compiler_params=pltpu.CompilerParams(
+            dimension_semantics=("arbitrary", "arbitrary"), vmem_limit_bytes=VMEM_LIMIT
+        ),
+        cost_estimate=FREE,
+        name=kernel.__name__,
+    )(at, *args)
 
 
 def ring(size, group):
     return [(i, i // group * group + (i + 1) % group) for i in range(size)]
 
 
+def across(size):
+    return [(i, (i + size // 2) % size) for i in range(size)]
+
+
 def swap(size, bit):
     return [(i, i ^ bit) for i in range(size)]
 
 
-def matmul(a, b, dims=NN):
-    return lax.dot_general(a, b, dims, preferred_element_type=F32)
-
-
-def gather_ring(piece, size, group):
-    pieces = [piece]
-    for _ in range(group - 1):
-        pieces.append(lax.ppermute(pieces[-1], "head", ring(size, group)))
-    return pieces
-
-
-def scatter_ring(part_of, size, group):
-    total = part_of(1 % group)
-    for s in range(2, group + 1):
-        moved = lax.ppermute(total.astype(BF), "head", ring(size, group))
-        total = part_of(s % group) + moved.astype(F32)
-    return total
-
-
-def norm_parts(x):
-    r = lax.rsqrt(jnp.mean(x * x, axis=-1, keepdims=True) + NORM_EPS)
-    return x * r, r
-
-
-def norm_back(n, r, gain, grad):
-    inner = gain * grad
-    return r * (inner - n * jnp.mean(n * inner, axis=-1, keepdims=True))
+def tie(*values):
+    return lax.optimization_barrier(values)
+
+
+def matmul(a, b):
+    return lax.dot_general(a, b, NN, preferred_element_type=F32)
 
 
 def sum_small(flat, sizes):
@@ -468,6 +718,21 @@
             flat = flat + lax.ppermute(flat, axis, swap(sizes[axis], bit))
             bit = bit * 2
     return flat
+
+
+def alternate(gate, up):
+    rows, units = gate.shape
+    lanes = lanes_of(units)
+    parts = [x.reshape(rows, units // lanes, lanes) for x in (gate, up)]
+    pair = jnp.stack(parts, axis=2)
+    return pair.reshape(rows, 2 * units)
+
+
+def apart(both):
+    rows, units = both.shape[0], both.shape[1] // 2
+    lanes = lanes_of(units)
+    pair = both.reshape(rows, units // lanes, 2, lanes)
+    return pair[:, :, 0].reshape(rows, units), pair[:, :, 1].reshape(rows, units)
 
 
 def per_device(
@@ -495,125 +760,248 @@
 ):
     rows, piece, width = tokens.shape
     size = lax.axis_size("head")
+    data = lax.axis_size("dp")
     me = lax.axis_index("head")
+    core = lax.rem(lax.axis_index("dp"), 2)
     length = piece * size
     heads = w_decay.shape[1]
+    key_width, value_width = heads * DK, heads * DV
+    shape3 = (rows, piece, width)
     flat_piece = rows * piece
+    group = size // 2
+    at = jnp.concatenate([(me * piece).astype(jnp.int32)[None], lengths])
     positions = me * piece + jnp.arange(piece, dtype=jnp.int32)
     mask = (positions[None, :] < lengths[:, None]).astype(F32)[:, :, None]
 
     def owner(s):
         return lax.rem(me + size - s, size)
 
-    def put(whole, part, s):
-        return lax.dynamic_update_slice_in_dim(whole, part, owner(s) * piece, 1)
-
-    def take(whole, s):
-        return lax.dynamic_slice_in_dim(whole, owner(s) * piece, piece, 1)
+    def step(x, group):
+        return lax.ppermute(x, "head", ring(size, group))
+
+    def opposite(x):
+        return lax.ppermute(x, "head", across(size))
 
     def gather_weight(w):
         return lax.all_gather(w, "dp", axis=0, tiled=True)
 
+    def outer_halves(xs, gs, places, tile=512):
+        away = outer_sum(xs, gs, places, 1 - core, data, tile)
+        moved = lax.ppermute(away, "dp", swap(data, 1))
+        return outer_sum(xs, gs, places, core, data, tile, (moved,))
+
+    def scatter_weight(total):
+        places = [[i + c for i in range(0, data, 2)] for c in range(2)]
+        return lax.psum_scatter(
+            total, "dp", scatter_dimension=0, tiled=True, axis_index_groups=places
+        )
+
+    normed = by_rows(enter_kernel, at, [tokens], gain_attn, [BF])[0]
     small_pad = jnp.zeros((w_decay.shape[0], 128 - 2 * heads), BF)
     w_qks = gather_weight(jnp.concatenate([w_query, w_key, w_decay, w_beta, small_pad], axis=1))
     w_vg = gather_weight(jnp.concatenate([w_value, w_gate_out], axis=1))
     wo_full = gather_weight(w_out)
-    wgate_full = gather_weight(w_gate)
-    wup_full = gather_weight(w_up)
-    wdown_full = gather_weight(w_down)
-
-    inputs32 = tokens.astype(F32)
-    n_one, r_one = norm_parts(inputs32)
-    normed = (n_one * gain_attn).astype(BF)
-    normed_pieces = gather_ring(normed, size, size)
-    normed_all = jnp.zeros((rows, length, width), BF)
-    pqks = jnp.zeros((rows, length, w_qks.shape[1]), F32)
-    pvg = jnp.zeros((rows, length, w_vg.shape[1]), F32)
-    batch_nn = (((2,), (0,)), ((), ()))
-    batch_nt = (((2,), (1,)), ((), ()))
-    for s, item in enumerate(normed_pieces):
-        pqks = put(pqks, matmul(item, w_qks, batch_nn), s)
-        pvg = put(pvg, matmul(item, w_vg, batch_nn), s)
-        normed_all = put(normed_all, item, s)
-
-    cq = lax.dynamic_slice_in_dim(conv_query, me * heads * DK, heads * DK, 1)
-    ck = lax.dynamic_slice_in_dim(conv_key, me * heads * DK, heads * DK, 1)
-    cv = lax.dynamic_slice_in_dim(conv_value, me * heads * DV, heads * DV, 1)
+
+    qks_buffer = jax.ShapeDtypeStruct((rows, length, 2 * key_width + 128), F32)
+    vg_buffer = jax.ShapeDtypeStruct((rows, length, 2 * value_width), F32)
+    def project_qks(item, s, into):
+        return rows_matmul([(item, w_qks)], piece, tile=into.shape[2], into=into, put=owner(s))
+
+    def project_vg(item, s, into):
+        return rows_matmul([(item, w_vg)], piece, into=into, put=owner(s))
+
+    pqks = project_qks(normed, 0, qks_buffer)
+    pvg = vg_buffer
+    pieces = [normed]
+    for s in range(1, size):
+        send = pieces[-1]
+        if s == 1:
+            send, w_gate, w_up, cotangent = tie(send, w_gate, w_up, cotangent)
+        item = step(send, size)
+        if s == 1:
+            w_gu = alternate(w_gate, w_up)
+            grad_mlp = (mask * cotangent.astype(F32)).astype(BF)
+            item, w_gu, grad_mlp = tie(item, w_gu, grad_mlp)
+        if s == size - 1:
+            for place, early in enumerate(pieces):
+                pvg = project_vg(early, place, pvg)
+            item, pqks, pvg, w_gu, w_down = tie(item, pqks, pvg, w_gu, w_down)
+        elif s > 1:
+            item, pqks = tie(item, pqks)
+        pqks = project_qks(item, s, pqks)
+        pieces.append(item)
+    normed_pieces = pieces
+    w_gu_other = opposite(w_gu)
+    w_down_other = opposite(w_down)
+    pvg = project_vg(item, size - 1, pvg)
+
+    cq = lax.dynamic_slice_in_dim(conv_query, me * key_width, key_width, 1)
+    ck = lax.dynamic_slice_in_dim(conv_key, me * key_width, key_width, 1)
+    cv = lax.dynamic_slice_in_dim(conv_value, me * value_width, value_width, 1)
     log_local = lax.dynamic_slice_in_dim(decay_log, me * heads, heads, 0)
     bias_local = lax.dynamic_slice_in_dim(decay_bias, me * heads, heads, 0)
     mixed, t_kept, s_kept, f_kept = mixer_forward(
         pqks, pvg, cq, ck, cv, log_local, bias_local, gain_head
     )
-    attended = scatter_ring(
-        lambda s: matmul(take(mixed, s), wo_full, batch_nt), size, size
-    )
-    middle = inputs32 + mask * attended
-    n_two, r_two = norm_parts(middle)
-    normed_two = (n_two * gain_mlp).astype(BF)
-    cot32 = cotangent.astype(F32)
-    grad_mlp = (mask * cot32).astype(BF)
-
-    group = GROUP or size
-    second = [x.reshape(flat_piece, width) for x in gather_ring(normed_two, size, group)]
-    grad_out = [x.reshape(flat_piece, width) for x in gather_ring(grad_mlp, size, group)]
-    hidden, grad_gate, grad_up = [], [], []
-    for x, g in zip(second, grad_out):
-        gate = matmul(x, wgate_full)
-        up = matmul(x, wup_full)
-        sig = jax.nn.sigmoid(gate)
-        act = gate * sig
-        hidden.append((act * up).astype(BF))
-        back = matmul(g, wdown_full)
-        grad_gate.append((back * up * sig * (1.0 + gate * (1.0 - sig))).astype(BF))
-        grad_up.append((back * act).astype(BF))
-    shape3 = (rows, piece, width)
-    grad_normed_two = scatter_ring(
-        lambda s: matmul(grad_gate[s], wgate_full, NT) + matmul(grad_up[s], wup_full, NT),
-        size, group,
-    ).reshape(shape3)
-    grad_gain_mlp = jnp.sum(grad_normed_two * n_two, axis=(0, 1))
-    grad_middle = cot32 + norm_back(n_two, r_two, gain_mlp, grad_normed_two)
-    grad_attn = (mask * grad_middle).astype(BF)
-    grad_attn_pieces = gather_ring(grad_attn, size, size)
-    grad_mixed = jnp.zeros((rows, length, heads * DV), F32)
-    grad_attn_all = jnp.zeros((rows, length, width), BF)
-    for s, item in enumerate(grad_attn_pieces):
-        grad_mixed = put(grad_mixed, matmul(item, wo_full, batch_nn), s)
-        grad_attn_all = put(grad_attn_all, item, s)
-
-    mlp_out = scatter_ring(
-        lambda s: matmul(hidden[s], wdown_full, NT), size, group
-    ).reshape(shape3)
-    mixed_rows = (middle + mask * mlp_out).astype(BF)
-    second_all = jnp.concatenate(second, axis=0)
-    grad_wdown = matmul(jnp.concatenate(grad_out, axis=0), jnp.concatenate(hidden, axis=0), TN)
-    grad_wgate = matmul(second_all, jnp.concatenate(grad_gate, axis=0), TN)
-    grad_wup = matmul(second_all, jnp.concatenate(grad_up, axis=0), TN)
-
-    def scatter_weight(g):
-        return lax.psum_scatter(g.astype(BF), "dp", scatter_dimension=0, tiled=True).astype(F32)
-
-    out_wdown = scatter_weight(grad_wdown)
-    out_wgate = scatter_weight(grad_wgate)
-    out_wup = scatter_weight(grad_wup)
-    flat = lambda x: x.reshape(rows * length, x.shape[2])
-    out_wout = scatter_weight(matmul(flat(grad_attn_all), flat(mixed), TN))
-
-    gqks, gvg, dcq, dck, dcv, dsm, dgain = mixer_backward(
-        grad_mixed, pqks, pvg, cq, ck, cv, log_local, bias_local, gain_head,
-        t_kept, s_kept, f_kept,
-    )
-    gain_sums = []
-
-    def part_one(s):
-        part = matmul(take(gqks, s), w_qks, batch_nt) + matmul(take(gvg, s), w_vg, batch_nt)
-        gain_sums.append(jnp.sum(part * take(normed_all, s).astype(F32), axis=(0, 1)))
-        return part
-
-    grad_normed = scatter_ring(part_one, size, size)
-    out_qks = scatter_weight(matmul(flat(normed_all), flat(gqks), TN))
-    out_vg = scatter_weight(matmul(flat(normed_all), flat(gvg), TN))
-    tokens_grad = (grad_middle + norm_back(n_one, r_one, gain_attn, grad_normed)).astype(BF)
+    mixed, w_gu_other, w_down_other = tie(mixed, w_gu_other, w_down_other)
+    wgu_full = [gather_weight(w_gu), gather_weight(w_gu_other)]
+    wdown_full = [gather_weight(w_down), gather_weight(w_down_other)]
+
+    def attn_part(s, dtype=F32):
+        return rows_matmul([(mixed, wo_full)], piece, nt=True, take=owner(s), dtype=dtype)
+
+    total = attn_part(1, BF)
+    for s in range(2, size + 1):
+        moved = step(total, size)
+        own = attn_part(s % size)
+        moved, own = tie(moved, own)
+        total = (own + moved.astype(F32)).astype(BF)
+    middle, normed_two = by_rows(middle_kernel, at, [own, moved, tokens], gain_mlp, [F32, BF])
+    flat2 = lambda x: x.reshape(flat_piece, width)
+    second, grad_out = [normed_two], [grad_mlp]
+    hidden, grad_gu = [[], []], [[], []]
+
+    def keep_block(b, block):
+        hidden[b].append(block[0].reshape(rows, piece, -1))
+        grad_gu[b].append(block[1].reshape(rows, piece, -1))
+
+    def mlp_part(s, dtype=F32):
+        pairs = [(hidden[b][s], wdown_full[b]) for b in range(2)]
+        return rows_matmul(pairs, piece, nt=True, dtype=dtype)
+
+    def two_part(s, dtype=F32):
+        pairs = [(grad_gu[b][s], wgu_full[b]) for b in range(2)]
+        return rows_matmul(pairs, piece, nt=True, dtype=dtype)
+
+    send, own_x, own_g = tie(normed_two, normed_two, grad_mlp)
+    for s in range(1, group):
+        moved = step(send, group)
+        if s == 1:
+            for b in range(2):
+                keep_block(b, mlp_block(flat2(own_g), wdown_full[b], flat2(own_x), wgu_full[b]))
+            moved, *held = tie(moved, *hidden[0], *hidden[1], *grad_gu[0], *grad_gu[1])
+            hidden, grad_gu = [held[:1], held[1:2]], [held[2:3], held[3:]]
+        second.append(moved)
+        send = moved
+    send, *second = tie(grad_mlp, *second)
+    for s in range(1, group):
+        moved = step(send, group)
+        if s == 1:
+            own_two = two_part(0)
+            begun = [
+                [matmul(flat2(x), wgu_full[b]) for b in range(2)] for x in second[1:]
+            ]
+            begun = [x for pair in begun for x in pair]
+            moved, own_two, *begun = tie(moved, own_two, *begun)
+        grad_out.append(moved)
+        send = moved
+    for s in range(1, group):
+        for b in range(2):
+            both = begun[2 * (s - 1) + b]
+            keep_block(b, mlp_block(flat2(grad_out[s]), wdown_full[b], both=both))
+    total, hidden[0][1], hidden[1][1] = tie(two_part(1, BF), hidden[0][1], hidden[1][1])
+    for s in range(2, group + 1):
+        moved = step(total, group)
+        if s == group:
+            own = own_two
+            own_mlp, send_mlp = mlp_part(0), mlp_part(1, BF)
+            moved, own_mlp, send_mlp = tie(moved, own_mlp, send_mlp)
+        else:
+            own = two_part(s)
+            total = (own + moved.astype(F32)).astype(BF)
+    grad_middle, grad_attn, dgain_mlp = by_rows(
+        middle_back_kernel, at, [own, moved, middle, cotangent], gain_mlp, [F32, BF], True
+    )
+
+    pair_gu, pair_down = [None, None], [None, None]
+    first = [0] * group
+    mixed_buffer = jax.ShapeDtypeStruct((rows, length, value_width), F32)
+    grad_mixed = mixed_buffer
+    attn_pieces = [grad_attn]
+    for s in range(1, size):
+        send = attn_pieces[-1]
+        if s < 3:
+            b = 2 - s
+            send, *held = tie(send, *hidden[b], *grad_gu[b])
+            hidden[b], grad_gu[b] = held[:group], held[group:]
+        item = step(send, size)
+        if s < 3:
+            pair_down[b] = outer_halves(grad_out, hidden[b], first, hidden[b][0].shape[2])
+            pair_gu[b] = outer_halves(second, grad_gu[b], first, 1408)
+            item, pair_gu[b], pair_down[b] = tie(item, pair_gu[b], pair_down[b])
+        if s == size - 1:
+            for place, early in enumerate(attn_pieces):
+                grad_mixed = rows_matmul(
+                    [(early, wo_full)], piece, into=grad_mixed, put=owner(place)
+                )
+            wout_parts = [
+                outer_sum(
+                    attn_pieces, [mixed] * s, [owner(x) for x in range(s)], side, data, dtype=F32
+                )
+                for side in (1 - core, core)
+            ]
+            item, grad_mixed, *wout_parts = tie(item, grad_mixed, *wout_parts)
+        attn_pieces.append(item)
+    grad_mixed = rows_matmul([(item, wo_full)], piece, into=grad_mixed, put=owner(size - 1))
+    sums_gu = [None, scatter_weight(pair_gu[1])]
+    sums_down = [None, scatter_weight(pair_down[1])]
+    sums_gu[0] = scatter_weight(pair_gu[0])
+    sums_down[0] = scatter_weight(pair_down[0])
+
+    grad_mixed, send_mlp, send_gu, send_down = tie(grad_mixed, send_mlp, sums_gu[1], sums_down[1])
+    moved = step(send_mlp, group)
+    moved_gu, moved_down = opposite(send_gu), opposite(send_down)
+    done = mixer_backward(
+        grad_mixed, pqks, pvg, cq, ck, cv, log_local, bias_local, gain_head, t_kept, s_kept, f_kept
+    )
+    moved, moved_gu, moved_down, gqks, gvg, dcq, dck, dcv, dsm, dgain = tie(
+        moved, moved_gu, moved_down, *done
+    )
+    for s in range(2, group):
+        moved = step((mlp_part(s) + moved.astype(F32)).astype(BF), group)
+    mixed_rows = by_rows(result_kernel, at, [own_mlp, moved, middle], None, [BF])[0]
+
+    def one_part(s, dtype=F32):
+        return rows_matmul(
+            [(gqks, w_qks), (gvg, w_vg)], piece, nt=True, take=owner(s),
+            weigh=normed_pieces[s], dtype=dtype,
+        )
+
+    places = [owner(s) for s in range(size)]
+    total, gain_sum = one_part(1, BF)
+    for s in range(2, size + 1):
+        if s == 2:
+            total, gvg = tie(total, gvg)
+        elif s == 3:
+            total, gqks, *last = tie(total, gqks, sums_down[0], sums_gu[0], attn_pieces[-1])
+            sums_down[0], sums_gu[0], attn_last = last
+        moved = step(total, size)
+        own, gain_part = one_part(s % size)
+        if s == 2:
+            pair_vg = outer_halves(normed_pieces, [gvg] * size, places)
+            moved, own, gain_part, pair_vg = tie(moved, own, gain_part, pair_vg)
+        elif s == 3:
+            pair_qks = outer_halves(normed_pieces, [gqks] * size, places, gqks.shape[2])
+            moved, own, gain_part, pair_qks = tie(moved, own, gain_part, pair_qks)
+        else:
+            moved, own, gain_part = tie(moved, own, gain_part)
+        gain_sum = gain_sum + gain_part
+        if s < size:
+            total = (own + moved.astype(F32)).astype(BF)
+    away = outer_sum([attn_last], [mixed], places[-1:], 1 - core, data, 512, wout_parts[:1])
+    crossed = lax.ppermute(away, "dp", swap(data, 1))
+    pair_wout = outer_sum(
+        [attn_last], [mixed], places[-1:], core, data, 512, (wout_parts[1], crossed)
+    )
+    pair_wout, own, moved = tie(pair_wout, own, moved)
+    tokens_grad = by_rows(
+        leave_kernel, at, [own, moved, tokens, grad_middle], gain_attn, [BF]
+    )[0]
+    out_vg = scatter_weight(pair_vg).astype(F32)
+    out_wout = scatter_weight(pair_wout).astype(F32)
+    out_qks = scatter_weight(pair_qks).astype(F32)
+    out_wgate, out_wup = apart(sums_gu[0].astype(F32) + moved_gu.astype(F32))
+    out_wdown = sums_down[0].astype(F32) + moved_down.astype(F32)
 
     def spread(part, axis):
         shape = part.shape[:axis] + (size,) + part.shape[axis:]
@@ -622,8 +1010,8 @@
         return whole.reshape(part.shape[:axis] + (size * part.shape[axis],) + part.shape[axis + 1 :])
 
     small = (
-        sum(gain_sums) / gain_attn,
-        grad_gain_mlp,
+        gain_sum / gain_attn,
+        dgain_mlp[0],
         dgain[0],
         spread(dcq[:4], 1),
         spread(dck[:4], 1),
@@ -631,20 +1019,17 @@
         spread(dsm[0, :heads], 0),
         spread(dsm[1, :heads], 0),
     )
-    lane_sizes = [x.size for x in small]
-    total = sum(lane_sizes)
+    total = sum(x.size for x in small)
     padded = -(-total // 1024) * 1024
     packed = jnp.concatenate(
         [x.reshape(-1) for x in small] + [jnp.zeros((padded - total,), F32)]
     ).reshape(padded // 128, 128)
-    packed = sum_small(packed, {"dp": lax.axis_size("dp"), "head": size}).reshape(-1)
+    packed = sum_small(packed, {"dp": data, "head": size}).reshape(-1)
     sums = []
-    at = 0
+    start = 0
     for x in small:
-        sums.append(packed[at : at + x.size].reshape(x.shape))
-        at = at + x.size
-    key_width = heads * DK
-    value_width = heads * DV
+        sums.append(packed[start : start + x.size].reshape(x.shape))
+        start = start + x.size
     return (
         mixed_rows,
         tokens_grad,
@@ -668,7 +1053,6 @@
         out_wdown,
     )
 
-
 def solution(mesh):
     rows = P("dp", "head", None)
     weight = P("dp", "head")

time: 1460 us -> 1200 us (0.82)
  Pallas kernels: 162 us -> 611 us
  matrix products: 410 us -> 26.6 us
  waiting for transfers between devices: 738 us -> 368 us
  local copies, waits for them, and re-layouts: 74.2 us -> 120 us
  other arithmetic: 49.5 us -> 28.7 us
    pallas_call x0 -> x49, Pallas kernels: none -> 450 us  [the longest x24 210 us: rows_matmul(): pl.pallas_call(functools.partial(rows_kernel, len(pairs), nt, weigh is no...]
    dot_general x54 -> x2, matrix products: 410 us -> 26.6 us  [matmul(): return lax.dot_general(a, b, NN, preferred_element_type=F32)]
    ppermute x24 -> x27, waiting for transfers between devices: 726 us -> 348 us  [the longest x16 334 us: step(): return lax.ppermute(x, 'head', ring(size, group))]
    unnamed x163 -> x209, local copies, waits for them, and re-layouts: 28.1 us -> 78.8 us
    dynamic_update_slice x6 -> x0, local copies, waits for them, and re-layouts: 19.9 us -> none  [put(): return lax.dynamic_update_slice_in_dim(whole, part, owner(s) * piece, 1)]
    convert_element_type x11 -> x6, other arithmetic: 31.7 us -> 17.2 us  [the longest x4 11.8 us: per_device(): total = (own + moved.astype(F32)).astype(BF)]
  transfers between devices with their start and end apart: 41 -> 46, of which waited for: 25 -> 19; matrix products, arithmetic and copies ran while one was open for 33% -> 8% of each run, Pallas kernels for 11% -> 46%
where the time goes in v2:
time: 1200 us; the launch traced here: 1190 us
  Pallas kernels  611 us (51%)
  waiting for transfers between devices  368 us (31%)
  local copies, waits for them, and re-layouts  120 us (10%)
  other arithmetic  28.7 us (2%)
  matrix products  26.6 us (2%)
  starting transfers between devices  18.9 us (2%)
  between operations  15.9 us (1%)
    ppermute x16, waiting for transfers between devices, step(): return lax.ppermute(x, 'head', ring(size, group))  334 us
    pallas_call x24, Pallas kernels, rows_matmul(): pl.pallas_call(functools.partial(rows_kernel, len(pairs), nt, weigh is no...  210 us
    pallas_call x16, Pallas kernels, outer_sum(): pl.pallas_call(functools.partial(outer_kernel, len(xs), data // 2), grid_...  163 us
    pallas_call x1, Pallas kernels, mixer_backward(): pl.pallas_call(functools.partial(mixer_backward_kernel, heads), grid=(row...  97.6 us
    unnamed x209, local copies, waits for them, and re-layouts  78.8 us
    pallas_call x1, Pallas kernels, mixer_forward(): pl.pallas_call(functools.partial(mixer_forward_kernel, heads), grid=(rows...  64 us
    pallas_call x4, Pallas kernels, mlp_block(): pl.pallas_call(functools.partial(kernel, lanes_of(units)), grid=(pl.cdiv(...  47.8 us
    pallas_call x5, Pallas kernels, by_rows(): pl.pallas_call(kernel, grid_spec=pltpu.PrefetchScalarGridSpec(num_scalar_...  28.9 us
  transfers between devices with their start and end apart: 46, of which 19 were waited for; matrix products, arithmetic and copies ran while one was open for 8% of the time, Pallas kernels for 46%

profile of v2, /device:TPU:0, one launch (start us, length us, event | category | flops | bytes accessed | tf_op | source)
XLA Modules:
  0.0 1189.8 jit_solution(16966001068634568163)
XLA Ops:
  39.6 29.0 %collective-permute-done.refs_0_.refs_4_.refs_1_ = bf16[1,512,2048]{2,1,0:T(8,128)(2,1)} collective-permute-done((bf16[1,512,2048]{2,1,0:T(8,128)(2,1)S(1)}, bf16[1,512,2048]{2,1,0:T(8,128)(2,1)}, u32[]{:S(2)}, u32[]{:S(2)}) %collective-permute-start) | collective-permute-done | bytes 2097184 | tf_op jit(solution)/shard_map/ppermute | solution.py:780
  82.4 35.2 %collective-permute-done.1.refs_0_.refs_4_.refs_2_ = bf16[1,512,2048]{2,1,0:T(8,128)(2,1)} collective-permute-done((bf16[1,512,2048]{2,1,0:T(8,128)(2,1)}, bf16[1,512,2048]{2,1,0:T(8,128)(2,1)}, u32[]{:S(2)}, u32[]{:S(2)}) %collective-permute-start.1) | collective-permute-done | bytes 2097184 | tf_op jit(solution)/shard_map/ppermute | solution.py:780
  190.1 64.0 %mixer_forward.1 = (bf16[1,2048,1024]{2,1,0:T(8,128)(2,1)S(1)}, bf16[1,16,4,128,128]{4,3,2,1,0:T(8,128)(2,1)S(1)}, bf16[1,16,4,128,256]{4,3,2,1,0:T(8,128)(2,1)S(1)}, bf16[1,2048,1024]{2,1,0:T(8,128)(2,1)}) custom-call(f32[1,2048,1152]{2,1,0:T(8,128)} %rows_matmul.30.pq.pk.ps.tq.tk, f32[1,2048,1152]{2,1,0:T(8,128)} %rows_matmul.30.pq.pk.ps.tq.tk, ...), custom_call_target="tpu_custom_call" | custom-call | bytes 224000000 | tf_op jit(solution)/shard_map/mixer_forward/pallas_call | solution.py:345
  273.7 42.8 %collective-permute-done.5 = bf16[1,512,2048]{2,1,0:T(8,128)(2,1)S(1)} collective-permute-done((bf16[1,512,2048]{2,1,0:T(8,128)(2,1)S(1)}, bf16[1,512,2048]{2,1,0:T(8,128)(2,1)S(1)}, u32[]{:S(2)}, u32[]{:S(2)}) %collective-permute-start.5) | collective-permute-done | bytes 2097184 | tf_op jit(solution)/shard_map/ppermute | solution.py:780
  323.0 42.0 %collective-permute-done.6 = bf16[1,512,2048]{2,1,0:T(8,128)(2,1)S(1)} collective-permute-done((bf16[1,512,2048]{2,1,0:T(8,128)(2,1)S(1)}, bf16[1,512,2048]{2,1,0:T(8,128)(2,1)S(1)}, u32[]{:S(2)}, u32[]{:S(2)}) %collective-permute-start.6) | collective-permute-done | bytes 2097184 | tf_op jit(solution)/shard_map/ppermute | solution.py:780
  374.0 38.8 %collective-permute-done.7.moved = bf16[1,512,2048]{2,1,0:T(8,128)(2,1)S(1)} collective-permute-done((bf16[1,512,2048]{2,1,0:T(8,128)(2,1)S(1)}, bf16[1,512,2048]{2,1,0:T(8,128)(2,1)S(1)}, u32[]{:S(2)}, u32[]{:S(2)}) %collective-permute-start.7) | collective-permute-done | bytes 2097184 | tf_op jit(solution)/shard_map/ppermute | solution.py:780
  419.1 15.1 %mlp_block.4 = (bf16[512,1408]{1,0:T(8,128)(2,1)S(1)}, bf16[512,2816]{1,0:T(8,128)(2,1)S(1)}) custom-call(bf16[512,2048]{1,0:T(8,128)(2,1)} %bitcast.13.x, bf16[2048,2816]{1,0:T(8,128)(2,1)} %all-gather.14.cloned.1.call-done.wgu.refs_1_, bf16[512,2048]{1,0:T(8,128)(2,1)} %bitcast.14.g, bf16[2048,1408]{1,0:T(8,128)(2,1)} %all-gather.16.cloned.1.call-done.wd.refs_1_), custom_call_target="tpu_custom_call" | custom-call | tf_op jit(solution)/shard_map/mlp_block/pallas_call | solution.py:594
  436.9 15.1 %mlp_block.5 = (bf16[512,1408]{1,0:T(8,128)(2,1)S(1)}, bf16[512,2816]{1,0:T(8,128)(2,1)S(1)}) custom-call(bf16[512,2048]{1,0:T(8,128)(2,1)} %bitcast.13.x, bf16[2048,2816]{1,0:T(8,128)(2,1)} %all-gather.18.cloned.1.call-done.wgu.refs_3_, bf16[512,2048]{1,0:T(8,128)(2,1)} %bitcast.14.g, bf16[2048,1408]{1,0:T(8,128)(2,1)} %all-gather.20.cloned.1.call-done.wd.refs_3_), custom_call_target="tpu_custom_call" | custom-call | tf_op jit(solution)/shard_map/mlp_block/pallas_call | solution.py:594
  452.1 12.8 %collective-permute-done.8.refs_1_ = bf16[1,512,2048]{2,1,0:T(8,128)(2,1)} collective-permute-done((bf16[1,512,2048]{2,1,0:T(8,128)(2,1)}, bf16[1,512,2048]{2,1,0:T(8,128)(2,1)}, u32[]{:S(2)}, u32[]{:S(2)}) %collective-permute-start.8) | collective-permute-done | bytes 2097184 | tf_op jit(solution)/shard_map/ppermute | solution.py:780
  464.9 12.6 %fusion.both = f32[512,2816]{1,0:T(8,128)} fusion(bf16[2048,2816]{1,0:T(8,128)(2,1)} %all-gather.18.cloned.1.call-done.wgu.refs_3_, bf16[1,512,2048]{2,1,0:T(8,128)(2,1)} %collective-permute-done.8.refs_1_), kind=kOutput, calls=%fused_computation.6 | convolution fusion | flops 5905580032 | bytes 19398656 | tf_op jit(solution)/shard_map/dot_general | solution.py:711
  477.5 16.2 %rows_matmul.36.own = f32[1,512,2048]{2,1,0:T(8,128)S(1)} custom-call(s32[2]{0:T(128)S(1)} %broadcast_6_at.2.at, bf16[1,512,2816]{2,1,0:T(8,128)(2,1)S(1)} %bitcast.75, bf16[2048,2816]{1,0:T(8,128)(2,1)} %all-gather.14.cloned.1.call-done.wgu.refs_1_, bf16[1,512,2816]{2,1,0:T(8,128)(2,1)S(1)} %bitcast.81, ...), custom_call_target="tpu_custom_call" | custom-call | tf_op jit(solution)/shard_map/rows_matmul/pallas_call | solution.py:476
  493.7 14.0 %fusion.2.both = f32[512,2816]{1,0:T(8,128)} fusion(bf16[2048,2816]{1,0:T(8,128)(2,1)} %all-gather.14.cloned.1.call-done.wgu.refs_1_, bf16[1,512,2048]{2,1,0:T(8,128)(2,1)} %collective-permute-done.8.refs_1_), kind=kOutput, calls=%fused_computation.8 | convolution fusion | flops 5905580032 | bytes 19398656 | tf_op jit(solution)/shard_map/dot_general | solution.py:711
  531.9 16.8 %rows_matmul.37 = bf16[1,512,2048]{2,1,0:T(8,128)(2,1)} custom-call(s32[2]{0:T(128)S(1)} %broadcast_6_at.2.at, bf16[1,512,2816]{2,1,0:T(8,128)(2,1)S(1)} %bitcast.78, bf16[2048,2816]{1,0:T(8,128)(2,1)} %all-gather.14.cloned.1.call-done.wgu.refs_1_, bf16[1,512,2816]{2,1,0:T(8,128)(2,1)S(1)} %bitcast.84, ...), custom_call_target="tpu_custom_call" | custom-call | tf_op jit(solution)/shard_map/rows_matmul/pallas_call | solution.py:476
  576.4 14.9 %collective-permute-done.10.moved = bf16[1,512,2048]{2,1,0:T(8,128)(2,1)} collective-permute-done((bf16[1,512,2048]{2,1,0:T(8,128)(2,1)}, bf16[1,512,2048]{2,1,0:T(8,128)(2,1)}, u32[]{:S(2)}, u32[]{:S(2)}) %collective-permute-start.10) | collective-permute-done | bytes 2097184 | tf_op jit(solution)/shard_map/ppermute | solution.py:780
  602.3 12.5 %outer_sum.16 = bf16[1024,2816]{1,0:T(8,128)(2,1)} custom-call(s32[3]{0:T(128)S(1)} %stack.62.at, bf16[1,512,2048]{2,1,0:T(8,128)(2,1)} %get-tuple-element.246.refs_0_, bf16[1,512,2048]{2,1,0:T(8,128)(2,1)} %collective-permute-done.8.refs_1_, bf16[1,512,2816]{2,1,0:T(8,128)(2,1)S(1)} %bitcast.82, bf16[1,512,2816]{2,1,0:T(8,128)(2,1)S(1)} %bitcast.85), custom_call_target="tpu_custom_call" | custom-call | tf_op jit(solution)/shard_map/outer_sum/pallas_call | solution.py:539
  641.6 13.4 %outer_sum.17 = bf16[1024,2816]{1,0:T(8,128)(2,1)} custom-call(s32[3]{0:T(128)S(1)} %stack.60.at, bf16[1,512,2048]{2,1,0:T(8,128)(2,1)} %get-tuple-element.246.refs_0_, bf16[1,512,2048]{2,1,0:T(8,128)(2,1)} %collective-permute-done.8.refs_1_, bf16[1,512,2816]{2,1,0:T(8,128)(2,1)S(1)} %bitcast.83, bf16[1,512,2816]{2,1,0:T(8,128)(2,1)S(1)} %bitcast.86, ...), custom_call_target="tpu_custom_call" | custom-call | tf_op jit(solution)/shard_map/outer_sum/pallas_call | solution.py:539
  655.0 15.8 %collective-permute-done.11.refs_0_.refs_1_ = bf16[1,512,2048]{2,1,0:T(8,128)(2,1)} collective-permute-done((bf16[1,512,2048]{2,1,0:T(8,128)(2,1)}, bf16[1,512,2048]{2,1,0:T(8,128)(2,1)}, u32[]{:S(2)}, u32[]{:S(2)}) %collective-permute-start.11) | collective-permute-done | bytes 2097184 | tf_op jit(solution)/shard_map/ppermute | solution.py:780
  675.2 12.5 %outer_sum.20 = bf16[1024,2816]{1,0:T(8,128)(2,1)} custom-call(s32[3]{0:T(128)S(1)} %stack.62.at, bf16[1,512,2048]{2,1,0:T(8,128)(2,1)} %get-tuple-element.246.refs_0_, bf16[1,512,2048]{2,1,0:T(8,128)(2,1)} %collective-permute-done.8.refs_1_, bf16[1,512,2816]{2,1,0:T(8,128)(2,1)S(1)} %bitcast.76, bf16[1,512,2816]{2,1,0:T(8,128)(2,1)S(1)} %bitcast.79), custom_call_target="tpu_custom_call" | custom-call | tf_op jit(solution)/shard_map/outer_sum/pallas_call | solution.py:539
  714.7 13.4 %outer_sum.21 = bf16[1024,2816]{1,0:T(8,128)(2,1)} custom-call(s32[3]{0:T(128)S(1)} %stack.60.at, bf16[1,512,2048]{2,1,0:T(8,128)(2,1)} %get-tuple-element.246.refs_0_, bf16[1,512,2048]{2,1,0:T(8,128)(2,1)} %collective-permute-done.8.refs_1_, bf16[1,512,2816]{2,1,0:T(8,128)(2,1)S(1)} %bitcast.77, bf16[1,512,2816]{2,1,0:T(8,128)(2,1)S(1)} %bitcast.80, ...), custom_call_target="tpu_custom_call" | custom-call | tf_op jit(solution)/shard_map/outer_sum/pallas_call | solution.py:539
  728.1 16.1 %collective-permute-done.14.refs_0_.refs_2_ = bf16[1,512,2048]{2,1,0:T(8,128)(2,1)} collective-permute-done((bf16[1,512,2048]{2,1,0:T(8,128)(2,1)}, bf16[1,512,2048]{2,1,0:T(8,128)(2,1)}, u32[]{:S(2)}, u32[]{:S(2)}) %collective-permute-start.14) | collective-permute-done | bytes 2097184 | tf_op jit(solution)/shard_map/ppermute | solution.py:780
  804.4 97.6 %mixer_backward.1 = (bf16[1,2048,1152]{2,1,0:T(8,128)(2,1)}, bf16[1,2048,2048]{2,1,0:T(8,128)(2,1)}, f32[8,512]{1,0:T(8,128)S(1)}, f32[8,512]{1,0:T(8,128)S(1)},...) custom-call(f32[1,2048,1024]{2,1,0:T(8,128)} %rows_matmul.43.dm, ...), custom_call_target="tpu_custom_call" | custom-call | bytes 339500000 | tf_op jit(solution)/shard_map/mixer_backward/pallas_call | solution.py:390
  904.4 12.9 %rows_matmul.44 = (bf16[1,512,2048]{2,1,0:T(8,128)(2,1)}, f32[1,8,2048]{2,1,0:T(8,128)S(1)}) custom-call(s32[2]{0:T(128)S(1)} %copy-done.87, bf16[1,2048,1152]{2,1,0:T(8,128)(2,1)S(1)} %copy-done.2, bf16[2048,1152]{1,0:T(8,128)(2,1)} %all-gather.8.cloned.1.call-done.refs_1_, ...), custom_call_target="tpu_custom_call" | custom-call | tf_op jit(solution)/shard_map/rows_matmul/pallas_call | solution.py:476
  917.3 16.0 %outer_sum.26 = bf16[1024,2048]{1,0:T(8,128)(2,1)} custom-call(s32[5]{0:T(128)S(1)} %stack.67.at, bf16[1,512,2048]{2,1,0:T(8,128)(2,1)S(1)} %enter_kernel.1.refs_0_.refs_4_, bf16[1,512,2048]{2,1,0:T(8,128)(2,1)} %collective-permute-done.refs_0_.refs_4_.refs_1_, bf16[1,512,2048]{2,1,0:T(8,128)(2,1)} %collective-permute-done.1.refs_0_.refs_4_.refs_2_, ...), custom_call_target="tpu_custom_call" | custom-call | tf_op jit(solution)/shard_map/outer_sum/pallas_call | solution.py:539
  935.5 12.8 %rows_matmul.45 = (f32[1,512,2048]{2,1,0:T(8,128)S(1)}, f32[1,8,2048]{2,1,0:T(8,128)S(1)}) custom-call(s32[2]{0:T(128)S(1)} %copy-done.85, bf16[1,2048,1152]{2,1,0:T(8,128)(2,1)} %get-tuple-element.293.refs_0_.refs_4_.refs_5_.refs_6_.refs_7_, bf16[2048,1152]{1,0:T(8,128)(2,1)} %all-gather.8.cloned.1.call-done.refs_1_, ...), custom_call_target="tpu_custom_call" | custom-call | tf_op jit(solution)/shard_map/rows_matmul/pallas_call | solution.py:476
  950.2 16.5 %outer_sum.27 = bf16[1024,2048]{1,0:T(8,128)(2,1)} custom-call(s32[5]{0:T(128)S(1)} %stack.66.at, bf16[1,512,2048]{2,1,0:T(8,128)(2,1)S(1)} %enter_kernel.1.refs_0_.refs_4_, bf16[1,512,2048]{2,1,0:T(8,128)(2,1)} %collective-permute-done.refs_0_.refs_4_.refs_1_, bf16[1,512,2048]{2,1,0:T(8,128)(2,1)} %collective-permute-done.1.refs_0_.refs_4_.refs_2_, ...), custom_call_target="tpu_custom_call" | custom-call | tf_op jit(solution)/shard_map/outer_sum/pallas_call | solution.py:539
  966.7 16.8 %collective-permute-done.21 = bf16[1,512,2048]{2,1,0:T(8,128)(2,1)} collective-permute-done((bf16[1,512,2048]{2,1,0:T(8,128)(2,1)}, bf16[1,512,2048]{2,1,0:T(8,128)(2,1)}, u32[]{:S(2)}, u32[]{:S(2)}) %collective-permute-start.21) | collective-permute-done | bytes 2097184 | tf_op jit(solution)/shard_map/ppermute | solution.py:780
  1000.4 13.0 %rows_matmul.46 = (f32[1,512,2048]{2,1,0:T(8,128)S(1)}, f32[1,8,2048]{2,1,0:T(8,128)S(1)}) custom-call(s32[2]{0:T(128)S(1)} %copy-done.83, bf16[1,2048,1152]{2,1,0:T(8,128)(2,1)} %get-tuple-element.293.refs_0_.refs_4_.refs_5_.refs_6_.refs_7_, bf16[2048,1152]{1,0:T(8,128)(2,1)} %all-gather.8.cloned.1.call-done.refs_1_, ...), custom_call_target="tpu_custom_call" | custom-call | tf_op jit(solution)/shard_map/rows_matmul/pallas_call | solution.py:476
  1016.8 12.5 %outer_sum.31 = bf16[1024,1152]{1,0:T(8,128)(2,1)} custom-call(s32[5]{0:T(128)S(1)} %stack.66.at, bf16[1,512,2048]{2,1,0:T(8,128)(2,1)S(1)} %enter_kernel.1.refs_0_.refs_4_, bf16[1,512,2048]{2,1,0:T(8,128)(2,1)} %collective-permute-done.refs_0_.refs_4_.refs_1_, bf16[1,512,2048]{2,1,0:T(8,128)(2,1)} %collective-permute-done.1.refs_0_.refs_4_.refs_2_, ...), custom_call_target="tpu_custom_call" | custom-call | tf_op jit(solution)/shard_map/outer_sum/pallas_call | solution.py:539
  1029.2 21.1 %collective-permute-done.24 = bf16[1,512,2048]{2,1,0:T(8,128)(2,1)} collective-permute-done((bf16[1,512,2048]{2,1,0:T(8,128)(2,1)}, bf16[1,512,2048]{2,1,0:T(8,128)(2,1)}, u32[]{:S(2)}, u32[]{:S(2)}) %collective-permute-start.24) | collective-permute-done | bytes 2097184 | tf_op jit(solution)/shard_map/ppermute | solution.py:780
  1062.5 12.1 %rows_matmul.47 = (f32[1,512,2048]{2,1,0:T(8,128)S(1)}, f32[1,8,2048]{2,1,0:T(8,128)S(1)}) custom-call(s32[2]{0:T(128)S(1)} %copy-done.81, bf16[1,2048,1152]{2,1,0:T(8,128)(2,1)} %get-tuple-element.293.refs_0_.refs_4_.refs_5_.refs_6_.refs_7_, bf16[2048,1152]{1,0:T(8,128)(2,1)} %all-gather.8.cloned.1.call-done.refs_1_, ...), custom_call_target="tpu_custom_call" | custom-call | tf_op jit(solution)/shard_map/rows_matmul/pallas_call | solution.py:476
  1076.6 29.4 %collective-permute-done.26.moved = bf16[1,512,2048]{2,1,0:T(8,128)(2,1)} collective-permute-done((bf16[1,512,2048]{2,1,0:T(8,128)(2,1)}, bf16[1,512,2048]{2,1,0:T(8,128)(2,1)}, u32[]{:S(2)}, u32[]{:S(2)}) %collective-permute-start.26) | collective-permute-done | bytes 2097184 | tf_op jit(solution)/shard_map/ppermute | solution.py:780
  1166.7 14.2 %reduce-scatter.20.cloned.1.call-done = bf16[256,1024]{1,0:T(8,128)(2,1)} async-done(((bf16[1024,1024]{1,0:T(8,128)(2,1)}), bf16[256,1024]{1,0:T(8,128)(2,1)}) %reduce-scatter.20.cloned.1.call-update) | async-done | bytes 524304 | tf_op jit(solution)/shard_map/reduce_scatter | solution.py:795
  (422 shorter events, 446.0 us)
Async XLA Ops:
  7.2 61.6 %all-gather.8.cloned.1.call-start = ((), (), s32[]{:S(2)}) async-start(), calls=%async_computation.7 | async-start | bytes 5308416 | tf_op jit(solution)/shard_map/all_gather | solution.py:786
  10.9 115.8 %all-gather.10.cloned.1.call-start = ((), (), s32[]{:S(2)}) async-start(), calls=%async_computation.8 | async-start | bytes 9437184 | tf_op jit(solution)/shard_map/all_gather | solution.py:786
  13.2 247.2 %all-gather.12.cloned.1.call-start = ((), (), s32[]{:S(2)}) async-start(), calls=%async_computation.9 | async-start | bytes 4718592 | tf_op jit(solution)/shard_map/all_gather | solution.py:786
  14.0 405.1 %all-gather.16.cloned.1.call-start = ((), (), s32[]{:S(2)}) async-start(), calls=%async_computation.11 | async-start | bytes 6488064 | tf_op jit(solution)/shard_map/all_gather | solution.py:786
  17.8 50.8 %collective-permute-start = (bf16[1,512,2048]{2,1,0:T(8,128)(2,1)S(1)}, bf16[1,512,2048]{2,1,0:T(8,128)(2,1)}, u32[]{:S(2)}, u32[]{:S(2)}) collective-permute-start(bf16[1,512,2048]{2,1,0:T(8,128)(2,1)S(1)} %enter_kernel.1.refs_0_.refs_4_), channel_id=1, source_target_pairs={{0,1},{1,2},{2,3},{3,0},{4,5},{5,6},{6,7},{7,4},{8,9},{9,10},{10,1... | collective-permute-start | bytes 6291464 | tf_op jit(solution)/shard_map/ppermute | solution.py:780
  68.7 48.9 %collective-permute-start.1 = (bf16[1,512,2048]{2,1,0:T(8,128)(2,1)}, bf16[1,512,2048]{2,1,0:T(8,128)(2,1)}, u32[]{:S(2)}, u32[]{:S(2)}) collective-permute-start(bf16[1,512,2048]{2,1,0:T(8,128)(2,1)} %collective-permute-done.refs_0_.refs_4_.refs_1_), channel_id=1, source_target_pairs={{0,1},{1,2},{2,3},{3,0},{4,5},{5,6},{6,7},{7,4},{8,9},{9,10},{10,1... | collective-permute-start | bytes 6291464 | tf_op jit(solution)/shard_map/ppermute | solution.py:780
  117.6 48.0 %collective-permute-start.2 = (bf16[1,512,2048]{2,1,0:T(8,128)(2,1)}, bf16[1,512,2048]{2,1,0:T(8,128)(2,1)}, u32[]{:S(2)}, u32[]{:S(2)}) collective-permute-start(bf16[1,512,2048]{2,1,0:T(8,128)(2,1)} %collective-permute-done.1.refs_0_.refs_4_.refs_2_), channel_id=1, source_target_pairs={{0,1},{1,2},{2,3},{3,0},{4,5},{5,6},{6,7},{7,4},{8,9},{9,10},{10,1... | collective-permute-start | bytes 6291464 | tf_op jit(solution)/shard_map/ppermute | solution.py:780
  165.6 253.5 %all-gather.14.cloned.1.call-start = ((), (), s32[]{:S(2)}) async-start(), calls=%async_computation.10 | async-start | bytes 12976128 | tf_op jit(solution)/shard_map/all_gather | solution.py:786
  166.2 270.7 %all-gather.20.cloned.1.call-start = ((), (), s32[]{:S(2)}) async-start(), calls=%async_computation.13 | async-start | bytes 6488064 | tf_op jit(solution)/shard_map/all_gather | solution.py:786
  166.3 93.2 %collective-permute-start.3 = (bf16[256,2816]{1,0:T(8,128)(2,1)}, bf16[256,2816]{1,0:T(8,128)(2,1)}, u32[]{:S(2)}, u32[]{:S(2)}) collective-permute-start(bf16[256,2816]{1,0:T(8,128)(2,1)} %reshape.233), channel_id=1, source_target_pairs={{0,2},{1,3},{2,0},{3,1},{4,6},{5,7},{6,4},{7,5},{8,10},{9,11},{10,... | collective-permute-start | bytes 4325384 | tf_op jit(solution)/shard_map/ppermute | solution.py:783
  166.4 93.1 %collective-permute-start.4 = (bf16[256,1408]{1,0:T(8,128)(2,1)S(1)}, bf16[256,1408]{1,0:T(8,128)(2,1)}, u32[]{:S(2)}, u32[]{:S(2)}) collective-permute-start(bf16[256,1408]{1,0:T(8,128)(2,1)S(1)} %copy-done.96), channel_id=1, source_target_pairs={{0,2},{1,3},{2,0},{3,1},{4,6},{5,7},{6,4},{7,5},{8,10},{9,11},{10,... | collective-permute-start | bytes 2162696 | tf_op jit(solution)/shard_map/ppermute | solution.py:783
  259.5 177.4 %all-gather.18.cloned.1.call-start = ((), (), s32[]{:S(2)}) async-start(), calls=%async_computation.12 | async-start | bytes 12976128 | tf_op jit(solution)/shard_map/all_gather | solution.py:786
  260.3 539.4 %reduce-scatter.10.cloned.1.call-start = ((), (), s32[]{:S(2)}) async-start(), calls=%async_computation.15 | async-start | bytes 3604480 | tf_op jit(solution)/shard_map/reduce_scatter | solution.py:795
  268.0 48.6 %collective-permute-start.5 = (bf16[1,512,2048]{2,1,0:T(8,128)(2,1)S(1)}, bf16[1,512,2048]{2,1,0:T(8,128)(2,1)S(1)}, u32[]{:S(2)}, u32[]{:S(2)}) collective-permute-start(bf16[1,512,2048]{2,1,0:T(8,128)(2,1)S(1)} %rows_matmul.32), channel_id=1, source_target_pairs={{0,1},{1,2},{2,3},{3,0},{4,5},{5,6},{6,7},{7,4},{8,9},{9,10},{10,1... | collective-permute-start | bytes 6291464 | tf_op jit(solution)/shard_map/ppermute | solution.py:780
  317.3 47.6 %collective-permute-start.6 = (bf16[1,512,2048]{2,1,0:T(8,128)(2,1)S(1)}, bf16[1,512,2048]{2,1,0:T(8,128)(2,1)S(1)}, u32[]{:S(2)}, u32[]{:S(2)}) collective-permute-start(bf16[1,512,2048]{2,1,0:T(8,128)(2,1)S(1)} %add_convert_fusion.3), channel_id=1, source_target_pairs={{0,1},{1,2},{2,3},{3,0},{4,5},{5,6},{6,7},{7,4},{8,9},{9,10},{10,1... | collective-permute-start | bytes 6291464 | tf_op jit(solution)/shard_map/ppermute | solution.py:780
  365.7 47.1 %collective-permute-start.7 = (bf16[1,512,2048]{2,1,0:T(8,128)(2,1)S(1)}, bf16[1,512,2048]{2,1,0:T(8,128)(2,1)S(1)}, u32[]{:S(2)}, u32[]{:S(2)}) collective-permute-start(bf16[1,512,2048]{2,1,0:T(8,128)(2,1)S(1)} %add_convert_fusion.2), channel_id=1, source_target_pairs={{0,1},{1,2},{2,3},{3,0},{4,5},{5,6},{6,7},{7,4},{8,9},{9,10},{10,1... | collective-permute-start | bytes 6291464 | tf_op jit(solution)/shard_map/ppermute | solution.py:780
  419.1 45.8 %collective-permute-start.8 = (bf16[1,512,2048]{2,1,0:T(8,128)(2,1)}, bf16[1,512,2048]{2,1,0:T(8,128)(2,1)}, u32[]{:S(2)}, u32[]{:S(2)}) collective-permute-start(bf16[1,512,2048]{2,1,0:T(8,128)(2,1)} %get-tuple-element.246.refs_0_), channel_id=1, source_target_pairs={{0,1},{1,0},{2,3},{3,2},{4,5},{5,4},{6,7},{7,6},{8,9},{9,8},{10,11... | collective-permute-start | bytes 6291464 | tf_op jit(solution)/shard_map/ppermute | solution.py:780
  621.0 49.7 %collective-permute-start.11 = (bf16[1,512,2048]{2,1,0:T(8,128)(2,1)}, bf16[1,512,2048]{2,1,0:T(8,128)(2,1)}, u32[]{:S(2)}, u32[]{:S(2)}) collective-permute-start(bf16[1,512,2048]{2,1,0:T(8,128)(2,1)} %get-tuple-element.245.refs_0_), channel_id=1, source_target_pairs={{0,1},{1,2},{2,3},{3,0},{4,5},{5,6},{6,7},{7,4},{8,9},{9,10},{10,1... | collective-permute-start | bytes 6291464 | tf_op jit(solution)/shard_map/ppermute | solution.py:780
  670.8 128.9 %reduce-scatter.8.cloned.1.call-start = ((), (), s32[]{:S(2)}) async-start(), calls=%async_computation.14 | async-start | bytes 7208960 | tf_op jit(solution)/shard_map/reduce_scatter | solution.py:795
  671.5 316.9 %reduce-scatter.12.cloned.1.call-start = ((), (), s32[]{:S(2)}) async-start(), calls=%async_computation.16 | async-start | bytes 3604480 | tf_op jit(solution)/shard_map/reduce_scatter | solution.py:795
  694.0 50.2 %collective-permute-start.14 = (bf16[1,512,2048]{2,1,0:T(8,128)(2,1)}, bf16[1,512,2048]{2,1,0:T(8,128)(2,1)}, u32[]{:S(2)}, u32[]{:S(2)}) collective-permute-start(bf16[1,512,2048]{2,1,0:T(8,128)(2,1)} %collective-permute-done.11.refs_0_.refs_1_), channel_id=1, source_target_pairs={{0,1},{1,2},{2,3},{3,0},{4,5},{5,6},{6,7},{7,4},{8,9},{9,10},{10,1... | collective-permute-start | bytes 6291464 | tf_op jit(solution)/shard_map/ppermute | solution.py:780
  744.2 244.2 %reduce-scatter.14.cloned.1.call-start = ((), (), s32[]{:S(2)}) async-start(), calls=%async_computation.17 | async-start | bytes 7208960 | tf_op jit(solution)/shard_map/reduce_scatter | solution.py:795
  745.0 414.5 %reduce-scatter.16.cloned.1.call-start = ((), (), s32[]{:S(2)}) async-start(), calls=%async_computation.18 | async-start | bytes 2949120 | tf_op jit(solution)/shard_map/reduce_scatter | solution.py:795
  745.0 49.0 %collective-permute-start.17 = (bf16[1,512,2048]{2,1,0:T(8,128)(2,1)}, bf16[1,512,2048]{2,1,0:T(8,128)(2,1)S(1)}, u32[]{:S(2)}, u32[]{:S(2)}) collective-permute-start(bf16[1,512,2048]{2,1,0:T(8,128)(2,1)} %collective-permute-done.14.refs_0_.refs_2_), channel_id=1, source_target_pairs={{0,1},{1,2},{2,3},{3,0},{4,5},{5,6},{6,7},{7,4},{8,9},{9,10},{10,1... | collective-permute-start | bytes 6291464 | tf_op jit(solution)/shard_map/ppermute | solution.py:780
  799.7 102.4 %collective-permute-start.18 = (bf16[1,512,2048]{2,1,0:T(8,128)(2,1)}, bf16[1,512,2048]{2,1,0:T(8,128)(2,1)}, u32[]{:S(2)}, u32[]{:S(2)}) collective-permute-start(bf16[1,512,2048]{2,1,0:T(8,128)(2,1)} %copy-done.61), channel_id=1, source_target_pairs={{0,1},{1,0},{2,3},{3,2},{4,5},{5,4},{6,7},{7,6},{8,9},{9,8},{10,11... | collective-permute-start | bytes 6291464 | tf_op jit(solution)/shard_map/ppermute | solution.py:780
  799.7 102.3 %collective-permute-start.19 = (bf16[256,2816]{1,0:T(8,128)(2,1)}, bf16[256,2816]{1,0:T(8,128)(2,1)}, u32[]{:S(2)}, u32[]{:S(2)}) collective-permute-start(bf16[256,2816]{1,0:T(8,128)(2,1)} %reduce-scatter.8.cloned.1.call-done), channel_id=1, source_target_pairs={{0,2},{1,3},{2,0},{3,1},{4,6},{5,7},{6,4},{7,5},{8,10},{9,11},{10,... | collective-permute-start | bytes 4325384 | tf_op jit(solution)/shard_map/ppermute | solution.py:783
  799.9 102.1 %collective-permute-start.20 = (bf16[256,1408]{1,0:T(8,128)(2,1)}, bf16[256,1408]{1,0:T(8,128)(2,1)S(1)}, u32[]{:S(2)}, u32[]{:S(2)}) collective-permute-start(bf16[256,1408]{1,0:T(8,128)(2,1)} %reduce-scatter.10.cloned.1.call-done), channel_id=1, source_target_pairs={{0,2},{1,3},{2,0},{3,1},{4,6},{5,7},{6,4},{7,5},{8,10},{9,11},{10,... | collective-permute-start | bytes 2162696 | tf_op jit(solution)/shard_map/ppermute | solution.py:783
  933.3 50.2 %collective-permute-start.21 = (bf16[1,512,2048]{2,1,0:T(8,128)(2,1)}, bf16[1,512,2048]{2,1,0:T(8,128)(2,1)}, u32[]{:S(2)}, u32[]{:S(2)}) collective-permute-start(bf16[1,512,2048]{2,1,0:T(8,128)(2,1)} %get-tuple-element.281), channel_id=1, source_target_pairs={{0,1},{1,2},{2,3},{3,0},{4,5},{5,6},{6,7},{7,4},{8,9},{9,10},{10,1... | collective-permute-start | bytes 6291464 | tf_op jit(solution)/shard_map/ppermute | solution.py:780
  1000.2 50.2 %collective-permute-start.24 = (bf16[1,512,2048]{2,1,0:T(8,128)(2,1)}, bf16[1,512,2048]{2,1,0:T(8,128)(2,1)}, u32[]{:S(2)}, u32[]{:S(2)}) collective-permute-start(bf16[1,512,2048]{2,1,0:T(8,128)(2,1)} %add_convert_fusion.1), channel_id=1, source_target_pairs={{0,1},{1,2},{2,3},{3,0},{4,5},{5,6},{6,7},{7,4},{8,9},{9,10},{10,1... | collective-permute-start | bytes 6291464 | tf_op jit(solution)/shard_map/ppermute | solution.py:780
  1050.3 113.6 %reduce-scatter.18.cloned.1.call-start = ((), (), s32[]{:S(2)}) async-start(), calls=%async_computation.19 | async-start | bytes 5242880 | tf_op jit(solution)/shard_map/reduce_scatter | solution.py:795
  1051.1 129.8 %reduce-scatter.20.cloned.1.call-start = ((), (), s32[]{:S(2)}) async-start(), calls=%async_computation.20 | async-start | bytes 2621440 | tf_op jit(solution)/shard_map/reduce_scatter | solution.py:795
  1056.6 49.4 %collective-permute-start.26 = (bf16[1,512,2048]{2,1,0:T(8,128)(2,1)}, bf16[1,512,2048]{2,1,0:T(8,128)(2,1)}, u32[]{:S(2)}, u32[]{:S(2)}) collective-permute-start(bf16[1,512,2048]{2,1,0:T(8,128)(2,1)} %add_convert_fusion), channel_id=1, source_target_pairs={{0,1},{1,2},{2,3},{3,0},{4,5},{5,6},{6,7},{7,4},{8,9},{9,10},{10,1... | collective-permute-start | bytes 6291464 | tf_op jit(solution)/shard_map/ppermute | solution.py:780
  (114 other events, 2256.0 us)
Sparse Core Ops, SparseCore 0:
  11.0 41.6 all-gather.7
  55.1 54.3 all-gather.9
  111.4 36.7 all-gather.11
  165.8 41.0 all-gather.15
  209.2 67.7 all-gather.13
  278.7 43.3 all-gather.19
  324.0 67.6 all-gather.17
  670.9 37.6 reduce-scatter.9
  711.6 65.7 reduce-scatter.7
  780.3 41.7 reduce-scatter.11
  825.1 65.8 reduce-scatter.13
  1050.5 33.2 reduce-scatter.15
  1086.7 55.8 reduce-scatter.17
  1145.7 35.1 reduce-scatter.19

commit v3 on v2

v3 whole, which is shorter than its diff:
```python
import functools

import jax
import jax.numpy as jnp
from jax import lax
from jax.experimental import pallas as pl
from jax.experimental.pallas import tpu as pltpu
from jax.sharding import PartitionSpec as P

DK = 128
DV = 256
CHUNK = 128
STEP = 4
BACK_STEP = 2
NORM_EPS = 1e-06
BF = jnp.bfloat16
F32 = jnp.float32
NN = (((1,), (0,)), ((), ()))
NT = (((1,), (1,)), ((), ()))
TN = (((0,), (0,)), ((), ()))


def mm(a, b, dims=NN):
    return lax.dot_general(a.astype(BF), b.astype(BF), dims, preferred_element_type=F32)


def split(a):
    high = a.astype(BF)
    return high, (a - high.astype(F32)).astype(BF)


def mm3(a, b, dims=NN):
    ah, al = split(a)
    bh, bl = split(b)
    return mm(ah, bh, dims) + mm(ah, bl, dims) + mm(al, bh, dims)


def exact(a, b, dims=NN):
    return lax.dot_general(a, b, dims, precision=lax.Precision.HIGHEST, preferred_element_type=F32)


def iotas(n):
    return (
        lax.broadcasted_iota(jnp.int32, (n, n), 0),
        lax.broadcasted_iota(jnp.int32, (n, n), 1),
    )


def lower_inverses(lowers):
    n = lowers[0].shape[0]
    row, col = iotas(n)
    eye = (row == col).astype(F32)
    pair = (row // 2 == col // 2).astype(F32)
    inverses = [eye - low * pair for low in lowers]
    size = 2
    while size < n:
        corner = ((row // (2 * size)) == (col // (2 * size))) & ((row // size) != (col // size))
        corner = corner.astype(F32)
        half = [x.astype(BF) for x in inverses]
        inner = [mm(x, low * corner) for x, low in zip(half, lowers)]
        inverses = [x - mm(i, h) for x, i, h in zip(inverses, inner, half)]
        size = size * 2
    residual = [eye - x - mm3(low, x) for low, x in zip(lowers, inverses)]
    return [x + mm(x, r) for x, r in zip(inverses, residual)]


def sigmoid(x):
    return 1.0 / (1.0 + jnp.exp(-x))


def conv_of(buf, taps, sl, start=0):
    total = taps[0:1, sl] * buf[start + 5 : start + 5 + CHUNK, sl]
    for i in range(1, 4):
        total = total + taps[i : i + 1, sl] * buf[start + 5 + i : start + 5 + i + CHUNK, sl]
    return total


def softplus(x):
    return jnp.maximum(x, 0.0) + jnp.log1p(jnp.exp(-jnp.abs(x)))


def silu_slope(a):
    s = sigmoid(a)
    value = a * s
    return value, s + value * (1.0 - s)


def unit(a):
    r = lax.rsqrt(jnp.sum(a * a, axis=-1, keepdims=True) + NORM_EPS)
    return a * r, r


def mixer_forward_kernel(
    heads, pq, pk, pv, pg, ps, cq, ck, cv, rates, bias, gain,
    mixed, t_out, s_out, f_out, bq, bk, bv, state,
):
    step = pl.program_id(1)
    span = STEP * CHUNK

    @pl.when(step == 0)
    def _():
        state[...] = jnp.zeros_like(state)
        for b in (bq, bk, bv):
            b[0:8, :] = jnp.zeros((8, b.shape[1]), F32)

    @pl.when(step > 0)
    def _():
        for b in (bq, bk, bv):
            b[0:8, :] = b[span : span + 8, :]

    for b, p in ((bq, pq), (bk, pk), (bv, pv)):
        b[8 : span + 8, :] = p[0].astype(F32)
    row, col = iotas(CHUNK)
    hs = range(heads)
    both_at = [(j, h) for j in range(STEP) for h in hs]
    ks = [slice(h * DK, (h + 1) * DK) for h in hs]
    vs = [slice(h * DV, (h + 1) * DV) for h in hs]
    lines = [slice(j * CHUNK, (j + 1) * CHUNK) for j in range(STEP)]
    cum, cum_t, betas = [], [], []
    for j in range(STEP):
        small = ps[0, lines[j], :]
        g = rates[...] * softplus(small + bias[...])
        betas.append(sigmoid(small))
        cum.append(exact((row >= col).astype(F32), g))
        cum_t.append(cum[j].T)
    q, k, v, within, kbeta, gamma, rem, last = {}, {}, {}, {}, {}, {}, {}, {}
    for x in both_at:
        j, h = x
        a = conv_of(bq, cq, ks[h], j * CHUNK)
        q[x] = unit(a * sigmoid(a))[0]
        a = conv_of(bk, ck, ks[h], j * CHUNK)
        k[x] = unit(a * sigmoid(a))[0]
        a = conv_of(bv, cv, vs[h], j * CHUNK)
        v[x] = a * sigmoid(a)
        gc = cum[j][:, h : h + 1]
        within[x] = jnp.exp(jnp.where(row >= col, gc - cum_t[j][h : h + 1, :], -1e30))
        kbeta[x] = betas[j][:, heads + h : heads + h + 1]
        gamma[x] = jnp.exp(gc)
        tail = cum[j][CHUNK - 1 : CHUNK, h : h + 1]
        rem[x] = jnp.exp(tail - gc)
        last[x] = jnp.exp(tail)
    kb = {x: k[x].astype(BF) for x in both_at}
    lowers = [
        jnp.where(row > col, kbeta[x] * (mm(kb[x], kb[x], NT) * within[x]), 0.0) for x in both_at
    ]
    scores = {x: mm(q[x], kb[x], NT) * within[x] for x in both_at}
    inv = dict(zip(both_at, lower_inverses(lowers)))
    states = [state[h] for h in hs]
    for j in range(STEP):
        sb = [s.astype(BF) for s in states]
        both = [
            mm(jnp.concatenate([gamma[j, h] * k[j, h], gamma[j, h] * q[j, h]], axis=0), sb[h])
            for h in hs
        ]
        fb = [
            mm(inv[j, h], kbeta[j, h] * (v[j, h] - both[h][:CHUNK])).astype(BF) for h in hs
        ]
        out = [(both[h][CHUNK:] + mm(scores[j, h], fb[h])) * DK**-0.5 for h in hs]
        states = [
            last[j, h] * states[h] + mm(rem[j, h] * k[j, h], fb[h], TN) for h in hs
        ]
        for h in hs:
            t_out[0, j, h] = inv[j, h].astype(t_out.dtype)
            s_out[0, j, h] = sb[h]
            f_out[0, lines[j], vs[h]] = fb[h]
            o = out[h]
            r = lax.rsqrt(jnp.mean(o * o, axis=-1, keepdims=True) + NORM_EPS)
            p = pg[0, lines[j], vs[h]].astype(F32)
            mixed[0, lines[j], vs[h]] = (o * r * gain[...] * (p * sigmoid(p))).astype(BF)
    for h in hs:
        state[h] = states[h]


def mixer_backward_kernel(
    heads, dm, pq, pk, pv, pg, ps, tq, tk, tv, cq, ck, cv, rates, bias, gain, t_in, s_in, f_in,
    gqks, gvg, dcq, dck, dcv, dsm, dgain,
    bq, bk, bv, eq, ek, ev, dstate,
):
    row_at = pl.program_id(0)
    step = pl.program_id(1)
    chunk = pl.num_programs(1) - 1 - step
    span = BACK_STEP * CHUNK

    @pl.when((row_at == 0) & (step == 0))
    def _():
        for r in (dcq, dck, dcv, dsm, dgain):
            r[...] = jnp.zeros_like(r)

    @pl.when(step == 0)
    def _():
        dstate[...] = jnp.zeros_like(dstate)
        for b in (eq, ek, ev):
            b[span : span + 8, :] = jnp.zeros((8, b.shape[1]), F32)

    @pl.when(step > 0)
    def _():
        for b in (eq, ek, ev):
            b[span : span + 8, :] = b[0:8, :]

    has_before = (chunk > 0).astype(F32)
    for b, p, t in ((bq, pq, tq), (bk, pk, tk), (bv, pv, tv)):
        b[0:8, :] = t[0].astype(F32) * has_before
        b[8 : span + 8, :] = p[0].astype(F32)
    row, col = iotas(CHUNK)
    lane = col
    hs = range(heads)
    at = [(j, h) for j in range(BACK_STEP) for h in hs]
    ks = [slice(h * DK, (h + 1) * DK) for h in hs]
    vs = [slice(h * DV, (h + 1) * DV) for h in hs]
    lines = [slice(j * CHUNK, (j + 1) * CHUNK) for j in range(BACK_STEP)]
    scale = DK**-0.5
    small, shifted, g, betas, cum, cum_t = [], [], [], [], [], []
    for j in range(BACK_STEP):
        small.append(ps[0, lines[j], :])
        shifted.append(small[j] + bias[...])
        g.append(rates[...] * softplus(shifted[j]))
        betas.append(sigmoid(small[j]))
        cum.append(exact((row >= col).astype(F32), g[j]))
        cum_t.append(cum[j].T)
    q, k, v, rq, rk, kbeta, gamma, rem, last, within = {}, {}, {}, {}, {}, {}, {}, {}, {}, {}
    sq, sk, sv = {}, {}, {}
    for x in at:
        j, h = x
        a, sq[x] = silu_slope(conv_of(bq, cq, ks[h], j * CHUNK))
        q[x], rq[x] = unit(a)
        a, sk[x] = silu_slope(conv_of(bk, ck, ks[h], j * CHUNK))
        k[x], rk[x] = unit(a)
        v[x], sv[x] = silu_slope(conv_of(bv, cv, vs[h], j * CHUNK))
        gc = cum[j][:, h : h + 1]
        within[x] = jnp.exp(jnp.where(row >= col, gc - cum_t[j][h : h + 1, :], -1e30))
        kbeta[x] = betas[j][:, heads + h : heads + h + 1]
        gamma[x] = jnp.exp(gc)
        tail = cum[j][CHUNK - 1 : CHUNK, h : h + 1]
        rem[x] = jnp.exp(tail - gc)
        last[x] = jnp.exp(tail)
    qb = {x: q[x].astype(BF) for x in at}
    kb = {x: k[x].astype(BF) for x in at}
    sb = {x: s_in[0, x[0], x[1]] for x in at}
    fb = {x: f_in[0, lines[x[0]], vs[x[1]]] for x in at}
    tb = {x: t_in[0, x[0], x[1]] for x in at}
    gram = {x: mm(kb[x], kb[x], NT) * within[x] for x in at}
    scores = {x: mm(qb[x], kb[x], NT) * within[x] for x in at}
    gk_gq = {x: jnp.concatenate([gamma[x] * k[x], gamma[x] * q[x]], axis=0) for x in at}
    both = {x: mm(gk_gq[x], sb[x]) for x in at}
    x_in = {x: v[x] - both[x][:CHUNK] for x in at}
    out = {x: (both[x][CHUNK:] + mm(scores[x], fb[x])) * scale for x in at}
    head_dgain = jnp.zeros((1, DV), F32)
    dout = {}
    for x in at:
        j, h = x
        o = out[x]
        r = lax.rsqrt(jnp.mean(o * o, axis=-1, keepdims=True) + NORM_EPS)
        n = o * r
        p = pg[0, lines[j], vs[h]].astype(F32)
        s = sigmoid(p)
        d = dm[0, lines[j], vs[h]].astype(F32)
        y = n * gain[...]
        start = heads * DV + h * DV
        gvg[0, lines[j], start : start + DV] = (d * y * (s * (1.0 + p * (1.0 - s)))).astype(BF)
        dy = d * (p * s)
        head_dgain = head_dgain + jnp.sum(dy * n, axis=0, keepdims=True)
        dn = dy * gain[...]
        dout[x] = scale * r * (dn - n * jnp.mean(n * dn, axis=-1, keepdims=True))
    dgain[0:1, :] += head_dgain
    dob = {x: dout[x].astype(BF) for x in at}
    krem = {x: rem[x] * k[x] for x in at}
    dfresh_own = {x: mm(scores[x], dob[x], TN) for x in at}
    dscore = {x: mm(dob[x], fb[x], NT) for x in at}
    ds_next, dsb, dr, dx, dx_do = {}, {}, {}, {}, {}
    ds = [dstate[h] for h in hs]
    for j in reversed(range(BACK_STEP)):
        for h in hs:
            ds_next[j, h] = ds[h]
            dsb[j, h] = ds[h].astype(BF)
        dfresh = [dfresh_own[j, h] + mm(krem[j, h], dsb[j, h]) for h in hs]
        for h in hs:
            dr[j, h] = mm(tb[j, h], dfresh[h], TN)
        for h in hs:
            dx[j, h] = kbeta[j, h] * dr[j, h]
            dx_do[j, h] = jnp.concatenate([-dx[j, h], dout[j, h]], axis=0).astype(BF)
        ds = [last[j, h] * ds[h] + mm(gk_gq[j, h], dx_do[j, h], TN) for h in hs]
    for h in hs:
        dstate[h] = ds[h]
    dgk_gq = {x: mm(dx_do[x], sb[x], NT) for x in at}
    dkrem = {x: mm(fb[x], dsb[x], NT) for x in at}
    dlow = {x: jnp.where(row > col, -mm(dr[x], fb[x], NT), 0.0) for x in at}
    dcum = [jnp.zeros((CHUNK, CHUNK), F32) for _ in range(BACK_STEP)]
    dcum_rows = [jnp.zeros((CHUNK, CHUNK), F32) for _ in range(BACK_STEP)]
    dbeta = [jnp.zeros((CHUNK, CHUNK), F32) for _ in range(BACK_STEP)]
    for x in at:
        j, h = x
        m = dscore[x] * within[x]
        dgram = kbeta[x] * (dlow[x] * within[x])
        lg = dlow[x] * gram[x]
        e = dscore[x] * scores[x] + kbeta[x] * lg
        dq = gamma[x] * dgk_gq[x][CHUNK:] + mm(m, kb[x])
        mk = jnp.concatenate([m, dgram], axis=0)
        dk = (
            gamma[x] * dgk_gq[x][:CHUNK]
            + rem[x] * dkrem[x]
            + mm(mk, jnp.concatenate([qb[x], kb[x]], axis=0), TN)
            + mm(dgram, kb[x])
        )
        rem_part = jnp.sum(dkrem[x] * krem[x], axis=-1, keepdims=True)
        head_dcum = (
            jnp.sum(e, axis=-1, keepdims=True)
            + jnp.sum(
                dgk_gq[x][:CHUNK] * gk_gq[x][:CHUNK] + dgk_gq[x][CHUNK:] * gk_gq[x][CHUNK:],
                axis=-1, keepdims=True,
            )
            - rem_part
        )
        state_part = jnp.sum(
            jnp.sum(ds_next[x] * sb[x].astype(F32), axis=0, keepdims=True), axis=1, keepdims=True
        )
        end_part = jnp.sum(rem_part, axis=0, keepdims=True) + last[x] * state_part
        head_dcum = head_dcum + jnp.where(row[:, 0:1] == CHUNK - 1, end_part, 0.0)
        dcum[j] = dcum[j] + jnp.where(lane == h, head_dcum, 0.0)
        dcum_rows[j] = dcum_rows[j] + jnp.where(
            row == h, jnp.sum(e, axis=0, keepdims=True), 0.0
        )
        head_dbeta = jnp.sum(dr[x] * x_in[x], axis=-1, keepdims=True) + jnp.sum(
            lg, axis=-1, keepdims=True
        )
        dbeta[j] = dbeta[j] + jnp.where(lane == heads + h, head_dbeta, 0.0)
        da = rq[x] * (dq - q[x] * jnp.sum(q[x] * dq, axis=-1, keepdims=True))
        eq[lines[j], ks[h]] = da * sq[x]
        da = rk[x] * (dk - k[x] * jnp.sum(k[x] * dk, axis=-1, keepdims=True))
        ek[lines[j], ks[h]] = da * sk[x]
        ev[lines[j], vs[h]] = dx[x] * sv[x]
    for j in range(BACK_STEP):
        dg = exact((row >= col).astype(F32), dcum[j] - dcum_rows[j].T, TN)
        dshift = dg * rates[...] * sigmoid(shifted[j])
        dsm[0:1, :] += jnp.sum(dg * g[j], axis=0, keepdims=True)
        dsm[1:2, :] += jnp.sum(dshift, axis=0, keepdims=True)
        gqks[0, lines[j], 2 * heads * DK :] = (
            jnp.where(lane < heads, dshift, 0.0) + dbeta[j] * betas[j] * (1.0 - betas[j])
        ).astype(BF)
    for b, e, taps, dtaps, out_ref, start in (
        (bq, eq, cq, dcq, gqks, 0), (bk, ek, ck, dck, gqks, heads * DK), (bv, ev, cv, dcv, gvg, 0),
    ):
        for first in range(0, b.shape[1], DK):
            sl = slice(first, first + DK)
            own = e[0:span, sl]
            total = taps[3:4, sl] * own
            for i in range(3):
                total = total + taps[i : i + 1, sl] * e[3 - i : 3 - i + span, sl]
            out_ref[0, :, start + first : start + first + DK] = total.astype(BF)
            for i in range(4):
                dtaps[i : i + 1, sl] += jnp.sum(
                    own * b[5 + i : 5 + i + span, sl], axis=0, keepdims=True
                )


def whole_spec(shape):
    return pl.BlockSpec(shape, lambda r, c: (0,) * len(shape))


def lane_pad(vec, at):
    return jnp.zeros((1, 128), F32).at[0, at : at + vec.shape[0]].set(vec)


def mixer_forward(pqks, pvg, cq, ck, cv, log_rates, rate_bias, gain):
    rows, length, value_width = pvg.shape
    value_width = value_width // 2
    key_width = value_width * DK // DV
    heads = key_width // DK
    chunks = length // CHUNK
    span = STEP * CHUNK
    seq = lambda width, at=0: pl.BlockSpec((1, span, width), lambda r, c: (r, c, at))
    per = lambda a, b: pl.BlockSpec((1, STEP, heads, a, b), lambda r, c: (r, c, 0, 0, 0))
    return pl.pallas_call(
        functools.partial(mixer_forward_kernel, heads),
        grid=(rows, chunks // STEP),
        in_specs=[seq(key_width), seq(key_width, 1), seq(value_width), seq(value_width, 1),
                  seq(128, 2 * heads),
                  whole_spec((4, key_width)), whole_spec((4, key_width)), whole_spec((4, value_width)),
                  whole_spec((1, 128)), whole_spec((1, 128)), whole_spec((1, DV))],
        out_specs=[seq(value_width), per(CHUNK, CHUNK), per(DK, DV), seq(value_width)],
        out_shape=[
            jax.ShapeDtypeStruct((rows, length, value_width), BF),
            jax.ShapeDtypeStruct((rows, chunks, heads, CHUNK, CHUNK), BF),
            jax.ShapeDtypeStruct((rows, chunks, heads, DK, DV), BF),
            jax.ShapeDtypeStruct((rows, length, value_width), BF),
        ],
        scratch_shapes=[
            pltpu.VMEM((span + 8, key_width), F32),
            pltpu.VMEM((span + 8, key_width), F32),
            pltpu.VMEM((span + 8, value_width), F32),
            pltpu.VMEM((heads, DK, DV), F32),
        ],
        compiler_params=pltpu.CompilerParams(
            dimension_semantics=("arbitrary", "arbitrary"), vmem_limit_bytes=40 << 20
        ),
        cost_estimate=pl.CostEstimate(flops=0, bytes_accessed=int(rows * chunks * heads * 3007812.5), transcendentals=0),
        name="mixer_forward",
    )(pqks, pqks, pvg, pvg, pqks, cq, ck, cv, lane_pad(-jnp.exp(log_rates), 0),
      lane_pad(rate_bias, 0), gain.reshape(1, DV))


def mixer_backward(dm, pqks, pvg, cq, ck, cv, log_rates, rate_bias, gain, t_in, s_in, f_in):
    rows, length, value_width = dm.shape
    key_width = value_width * DK // DV
    heads = key_width // DK
    chunks = length // CHUNK
    span = BACK_STEP * CHUNK
    steps = chunks // BACK_STEP
    seq = lambda width, at=0: pl.BlockSpec(
        (1, span, width), lambda r, c: (r, steps - 1 - c, at)
    )
    before = lambda width, at=0: pl.BlockSpec(
        (1, 8, width),
        lambda r, c: (r, jnp.maximum((steps - 1 - c) * (span // 8) - 1, 0), at),
    )
    per = lambda a, b: pl.BlockSpec(
        (1, BACK_STEP, heads, a, b), lambda r, c: (r, steps - 1 - c, 0, 0, 0)
    )
    seq_shape = lambda width: jax.ShapeDtypeStruct((rows, length, width), BF)
    return pl.pallas_call(
        functools.partial(mixer_backward_kernel, heads),
        grid=(rows, steps),
        in_specs=[seq(value_width), seq(key_width), seq(key_width, 1), seq(value_width),
                  seq(value_width, 1), seq(128, 2 * heads),
                  before(key_width), before(key_width, 1), before(value_width),
                  whole_spec((4, key_width)), whole_spec((4, key_width)), whole_spec((4, value_width)),
                  whole_spec((1, 128)), whole_spec((1, 128)), whole_spec((1, DV)),
                  per(CHUNK, CHUNK), per(DK, DV), seq(value_width)],
        out_specs=[seq(2 * key_width + 128), seq(2 * value_width),
                   whole_spec((8, key_width)), whole_spec((8, key_width)), whole_spec((8, value_width)),
                   whole_spec((8, 128)), whole_spec((8, DV))],
        out_shape=[seq_shape(2 * key_width + 128), seq_shape(2 * value_width),
                   jax.ShapeDtypeStruct((8, key_width), F32),
                   jax.ShapeDtypeStruct((8, key_width), F32),
                   jax.ShapeDtypeStruct((8, value_width), F32),
                   jax.ShapeDtypeStruct((8, 128), F32),
                   jax.ShapeDtypeStruct((8, DV), F32)],
        scratch_shapes=[
            pltpu.VMEM((span + 8, key_width), F32),
            pltpu.VMEM((span + 8, key_width), F32),
            pltpu.VMEM((span + 8, value_width), F32),
            pltpu.VMEM((span + 8, key_width), F32),
            pltpu.VMEM((span + 8, key_width), F32),
            pltpu.VMEM((span + 8, value_width), F32),
            pltpu.VMEM((heads, DK, DV), F32),
        ],
        compiler_params=pltpu.CompilerParams(
            dimension_semantics=("arbitrary", "arbitrary"), vmem_limit_bytes=48 << 20
        ),
        cost_estimate=pl.CostEstimate(flops=0, bytes_accessed=int(rows * chunks * heads * 4921875.0), transcendentals=0),
        name="mixer_backward",
    )(dm, pqks, pqks, pvg, pvg, pqks, pqks, pqks, pvg, cq, ck, cv, lane_pad(-jnp.exp(log_rates), 0),
      lane_pad(rate_bias, 0), gain.reshape(1, DV), t_in, s_in, f_in)


FREE = pl.CostEstimate(flops=0, bytes_accessed=0, transcendentals=0)
VMEM_LIMIT = 44 << 20
WIDE_LIMIT = 58 << 20
SMALL_LIMIT = 16 << 20


def rows_kernel(count, nt, has_weigh, at, *refs):
    out = refs[-2] if has_weigh else refs[-1]
    total = None
    for i in range(count):
        part = lax.dot_general(
            refs[2 * i][0], refs[2 * i + 1][...], NT if nt else NN, preferred_element_type=F32
        )
        total = part if total is None else total + part
    if has_weigh:
        refs[-1][0, 0:1, :] = jnp.sum(
            total * refs[2 * count][0].astype(F32), axis=0, keepdims=True
        )
    out[0] = total.astype(out.dtype)


def rows_matmul(
    pairs, piece, nt=False, tile=512, take=0, weigh=None, into=None, put=0, dtype=BF, limit=WIDE_LIMIT
):
    rows = pairs[0][0].shape[0]
    width = pairs[0][1].shape[0 if nt else 1]
    tile = min(tile, width)
    at = jnp.stack([jnp.int32(take), jnp.int32(put)])
    specs, args = [], []
    for a, w in pairs:
        depth = a.shape[2]
        specs.append(pl.BlockSpec((1, piece, depth), lambda r, n, at: (r, at[0], 0)))
        if nt:
            specs.append(pl.BlockSpec((tile, depth), lambda r, n, at: (n, 0)))
        else:
            specs.append(pl.BlockSpec((depth, tile), lambda r, n, at: (0, n)))
        args.extend((a, w))
    if weigh is not None:
        specs.append(pl.BlockSpec((1, piece, tile), lambda r, n, at: (r, 0, n)))
        args.append(weigh)
    aliases = {}
    shape = (rows, piece, width)
    if into is not None:
        shape = into.shape
        dtype = into.dtype
        if not isinstance(into, jax.ShapeDtypeStruct):
            specs.append(pl.BlockSpec(memory_space=pl.ANY))
            args.append(into)
            aliases = {len(args): 0}
    out_specs = [pl.BlockSpec((1, piece, tile), lambda r, n, at: (r, at[1], n))]
    out_shape = [jax.ShapeDtypeStruct(shape, dtype)]
    if weigh is not None:
        out_specs.append(pl.BlockSpec((1, 8, tile), lambda r, n, at: (r, 0, n)))
        out_shape.append(jax.ShapeDtypeStruct((rows, 8, width), F32))
    out = pl.pallas_call(
        functools.partial(rows_kernel, len(pairs), nt, weigh is not None),
        grid_spec=pltpu.PrefetchScalarGridSpec(
            num_scalar_prefetch=1,
            grid=(rows, pl.cdiv(width, tile)),
            in_specs=specs,
            out_specs=out_specs,
        ),
        out_shape=out_shape,
        input_output_aliases=aliases,
        compiler_params=pltpu.CompilerParams(
            dimension_semantics=("arbitrary", "arbitrary"), vmem_limit_bytes=limit
        ),
        cost_estimate=FREE,
        name="rows_matmul",
    )(at, *args)
    return out[0] if weigh is None else (out[0], jnp.sum(out[1][:, 0:1], axis=0))


def outer_kernel(count, blocks, groups, parts, at, *refs):
    xs, gs = refs[:count], refs[count : 2 * count]
    extras = list(refs[2 * count : -1 - parts])
    outs, flipped = refs[-1 - parts : -1], refs[-1]
    rows, piece, width = xs[0].shape
    depth = rows * piece
    block = flipped.shape[0] // blocks

    @pl.when(pl.program_id(0) == 0)
    def _():
        for i, x in enumerate(xs):
            for k in range(blocks):
                start = pl.multiple_of((2 * k + at[0]) * block, block)
                part = x[:, :, pl.ds(start, block)].reshape(depth, block)
                flipped[k * block : (k + 1) * block, i * depth : (i + 1) * depth] = part.T

    total = None
    for i, g in enumerate(gs):
        part = lax.dot_general(
            flipped[:, i * depth : (i + 1) * depth],
            g[...].reshape(depth, g.shape[2]),
            NN,
            preferred_element_type=F32,
        )
        total = part if total is None else total + part
    for size in groups:
        held, extras = extras[:size], extras[size:]
        total = total + jnp.concatenate([x[...].astype(F32) for x in held], axis=0)
    lines = total.shape[0] // parts
    for i, out in enumerate(outs):
        out[...] = total[i * lines : (i + 1) * lines].astype(out.dtype)


def outer_sum(xs, gs, places, core, data, tile=512, adds=(), dtype=BF, parts=1):
    rows, piece, width = xs[0].shape
    columns = gs[0].shape[2]
    tile = min(tile, columns)
    at = jnp.stack([jnp.int32(core)] + [jnp.int32(x) for x in places])
    whole = pl.BlockSpec(
        (rows, piece, width), lambda n, at: (0, 0, 0), pipeline_mode=pl.Buffered(1)
    )
    specs = [whole] * len(xs)
    for i in range(len(gs)):
        specs.append(
            pl.BlockSpec((rows, piece, tile), lambda n, at, i=i: (0, at[1 + i], n))
        )
    args = [*xs, *gs]
    lines = lambda count: pl.BlockSpec((width // 2 // count, tile), lambda n, at: (0, n))
    for group in adds:
        specs.extend([lines(len(group))] * len(group))
        args.extend(group)
    return pl.pallas_call(
        functools.partial(outer_kernel, len(xs), data // 2, [len(x) for x in adds], parts),
        grid_spec=pltpu.PrefetchScalarGridSpec(
            num_scalar_prefetch=1,
            grid=(columns // tile,),
            in_specs=specs,
            out_specs=[lines(parts)] * parts,
            scratch_shapes=[pltpu.VMEM((width // 2, len(xs) * rows * piece), BF)],
        ),
        out_shape=[jax.ShapeDtypeStruct((width // 2 // parts, columns), dtype)] * parts,
        compiler_params=pltpu.CompilerParams(
            dimension_semantics=("arbitrary",), vmem_limit_bytes=VMEM_LIMIT
        ),
        cost_estimate=FREE,
        name="outer_sum",
    )(at, *args)


UNITS = 256


def lanes_of(units):
    return 128 if units % 128 == 0 else 64


def mlp_kernel(lanes, x, wgu, g, wd, hidden, grads):
    mlp_finish(lanes, lax.dot_general(x[...], wgu[...], NN, preferred_element_type=F32), g, wd, hidden, grads)


def mlp_finish(lanes, both, g, wd, hidden, grads):
    back = lax.dot_general(g[...], wd[...], NN, preferred_element_type=F32)
    for at in range(0, UNITS, lanes):
        first, second = 2 * at, 2 * at + lanes
        gate = both[:, first : first + lanes]
        up = both[:, second : second + lanes]
        own = back[:, at : at + lanes]
        sig = sigmoid(gate)
        act = gate * sig
        hidden[:, at : at + lanes] = (act * up).astype(BF)
        own_gate = own * up * (sig * (1.0 + gate * (1.0 - sig)))
        grads[:, first : first + lanes] = own_gate.astype(BF)
        grads[:, second : second + lanes] = (own * act).astype(BF)


def mlp_block(g, wd, x=None, wgu=None, both=None):
    piece, width = g.shape
    units = wd.shape[1]
    whole = pl.BlockSpec((piece, width), lambda n: (0, 0))
    part = lambda depth, size: pl.BlockSpec((depth, size), lambda n: (0, n))
    if both is None:
        kernel, args = mlp_kernel, (x, wgu, g, wd)
        specs = [whole, part(width, 2 * UNITS), whole, part(width, UNITS)]
    else:
        kernel, args = mlp_finish, (both, g, wd)
        specs = [part(piece, 2 * UNITS), whole, part(width, UNITS)]
    return pl.pallas_call(
        functools.partial(kernel, lanes_of(units)),
        grid=(pl.cdiv(units, UNITS),),
        in_specs=specs,
        out_specs=[part(piece, UNITS), part(piece, 2 * UNITS)],
        out_shape=[
            jax.ShapeDtypeStruct((piece, units), BF),
            jax.ShapeDtypeStruct((piece, 2 * units), BF),
        ],
        compiler_params=pltpu.CompilerParams(
            dimension_semantics=("arbitrary",), vmem_limit_bytes=WIDE_LIMIT
        ),
        cost_estimate=FREE,
        name="mlp_block",
    )(*args)


NORM_ROWS = 128


def row_stats(x):
    r = lax.rsqrt(jnp.mean(x * x, axis=-1, keepdims=True) + NORM_EPS)
    return x * r, r


def norm_grad(n, r, inner):
    return r * (inner - n * jnp.mean(n * inner, axis=-1, keepdims=True))


def valid_rows(at):
    start = at[0] + pl.program_id(1) * NORM_ROWS
    positions = start + lax.broadcasted_iota(jnp.int32, (NORM_ROWS, 1), 0)
    return (positions < at[1 + pl.program_id(0)]).astype(F32)


def enter_kernel(at, tokens, gain, normed):
    normed[0] = (row_stats(tokens[0].astype(F32))[0] * gain[...]).astype(BF)


def middle_kernel(at, own, moved, tokens, gain, middle, normed):
    total = own[0] + moved[0].astype(F32)
    x = tokens[0].astype(F32) + valid_rows(at) * total
    middle[0] = x
    normed[0] = (row_stats(x)[0] * gain[...]).astype(BF)


def middle_back_kernel(at, own, moved, middle, cot, gain, grad_middle, grad_attn, dgain):
    @pl.when((pl.program_id(0) == 0) & (pl.program_id(1) == 0))
    def _():
        dgain[...] = jnp.zeros_like(dgain)

    grad = own[0] + moved[0].astype(F32)
    n, r = row_stats(middle[0])
    dgain[0:1, :] += jnp.sum(grad * n, axis=0, keepdims=True)
    total = cot[0].astype(F32) + norm_grad(n, r, gain[...] * grad)
    grad_middle[0] = total
    grad_attn[0] = (valid_rows(at) * total).astype(BF)


def leave_kernel(at, own, moved, tokens, grad_middle, gain, out):
    grad = own[0] + moved[0].astype(F32)
    n, r = row_stats(tokens[0].astype(F32))
    out[0] = (grad_middle[0] + norm_grad(n, r, gain[...] * grad)).astype(BF)


def result_kernel(at, own, moved, middle, out):
    total = own[0] + moved[0].astype(F32)
    out[0] = (middle[0] + valid_rows(at) * total).astype(BF)


def by_rows(kernel, at, arrays, gain, out_types, with_sum=False):
    rows, piece, width = arrays[0].shape
    block = pl.BlockSpec((1, NORM_ROWS, width), lambda r, t, at: (r, t, 0))
    out_shape = [jax.ShapeDtypeStruct((rows, piece, width), x) for x in out_types]
    out_specs = [block] * len(out_types)
    specs = [block] * len(arrays)
    args = list(arrays)
    if gain is not None:
        specs.append(pl.BlockSpec((1, width), lambda r, t, at: (0, 0)))
        args.append(gain.reshape(1, width))
    if with_sum:
        out_shape.append(jax.ShapeDtypeStruct((8, width), F32))
        out_specs.append(pl.BlockSpec((8, width), lambda r, t, at: (0, 0)))
    return pl.pallas_call(
        kernel,
        grid_spec=pltpu.PrefetchScalarGridSpec(
            num_scalar_prefetch=1,
            grid=(rows, piece // NORM_ROWS),
            in_specs=specs,
            out_specs=out_specs,
        ),
        out_shape=out_shape,
        compiler_params=pltpu.CompilerParams(
            dimension_semantics=("arbitrary", "arbitrary"), vmem_limit_bytes=SMALL_LIMIT
        ),
        cost_estimate=FREE,
        name=kernel.__name__,
    )(at, *args)


def ring(size, group):
    return [(i, i // group * group + (i + 1) % group) for i in range(size)]


def across(size):
    return [(i, (i + size // 2) % size) for i in range(size)]


def swap(size, bit):
    return [(i, i ^ bit) for i in range(size)]


def tie(*values):
    return lax.optimization_barrier(values)


def matmul(a, b):
    return lax.dot_general(a, b, NN, preferred_element_type=F32)


def sum_over(x, axis, size):
    bit = 1
    while bit < size:
        x = x + lax.ppermute(x, axis, swap(size, bit))
        bit = bit * 2
    return x


def alternate(gate, up):
    units = gate.shape[1]
    lanes = lanes_of(units)
    parts = [x[:, at : at + lanes] for at in range(0, units, lanes) for x in (gate, up)]
    return jnp.concatenate(parts, axis=1)


def apart(both):
    units = both.shape[1] // 2
    lanes = lanes_of(units)
    parts = [both[:, at : at + lanes] for at in range(0, 2 * units, lanes)]
    return jnp.concatenate(parts[0::2], axis=1), jnp.concatenate(parts[1::2], axis=1)


def per_device(
    tokens,
    lengths,
    gain_attn,
    w_query,
    w_key,
    w_value,
    w_decay,
    w_beta,
    w_gate_out,
    conv_query,
    conv_key,
    conv_value,
    decay_log,
    decay_bias,
    gain_head,
    w_out,
    gain_mlp,
    w_gate,
    w_up,
    w_down,
    cotangent,
):
    rows, piece, width = tokens.shape
    size = lax.axis_size("head")
    data = lax.axis_size("dp")
    me = lax.axis_index("head")
    core = lax.rem(lax.axis_index("dp"), 2)
    length = piece * size
    heads = w_decay.shape[1]
    key_width, value_width = heads * DK, heads * DV
    shape3 = (rows, piece, width)
    flat_piece = rows * piece
    group = size // 2
    at = jnp.concatenate([(me * piece).astype(jnp.int32)[None], lengths])
    positions = me * piece + jnp.arange(piece, dtype=jnp.int32)
    mask = (positions[None, :] < lengths[:, None]).astype(F32)[:, :, None]

    def owner(s):
        return lax.rem(me + size - s, size)

    def step(x, group):
        return lax.ppermute(x, "head", ring(size, group))

    def opposite(x):
        return lax.ppermute(x, "head", across(size))

    def gather_weight(w):
        return lax.all_gather(w, "dp", axis=0, tiled=True)

    def cross(parts):
        return [lax.ppermute(x, "dp", swap(data, 1)) for x in parts]

    def outer_halves(xs, gs, places, tile=512, parts=2, away=(), near=()):
        away = outer_sum(xs, gs, places, 1 - core, data, tile, away, parts=parts)
        return outer_sum(xs, gs, places, core, data, tile, [cross(away), *near])[0]

    def scatter_weight(total):
        places = [[i + c for i in range(0, data, 2)] for c in range(2)]
        return lax.psum_scatter(
            total, "dp", scatter_dimension=0, tiled=True, axis_index_groups=places
        )

    normed = by_rows(enter_kernel, at, [tokens], gain_attn, [BF])[0]
    small_pad = jnp.zeros((w_decay.shape[0], 128 - 2 * heads), BF)
    w_qks = gather_weight(jnp.concatenate([w_query, w_key, w_decay, w_beta, small_pad], axis=1))
    w_vg = gather_weight(jnp.concatenate([w_value, w_gate_out], axis=1))
    wo_full = gather_weight(w_out)

    qks_buffer = jax.ShapeDtypeStruct((rows, length, 2 * key_width + 128), F32)
    vg_buffer = jax.ShapeDtypeStruct((rows, length, 2 * value_width), F32)
    def project_qks(item, s, into):
        return rows_matmul([(item, w_qks)], piece, tile=into.shape[2], into=into, put=owner(s))

    def project_vg(item, s, into):
        return rows_matmul([(item, w_vg)], piece, into=into, put=owner(s))

    pqks = project_qks(normed, 0, qks_buffer)
    pvg = vg_buffer
    pieces = [normed]
    for s in range(1, size):
        send = pieces[-1]
        if s == 1:
            send, w_gate, w_up, cotangent = tie(send, w_gate, w_up, cotangent)
        item = step(send, size)
        if s == 1:
            w_gu = alternate(w_gate, w_up)
            grad_mlp = (mask * cotangent.astype(F32)).astype(BF)
            item, w_gu, grad_mlp = tie(item, w_gu, grad_mlp)
        if s == size - 1:
            for place, early in enumerate(pieces):
                pvg = project_vg(early, place, pvg)
            item, pqks, pvg, w_gu, w_down, grad_mlp = tie(
                item, pqks, pvg, w_gu, w_down, grad_mlp
            )
        elif s > 1:
            item, pqks = tie(item, pqks)
        pqks = project_qks(item, s, pqks)
        pieces.append(item)
    normed_pieces = pieces
    w_gu_other = opposite(w_gu)
    w_down_other = opposite(w_down)
    grad_out = [grad_mlp]
    for _ in range(1, group):
        grad_out.append(step(grad_out[-1], group))
    pvg = project_vg(item, size - 1, pvg)

    cq = lax.dynamic_slice_in_dim(conv_query, me * key_width, key_width, 1)
    ck = lax.dynamic_slice_in_dim(conv_key, me * key_width, key_width, 1)
    cv = lax.dynamic_slice_in_dim(conv_value, me * value_width, value_width, 1)
    log_local = lax.dynamic_slice_in_dim(decay_log, me * heads, heads, 0)
    bias_local = lax.dynamic_slice_in_dim(decay_bias, me * heads, heads, 0)
    mixed, t_kept, s_kept, f_kept = mixer_forward(
        pqks, pvg, cq, ck, cv, log_local, bias_local, gain_head
    )
    mixed, w_gu_other, w_down_other, *grad_out = tie(mixed, w_gu_other, w_down_other, *grad_out)
    wgu_full = [gather_weight(w_gu), gather_weight(w_gu_other)]
    wdown_full = [gather_weight(w_down), gather_weight(w_down_other)]

    def attn_part(s, dtype=F32, limit=VMEM_LIMIT):
        return rows_matmul(
            [(mixed, wo_full)], piece, nt=True, take=owner(s), dtype=dtype, limit=limit
        )

    total = attn_part(1, BF, WIDE_LIMIT)
    for s in range(2, size + 1):
        moved = step(total, size)
        own = attn_part(s % size)
        moved, own = tie(moved, own)
        total = (own + moved.astype(F32)).astype(BF)
    middle, normed_two = by_rows(middle_kernel, at, [own, moved, tokens], gain_mlp, [F32, BF])
    flat2 = lambda x: x.reshape(flat_piece, width)
    second = [normed_two]
    hidden, grad_gu = [[], []], [[], []]

    def keep_block(b, block):
        hidden[b].append(block[0].reshape(rows, piece, -1))
        grad_gu[b].append(block[1].reshape(rows, piece, -1))

    def mlp_part(s, dtype=F32):
        pairs = [(hidden[b][s], wdown_full[b]) for b in range(2)]
        return rows_matmul(pairs, piece, nt=True, dtype=dtype)

    def two_part(s, dtype=F32):
        pairs = [(grad_gu[b][s], wgu_full[b]) for b in range(2)]
        return rows_matmul(pairs, piece, nt=True, dtype=dtype)

    send, own_x, own_g = tie(normed_two, normed_two, grad_out[0])
    for s in range(1, group):
        moved = step(send, group)
        if s == 1:
            for b in range(2):
                keep_block(b, mlp_block(flat2(own_g), wdown_full[b], flat2(own_x), wgu_full[b]))
            own_two = two_part(0)
            moved, own_two, *held = tie(moved, own_two, *hidden[0], *hidden[1], *grad_gu[0], *grad_gu[1])
            hidden, grad_gu = [held[:1], held[1:2]], [held[2:3], held[3:]]
        second.append(moved)
        send = moved
    for s in range(1, group):
        for b in range(2):
            keep_block(
                b, mlp_block(flat2(grad_out[s]), wdown_full[b], flat2(second[s]), wgu_full[b])
            )
    first = [0] * group
    units = hidden[0][0].shape[2]

    def away_pair(b):
        return (
            outer_sum(second, grad_gu[b], first, 1 - core, data, 1408),
            outer_sum(grad_out, hidden[b], first, 1 - core, data, units),
        )

    def near_pair(b, parts):
        return (
            outer_sum(second, grad_gu[b], first, core, data, 1408, [cross(parts[:1])])[0],
            outer_sum(grad_out, hidden[b], first, core, data, units, [cross(parts[1:])])[0],
        )

    total = two_part(1, BF)
    total, *held = tie(total, *hidden[0], *hidden[1], *grad_gu[1])
    hidden, grad_gu[1] = [held[:group], held[group : 2 * group]], held[2 * group :]
    for s in range(2, group + 1):
        moved = step(total, group)
        if s == group:
            own = own_two
            own_mlp, send_mlp = mlp_part(0), mlp_part(1, BF)
            away_gu, away_down = away_pair(1)
            moved, own_mlp, send_mlp, *away = tie(
                moved, own_mlp, send_mlp, *away_gu, *away_down
            )
        else:
            own = two_part(s)
            total = (own + moved.astype(F32)).astype(BF)
    grad_middle, grad_attn, dgain_mlp = by_rows(
        middle_back_kernel, at, [own, moved, middle, cotangent], gain_mlp, [F32, BF], True
    )

    pair_gu, pair_down = [None, None], [None, None]
    mixed_buffer = jax.ShapeDtypeStruct((rows, length, value_width), F32)
    grad_mixed = mixed_buffer
    attn_pieces = [grad_attn]
    for s in range(1, size):
        send = attn_pieces[-1]
        if s == 1:
            send, *held = tie(send, *away, *hidden[0], *grad_gu[0])
            away, hidden[0], grad_gu[0] = held[:2], held[2 : 2 + group], held[2 + group :]
        elif s == 2:
            send, *away = tie(send, *away)
        item = step(send, size)
        if s == 1:
            pair_gu[1], pair_down[1] = near_pair(1, away)
            away_gu, away_down = away_pair(0)
            item, pair_gu[1], pair_down[1], *away = tie(
                item, pair_gu[1], pair_down[1], *away_gu, *away_down
            )
        elif s == 2:
            pair_gu[0], pair_down[0] = near_pair(0, away)
            item, pair_gu[0], pair_down[0] = tie(item, pair_gu[0], pair_down[0])
        if s == size - 1:
            for place, early in enumerate(attn_pieces):
                grad_mixed = rows_matmul(
                    [(early, wo_full)], piece, into=grad_mixed, put=owner(place)
                )
            wout_parts = [
                outer_sum(
                    attn_pieces, [mixed] * s, [owner(x) for x in range(s)], side, data, dtype=F32
                )[0]
                for side in (1 - core, core)
            ]
            item, grad_mixed, *wout_parts = tie(item, grad_mixed, *wout_parts)
        attn_pieces.append(item)
    grad_mixed = rows_matmul([(item, wo_full)], piece, into=grad_mixed, put=owner(size - 1))
    sums_gu = [None, scatter_weight(pair_gu[1])]
    sums_down = [None, scatter_weight(pair_down[1])]
    sums_gu[0] = scatter_weight(pair_gu[0])
    sums_down[0] = scatter_weight(pair_down[0])

    grad_mixed, send_mlp, send_gu, send_down = tie(grad_mixed, send_mlp, sums_gu[1], sums_down[1])
    moved = step(send_mlp, group)
    moved_gu, moved_down = opposite(send_gu), opposite(send_down)
    done = mixer_backward(
        grad_mixed, pqks, pvg, cq, ck, cv, log_local, bias_local, gain_head, t_kept, s_kept, f_kept
    )
    moved, moved_gu, moved_down, gqks, gvg, dcq, dck, dcv, dsm, dgain = tie(
        moved, moved_gu, moved_down, *done
    )
    for s in range(2, group):
        moved = step((mlp_part(s) + moved.astype(F32)).astype(BF), group)
    moved_mlp = moved

    def one_part(s, dtype=F32):
        return rows_matmul(
            [(gqks, w_qks), (gvg, w_vg)], piece, nt=True, take=owner(s),
            weigh=normed_pieces[s], dtype=dtype,
        )

    places = [owner(s) for s in range(size)]
    total, gain_sum = one_part(1, BF)
    for s in range(2, size + 1):
        if s == 3:
            total, attn_last, *last = tie(total, attn_pieces[-1], sums_down[0], sums_gu[0])
            sums_down[0], sums_gu[0] = last
        total, gqks, gvg = tie(total, gqks, gvg)
        if s == size:
            total, moved_mlp, *small = tie(
                total, moved_mlp, dcq, dck, dcv, dsm, dgain, dgain_mlp
            )
        moved = step(total, size)
        if s < size:
            own, gain_part = one_part(s)
            gain_sum = gain_sum + gain_part
        if s == 2:
            pair_vg = outer_halves(normed_pieces, [gvg] * size, places, 512, 4)
            moved, own, pair_vg = tie(moved, own, pair_vg)
        elif s == 3:
            pair_qks = outer_halves(normed_pieces, [gqks] * size, places, gqks.shape[2])
            pair_wout = outer_halves(
                [attn_last], [mixed], places[-1:], 512, 2, [wout_parts[:1]], [wout_parts[1:]]
            )
            moved, own, pair_qks, pair_wout, out_vg = tie(
                moved, own, pair_qks, pair_wout, scatter_weight(pair_vg)
            )
        if s < size:
            total = (own + moved.astype(F32)).astype(BF)
            continue
        own, gain_part = one_part(0)
        small = jnp.concatenate(
            [x[:4] for x in small] + [jnp.broadcast_to(gain_sum + gain_part, (4, width))],
            axis=1,
        )
        small = sum_over(small, "dp", data)
        out_wgate, out_wup = apart(sums_gu[0].astype(F32) + moved_gu.astype(F32))
        out_wdown = sums_down[0].astype(F32) + moved_down.astype(F32)
        mixed_rows = by_rows(result_kernel, at, [own_mlp, moved_mlp, middle], None, [BF])[0]
        moved, own, small, out_wgate, out_wup, out_wdown, mixed_rows = tie(
            moved, own, small, out_wgate, out_wup, out_wdown, mixed_rows
        )
    tokens_grad = by_rows(
        leave_kernel, at, [own, moved, tokens, grad_middle], gain_attn, [BF]
    )[0]
    out_vg = out_vg.astype(F32)
    out_wout = scatter_weight(pair_wout).astype(F32)
    out_qks = scatter_weight(pair_qks).astype(F32)

    taps_width = 2 * key_width + value_width
    own_width = taps_width + 128
    spread = lax.dynamic_update_slice_in_dim(
        jnp.zeros((4, size * own_width), F32), small[:, :own_width], me * own_width, 1
    )
    small = sum_over(jnp.concatenate([spread, small[:, own_width:]], axis=1), "head", size)
    by_head = [small[:, i * own_width : (i + 1) * own_width] for i in range(size)]
    taps = lambda start, stop: jnp.concatenate([x[:, start:stop] for x in by_head], axis=1)
    conv_sums = (
        taps(0, key_width),
        taps(key_width, 2 * key_width),
        taps(2 * key_width, taps_width),
    )
    decay_sums = [
        jnp.concatenate([x[i, taps_width : taps_width + heads] for x in by_head]) for i in range(2)
    ]
    gains = small[0, size * own_width :]
    gain_head_out = gains[:DV]
    gain_mlp_out = gains[DV : DV + width]
    gain_attn_out = gains[DV + width :] / gain_attn
    return (
        mixed_rows,
        tokens_grad,
        gain_attn_out,
        out_qks[:, :key_width],
        out_qks[:, key_width : 2 * key_width],
        out_vg[:, :value_width],
        out_qks[:, 2 * key_width : 2 * key_width + heads],
        out_qks[:, 2 * key_width + heads : 2 * key_width + 2 * heads],
        out_vg[:, value_width:],
        conv_sums[0],
        conv_sums[1],
        conv_sums[2],
        decay_sums[0],
        decay_sums[1],
        gain_head_out,
        out_wout,
        gain_mlp_out,
        out_wgate,
        out_wup,
        out_wdown,
    )

def solution(mesh):
    rows = P("dp", "head", None)
    weight = P("dp", "head")
    same = P()
    return jax.shard_map(
        per_device,
        mesh=mesh,
        in_specs=(
            rows, P("dp"), same, weight, weight, weight, weight, weight, weight, same, same, same,
            same, same, same, weight, same, weight, weight, weight, rows,
        ),
        out_specs=(
            rows, rows, same, weight, weight, weight, weight, weight, weight, same, same, same,
            same, same, same, weight, same, weight, weight, weight,
        ),
        check_vma=False,
    )
```

time: 1200 us -> 1080 us (0.900)
  waiting for transfers between devices: 368 us -> 282 us
  matrix products: 26.6 us -> 0 us
  local copies, waits for them, and re-layouts: 120 us -> 106 us
    ppermute x16, waiting for transfers between devices: 334 us -> 221 us  [step(): return lax.ppermute(x, 'head', ring(size, group))]
    pallas_call x24, Pallas kernels: 210 us -> 241 us  [rows_matmul(): pl.pallas_call(functools.partial(rows_kernel, len(pairs), nt, weigh is no...]
    dot_general x2 -> x0, matrix products: 26.6 us -> none  [matmul(): return lax.dot_general(a, b, NN, preferred_element_type=F32)]
    ppermute x4, waiting for transfers between devices: 0.01 us -> 26.3 us  [opposite(): return lax.ppermute(x, 'head', across(size))]
    pallas_call x1, Pallas kernels: 64 us -> 45.7 us  [mixer_forward(): pl.pallas_call(functools.partial(mixer_forward_kernel, heads), grid=(rows...]
    unnamed x209 -> x217, local copies, waits for them, and re-layouts: 78.8 us -> 95.3 us
    pallas_call x4, Pallas kernels: 47.8 us -> 63.7 us  [mlp_block(): pl.pallas_call(functools.partial(kernel, lanes_of(units)), grid=(pl.cdiv(...]
  transfers between devices with their start and end apart: 46 -> 51, of which waited for: 19 -> 17; matrix products, arithmetic and copies ran while one was open for 8% -> 6% of each run, Pallas kernels for 46% -> 52%
where the time goes in v3:
time: 1080 us; the launch traced here: 1070 us
  Pallas kernels  617 us (57%)
  waiting for transfers between devices  282 us (26%)
  local copies, waits for them, and re-layouts  106 us (10%)
  other arithmetic  32.1 us (3%)
  starting transfers between devices  21.9 us (2%)
  between operations  15.7 us (1%)
    pallas_call x24, Pallas kernels, rows_matmul(): pl.pallas_call(functools.partial(rows_kernel, len(pairs), nt, weigh is no...  241 us
    ppermute x16, waiting for transfers between devices, step(): return lax.ppermute(x, 'head', ring(size, group))  221 us
    pallas_call x16, Pallas kernels, outer_sum(): pl.pallas_call(functools.partial(outer_kernel, len(xs), data // 2, [len(x...  162 us
    unnamed x217, local copies, waits for them, and re-layouts  95.3 us
    pallas_call x1, Pallas kernels, mixer_backward(): pl.pallas_call(functools.partial(mixer_backward_kernel, heads), grid=(row...  86 us
    pallas_call x4, Pallas kernels, mlp_block(): pl.pallas_call(functools.partial(kernel, lanes_of(units)), grid=(pl.cdiv(...  63.7 us
    pallas_call x1, Pallas kernels, mixer_forward(): pl.pallas_call(functools.partial(mixer_forward_kernel, heads), grid=(rows...  45.7 us
    ppermute x4, waiting for transfers between devices, opposite(): return lax.ppermute(x, 'head', across(size))  26.3 us
  transfers between devices with their start and end apart: 51, of which 17 were waited for; matrix products, arithmetic and copies ran while one was open for 6% of the time, Pallas kernels for 52%

profile of v3, /device:TPU:0, one launch (start us, length us, event | category | flops | bytes accessed | tf_op | source)
XLA Modules:
  0.0 1075.0 jit_solution(292505121448724047)
XLA Ops:
  41.2 26.1 %collective-permute-done.refs_0_.refs_4_.refs_1_ = bf16[1,512,2048]{2,1,0:T(8,128)(2,1)} collective-permute-done((bf16[1,512,2048]{2,1,0:T(8,128)(2,1)S(1)}, bf16[1,512,2048]{2,1,0:T(8,128)(2,1)}, u32[]{:S(2)}, u32[]{:S(2)}) %collective-permute-start) | collective-permute-done | bytes 2097184 | tf_op jit(solution)/shard_map/ppermute | solution.py:818
  84.4 31.8 %collective-permute-done.1.refs_0_.refs_4_.refs_2_ = bf16[1,512,2048]{2,1,0:T(8,128)(2,1)S(1)} collective-permute-done((bf16[1,512,2048]{2,1,0:T(8,128)(2,1)}, bf16[1,512,2048]{2,1,0:T(8,128)(2,1)S(1)}, u32[]{:S(2)}, u32[]{:S(2)}) %collective-permute-start.1) | collective-permute-done | bytes 2097184 | tf_op jit(solution)/shard_map/ppermute | solution.py:818
  189.2 45.7 %mixer_forward.1 = (bf16[1,2048,1024]{2,1,0:T(8,128)(2,1)S(1)}, bf16[1,16,4,128,128]{4,3,2,1,0:T(8,128)(2,1)S(1)}, bf16[1,16,4,128,256]{4,3,2,1,0:T(8,128)(2,1)S(1)}, bf16[1,2048,1024]{2,1,0:T(8,128)(2,1)}) custom-call(f32[1,2048,1152]{2,1,0:T(8,128)} %rows_matmul.30.pq.pk.ps.tq.tk, f32[1,2048,1152]{2,1,0:T(8,128)} %rows_matmul.30.pq.pk.ps.tq.tk, ...), custom_call_target="tpu_custom_call" | custom-call | bytes 192500000 | tf_op jit(solution)/shard_map/mixer_forward/pallas_call | solution.py:372
  240.3 19.3 %collective-permute-done.4 = bf16[256,1408]{1,0:T(8,128)(2,1)} collective-permute-done((bf16[256,1408]{1,0:T(8,128)(2,1)S(1)}, bf16[256,1408]{1,0:T(8,128)(2,1)}, u32[]{:S(2)}, u32[]{:S(2)}) %collective-permute-start.4) | collective-permute-done | bytes 720928 | tf_op jit(solution)/shard_map/ppermute | solution.py:821
  274.1 40.0 %collective-permute-done.6 = bf16[1,512,2048]{2,1,0:T(8,128)(2,1)S(1)} collective-permute-done((bf16[1,512,2048]{2,1,0:T(8,128)(2,1)}, bf16[1,512,2048]{2,1,0:T(8,128)(2,1)S(1)}, u32[]{:S(2)}, u32[]{:S(2)}) %collective-permute-start.6) | collective-permute-done | bytes 2097184 | tf_op jit(solution)/shard_map/ppermute | solution.py:818
  320.5 39.4 %collective-permute-done.7 = bf16[1,512,2048]{2,1,0:T(8,128)(2,1)S(1)} collective-permute-done((bf16[1,512,2048]{2,1,0:T(8,128)(2,1)S(1)}, bf16[1,512,2048]{2,1,0:T(8,128)(2,1)S(1)}, u32[]{:S(2)}, u32[]{:S(2)}) %collective-permute-start.7) | collective-permute-done | bytes 2097184 | tf_op jit(solution)/shard_map/ppermute | solution.py:818
  366.4 39.5 %collective-permute-done.8.moved = bf16[1,512,2048]{2,1,0:T(8,128)(2,1)S(1)} collective-permute-done((bf16[1,512,2048]{2,1,0:T(8,128)(2,1)S(1)}, bf16[1,512,2048]{2,1,0:T(8,128)(2,1)S(1)}, u32[]{:S(2)}, u32[]{:S(2)}) %collective-permute-start.8) | collective-permute-done | bytes 2097184 | tf_op jit(solution)/shard_map/ppermute | solution.py:818
  411.9 15.9 %mlp_block.4 = (bf16[512,1408]{1,0:T(8,128)(2,1)}, bf16[512,2816]{1,0:T(8,128)(2,1)}) custom-call(bf16[512,2048]{1,0:T(8,128)(2,1)} %bitcast.50, bf16[2048,2816]{1,0:T(8,128)(2,1)} %all-gather.14.cloned.1.call-done.wgu.refs_1_, bf16[512,2048]{1,0:T(8,128)(2,1)} %bitcast.48, bf16[2048,1408]{1,0:T(8,128)(2,1)} %all-gather.16.cloned.1.call-done.wd.refs_1_), custom_call_target="tpu_custom_call" | custom-call | tf_op jit(solution)/shard_map/mlp_block/pallas_call | solution.py:634
  427.8 16.0 %mlp_block.5 = (bf16[512,1408]{1,0:T(8,128)(2,1)}, bf16[512,2816]{1,0:T(8,128)(2,1)}) custom-call(bf16[512,2048]{1,0:T(8,128)(2,1)} %bitcast.51, bf16[2048,2816]{1,0:T(8,128)(2,1)} %all-gather.18.cloned.1.call-done.wgu.refs_3_, bf16[512,2048]{1,0:T(8,128)(2,1)} %bitcast.49, bf16[2048,1408]{1,0:T(8,128)(2,1)} %all-gather.20.cloned.1.call-done.wd.refs_3_), custom_call_target="tpu_custom_call" | custom-call | tf_op jit(solution)/shard_map/mlp_block/pallas_call | solution.py:634
  444.2 18.9 %rows_matmul.36.own = f32[1,512,2048]{2,1,0:T(8,128)} custom-call(s32[2]{0:T(128)} %broadcast.93.at, bf16[1,512,2816]{2,1,0:T(8,128)(2,1)} %bitcast.52, bf16[2048,2816]{1,0:T(8,128)(2,1)} %all-gather.14.cloned.1.call-done.wgu.refs_1_, bf16[1,512,2816]{2,1,0:T(8,128)(2,1)} %bitcast.58, bf16[2048,2816]{1,0:T(8,128)(2,1)} %all-gather.18.cloned.1.call-done.wgu.refs_3_), custom_call_target="tpu_custom_call" | custom-call | tf_op jit(solution)/shard_map/rows_matmul/pallas_call | solution.py:509
  463.1 15.9 %mlp_block.7 = (bf16[512,1408]{1,0:T(8,128)(2,1)}, bf16[512,2816]{1,0:T(8,128)(2,1)}) custom-call(bf16[512,2048]{1,0:T(8,128)(2,1)} %bitcast.17.x, bf16[2048,2816]{1,0:T(8,128)(2,1)} %all-gather.18.cloned.1.call-done.wgu.refs_3_, bf16[512,2048]{1,0:T(8,128)(2,1)} %bitcast.18.g, bf16[2048,1408]{1,0:T(8,128)(2,1)} %all-gather.20.cloned.1.call-done.wd.refs_3_), custom_call_target="tpu_custom_call" | custom-call | tf_op jit(solution)/shard_map/mlp_block/pallas_call | solution.py:634
  479.0 15.9 %mlp_block.6 = (bf16[512,1408]{1,0:T(8,128)(2,1)}, bf16[512,2816]{1,0:T(8,128)(2,1)}) custom-call(bf16[512,2048]{1,0:T(8,128)(2,1)} %bitcast.17.x, bf16[2048,2816]{1,0:T(8,128)(2,1)} %all-gather.14.cloned.1.call-done.wgu.refs_1_, bf16[512,2048]{1,0:T(8,128)(2,1)} %bitcast.18.g, bf16[2048,1408]{1,0:T(8,128)(2,1)} %all-gather.16.cloned.1.call-done.wd.refs_1_), custom_call_target="tpu_custom_call" | custom-call | tf_op jit(solution)/shard_map/mlp_block/pallas_call | solution.py:634
  494.9 19.2 %rows_matmul.37 = bf16[1,512,2048]{2,1,0:T(8,128)(2,1)} custom-call(s32[2]{0:T(128)} %broadcast.93.at, bf16[1,512,2816]{2,1,0:T(8,128)(2,1)} %bitcast.55, bf16[2048,2816]{1,0:T(8,128)(2,1)} %all-gather.14.cloned.1.call-done.wgu.refs_1_, bf16[1,512,2816]{2,1,0:T(8,128)(2,1)} %bitcast.61, bf16[2048,2816]{1,0:T(8,128)(2,1)} %all-gather.18.cloned.1.call-done.wgu.refs_3_), custom_call_target="tpu_custom_call" | custom-call | tf_op jit(solution)/shard_map/rows_matmul/pallas_call | solution.py:509
  525.6 11.5 %outer_sum.16 = bf16[1024,2816]{1,0:T(8,128)(2,1)} custom-call(s32[3]{0:T(128)S(1)} %stack.57.at, bf16[1,512,2048]{2,1,0:T(8,128)(2,1)S(1)} %copy-done.13, bf16[1,512,2048]{2,1,0:T(8,128)(2,1)} %collective-permute-done.9.refs_1_, bf16[1,512,2816]{2,1,0:T(8,128)(2,1)S(1)} %bitcast.59, bf16[1,512,2816]{2,1,0:T(8,128)(2,1)S(1)} %bitcast.62), custom_call_target="tpu_custom_call" | custom-call | tf_op jit(solution)/shard_map/outer_sum/pallas_call | solution.py:579
  537.1 11.8 %rows_matmul.39 = bf16[1,512,2048]{2,1,0:T(8,128)(2,1)} custom-call(s32[2]{0:T(128)} %broadcast.93.at, bf16[1,512,1408]{2,1,0:T(8,128)(2,1)} %bitcast.64, bf16[2048,1408]{1,0:T(8,128)(2,1)} %all-gather.16.cloned.1.call-done.wd.refs_1_, bf16[1,512,1408]{2,1,0:T(8,128)(2,1)} %bitcast.67, bf16[2048,1408]{1,0:T(8,128)(2,1)} %all-gather.20.cloned.1.call-done.wd.refs_3_), custom_call_target="tpu_custom_call" | custom-call | tf_op jit(solution)/shard_map/rows_matmul/pallas_call | solution.py:509
  548.8 12.2 %rows_matmul.38.own = f32[1,512,2048]{2,1,0:T(8,128)} custom-call(s32[2]{0:T(128)} %broadcast.93.at, bf16[1,512,1408]{2,1,0:T(8,128)(2,1)} %bitcast.70, bf16[2048,1408]{1,0:T(8,128)(2,1)} %all-gather.16.cloned.1.call-done.wd.refs_1_, bf16[1,512,1408]{2,1,0:T(8,128)(2,1)} %bitcast.73, bf16[2048,1408]{1,0:T(8,128)(2,1)} %all-gather.20.cloned.1.call-done.wd.refs_3_), custom_call_target="tpu_custom_call" | custom-call | tf_op jit(solution)/shard_map/rows_matmul/pallas_call | solution.py:509
  587.1 11.9 %outer_sum.20 = bf16[1024,2816]{1,0:T(8,128)(2,1)} custom-call(s32[3]{0:T(128)S(1)} %stack.57.at, bf16[1,512,2048]{2,1,0:T(8,128)(2,1)S(1)} %copy-done.13, bf16[1,512,2048]{2,1,0:T(8,128)(2,1)} %collective-permute-done.9.refs_1_, bf16[1,512,2816]{2,1,0:T(8,128)(2,1)S(1)} %bitcast.53, bf16[1,512,2816]{2,1,0:T(8,128)(2,1)S(1)} %bitcast.56), custom_call_target="tpu_custom_call" | custom-call | tf_op jit(solution)/shard_map/outer_sum/pallas_call | solution.py:579
  612.3 12.4 %outer_sum.18 = bf16[1024,2816]{1,0:T(8,128)(2,1)} custom-call(s32[3]{0:T(128)S(1)} %stack.59.at, bf16[1,512,2048]{2,1,0:T(8,128)(2,1)S(1)} %copy-done.14, bf16[1,512,2048]{2,1,0:T(8,128)(2,1)} %collective-permute-done.9.refs_1_, bf16[1,512,2816]{2,1,0:T(8,128)(2,1)S(1)} %bitcast.60, bf16[1,512,2816]{2,1,0:T(8,128)(2,1)S(1)} %bitcast.63, ...), custom_call_target="tpu_custom_call" | custom-call | tf_op jit(solution)/shard_map/outer_sum/pallas_call | solution.py:579
  627.5 12.7 %collective-permute-done.16.refs_4_ = bf16[1024,1408]{1,0:T(8,128)(2,1)S(1)} collective-permute-done((bf16[1024,1408]{1,0:T(8,128)(2,1)}, bf16[1024,1408]{1,0:T(8,128)(2,1)S(1)}, u32[]{:S(2)}, u32[]{:S(2)}) %collective-permute-start.16) | collective-permute-done | bytes 2883616 | tf_op jit(solution)/shard_map/ppermute | solution.py:827
  657.0 12.6 %outer_sum.22 = bf16[1024,2816]{1,0:T(8,128)(2,1)} custom-call(s32[3]{0:T(128)S(1)} %stack.59.at, bf16[1,512,2048]{2,1,0:T(8,128)(2,1)S(1)} %copy-done.15, bf16[1,512,2048]{2,1,0:T(8,128)(2,1)} %collective-permute-done.9.refs_1_, bf16[1,512,2816]{2,1,0:T(8,128)(2,1)S(1)} %bitcast.54, bf16[1,512,2816]{2,1,0:T(8,128)(2,1)S(1)} %bitcast.57, ...), custom_call_target="tpu_custom_call" | custom-call | tf_op jit(solution)/shard_map/outer_sum/pallas_call | solution.py:579
  691.4 10.3 outer_sum.25.refs_4_
  738.2 86.0 %mixer_backward.1 = (bf16[1,2048,1152]{2,1,0:T(8,128)(2,1)}, bf16[1,2048,2048]{2,1,0:T(8,128)(2,1)}, f32[8,512]{1,0:T(8,128)S(1)}, f32[8,512]{1,0:T(8,128)S(1)},...) custom-call(f32[1,2048,1024]{2,1,0:T(8,128)} %rows_matmul.43.dm, ...), custom_call_target="tpu_custom_call" | custom-call | bytes 315000000 | tf_op jit(solution)/shard_map/mixer_backward/pallas_call | solution.py:419
  833.1 13.8 %rows_matmul.44 = (bf16[1,512,2048]{2,1,0:T(8,128)(2,1)}, f32[1,8,2048]{2,1,0:T(8,128)}) custom-call(s32[2]{0:T(128)} %pad_add_fusion.3.at, bf16[1,2048,1152]{2,1,0:T(8,128)(2,1)} %get-tuple-element.348.refs_0_.refs_4_.refs_5_.refs_6_.refs_7_, bf16[2048,1152]{1,0:T(8,128)(2,1)} %all-gather.8.cloned.1.call-done.refs_1_, ...), custom_call_target="tpu_custom_call" | custom-call | tf_op jit(solution)/shard_map/rows_matmul/pallas_call | solution.py:509
  847.1 16.0 %outer_sum.26 = (bf16[256,2048]{1,0:T(8,128)(2,1)}, bf16[256,2048]{1,0:T(8,128)(2,1)}, bf16[256,2048]{1,0:T(8,128)(2,1)}, bf16[256,2048]{1,0:T(8,128)(2,1)}) custom-call(s32[5]{0:T(128)S(1)} %stack.63.at, bf16[1,512,2048]{2,1,0:T(8,128)(2,1)S(1)} %copy-done.6, bf16[1,512,2048]{2,1,0:T(8,128)(2,1)} %collective-permute-done.refs_0_.refs_4_.refs_1_, ...), custom_call_target="tpu_custom_call" | custom-call | tf_op jit(solution)/shard_map/outer_sum/pallas_call | solution.py:579
  864.2 13.8 %rows_matmul.45 = (f32[1,512,2048]{2,1,0:T(8,128)}, f32[1,8,2048]{2,1,0:T(8,128)}) custom-call(s32[2]{0:T(128)} %copy-done.68, bf16[1,2048,1152]{2,1,0:T(8,128)(2,1)} %get-tuple-element.348.refs_0_.refs_4_.refs_5_.refs_6_.refs_7_, bf16[2048,1152]{1,0:T(8,128)(2,1)} %all-gather.8.cloned.1.call-done.refs_1_, ...), custom_call_target="tpu_custom_call" | custom-call | tf_op jit(solution)/shard_map/rows_matmul/pallas_call | solution.py:509
  878.1 16.2 %outer_sum.27 = bf16[1024,2048]{1,0:T(8,128)(2,1)} custom-call(s32[5]{0:T(128)S(1)} %stack.62.at, bf16[1,512,2048]{2,1,0:T(8,128)(2,1)S(1)} %copy-done.6, bf16[1,512,2048]{2,1,0:T(8,128)(2,1)} %collective-permute-done.refs_0_.refs_4_.refs_1_, bf16[1,512,2048]{2,1,0:T(8,128)(2,1)} %copy-done.7, ...), custom_call_target="tpu_custom_call" | custom-call | tf_op jit(solution)/shard_map/outer_sum/pallas_call | solution.py:579
  910.2 11.3 %outer_sum.28 = (bf16[512,1152]{1,0:T(8,128)(2,1)}, bf16[512,1152]{1,0:T(8,128)(2,1)}) custom-call(s32[5]{0:T(128)S(1)} %stack.63.at, bf16[1,512,2048]{2,1,0:T(8,128)(2,1)S(1)} %copy-done.6, bf16[1,512,2048]{2,1,0:T(8,128)(2,1)} %collective-permute-done.refs_0_.refs_4_.refs_1_, bf16[1,512,2048]{2,1,0:T(8,128)(2,1)S(1)} %copy-done.8, ...), custom_call_target="tpu_custom_call" | custom-call | tf_op jit(solution)/shard_map/outer_sum/pallas_call | solution.py:579
  934.2 14.1 %rows_matmul.46 = (f32[1,512,2048]{2,1,0:T(8,128)}, f32[1,8,2048]{2,1,0:T(8,128)}) custom-call(s32[2]{0:T(128)} %copy-done.67, bf16[1,2048,1152]{2,1,0:T(8,128)(2,1)} %get-tuple-element.348.refs_0_.refs_4_.refs_5_.refs_6_.refs_7_, bf16[2048,1152]{1,0:T(8,128)(2,1)} %all-gather.8.cloned.1.call-done.refs_1_, ...), custom_call_target="tpu_custom_call" | custom-call | tf_op jit(solution)/shard_map/rows_matmul/pallas_call | solution.py:509
  961.0 11.6 %outer_sum.29 = bf16[1024,1152]{1,0:T(8,128)(2,1)} custom-call(s32[5]{0:T(128)S(1)} %stack.62.at, bf16[1,512,2048]{2,1,0:T(8,128)(2,1)S(1)} %copy-done.6, bf16[1,512,2048]{2,1,0:T(8,128)(2,1)} %collective-permute-done.refs_0_.refs_4_.refs_1_, bf16[1,512,2048]{2,1,0:T(8,128)(2,1)S(1)} %copy-done.9, ...), custom_call_target="tpu_custom_call" | custom-call | tf_op jit(solution)/shard_map/outer_sum/pallas_call | solution.py:579
  979.7 14.5 %rows_matmul.47 = (f32[1,512,2048]{2,1,0:T(8,128)}, f32[1,8,2048]{2,1,0:T(8,128)}) custom-call(s32[2]{0:T(128)} %copy-done.66, bf16[1,2048,1152]{2,1,0:T(8,128)(2,1)} %get-tuple-element.348.refs_0_.refs_4_.refs_5_.refs_6_.refs_7_, bf16[2048,1152]{1,0:T(8,128)(2,1)} %all-gather.8.cloned.1.call-done.refs_1_, ...), custom_call_target="tpu_custom_call" | custom-call | tf_op jit(solution)/shard_map/rows_matmul/pallas_call | solution.py:509
  1010.6 16.9 %collective-permute-done.31.moved = bf16[1,512,2048]{2,1,0:T(8,128)(2,1)} collective-permute-done((bf16[1,512,2048]{2,1,0:T(8,128)(2,1)}, bf16[1,512,2048]{2,1,0:T(8,128)(2,1)}, u32[]{:S(2)}, u32[]{:S(2)}) %collective-permute-start.31) | collective-permute-done | bytes 2097184 | tf_op jit(solution)/shard_map/ppermute | solution.py:818
  1054.6 10.1 reduce-scatter.18.cloned.1.call-done
  (413 shorter events, 395.9 us)
Async XLA Ops:
  7.2 61.3 %all-gather.8.cloned.1.call-start = ((), (), s32[]{:S(2)}) async-start(), calls=%async_computation.7 | async-start | bytes 5308416 | tf_op jit(solution)/shard_map/all_gather | solution.py:824
  11.0 114.8 %all-gather.10.cloned.1.call-start = ((), (), s32[]{:S(2)}) async-start(), calls=%async_computation.8 | async-start | bytes 9437184 | tf_op jit(solution)/shard_map/all_gather | solution.py:824
  12.1 248.9 %all-gather.12.cloned.1.call-start = ((), (), s32[]{:S(2)}) async-start(), calls=%async_computation.9 | async-start | bytes 4718592 | tf_op jit(solution)/shard_map/all_gather | solution.py:824
  16.5 50.8 %collective-permute-start = (bf16[1,512,2048]{2,1,0:T(8,128)(2,1)S(1)}, bf16[1,512,2048]{2,1,0:T(8,128)(2,1)}, u32[]{:S(2)}, u32[]{:S(2)}) collective-permute-start(bf16[1,512,2048]{2,1,0:T(8,128)(2,1)S(1)} %enter_kernel.1.refs_0_.refs_4_), channel_id=1, source_target_pairs={{0,1},{1,2},{2,3},{3,0},{4,5},{5,6},{6,7},{7,4},{8,9},{9,10},{10,1... | collective-permute-start | bytes 6291464 | tf_op jit(solution)/shard_map/ppermute | solution.py:818
  19.6 390.9 %all-gather.16.cloned.1.call-start = ((), (), s32[]{:S(2)}) async-start(), calls=%async_computation.11 | async-start | bytes 6488064 | tf_op jit(solution)/shard_map/all_gather | solution.py:824
  67.4 48.8 %collective-permute-start.1 = (bf16[1,512,2048]{2,1,0:T(8,128)(2,1)}, bf16[1,512,2048]{2,1,0:T(8,128)(2,1)S(1)}, u32[]{:S(2)}, u32[]{:S(2)}) collective-permute-start(bf16[1,512,2048]{2,1,0:T(8,128)(2,1)} %collective-permute-done.refs_0_.refs_4_.refs_1_), channel_id=1, source_target_pairs={{0,1},{1,2},{2,3},{3,0},{4,5},{5,6},{6,7},{7,4},{8,9},{9,10},{10,1... | collective-permute-start | bytes 6291464 | tf_op jit(solution)/shard_map/ppermute | solution.py:818
  116.2 48.3 %collective-permute-start.2 = (bf16[1,512,2048]{2,1,0:T(8,128)(2,1)S(1)}, bf16[1,512,2048]{2,1,0:T(8,128)(2,1)}, u32[]{:S(2)}, u32[]{:S(2)}) collective-permute-start(bf16[1,512,2048]{2,1,0:T(8,128)(2,1)S(1)} %collective-permute-done.1.refs_0_.refs_4_.refs_2_), channel_id=1, source_target_pairs={{0,1},{1,2},{2,3},{3,0},{4,5},{5,6},{6,7},{7,4},{8,9},{9,10},{10,1... | collective-permute-start | bytes 6291464 | tf_op jit(solution)/shard_map/ppermute | solution.py:818
  164.5 246.0 %all-gather.14.cloned.1.call-start = ((), (), s32[]{:S(2)}) async-start(), calls=%async_computation.10 | async-start | bytes 12976128 | tf_op jit(solution)/shard_map/all_gather | solution.py:824
  165.1 262.6 %all-gather.20.cloned.1.call-start = ((), (), s32[]{:S(2)}) async-start(), calls=%async_computation.13 | async-start | bytes 6488064 | tf_op jit(solution)/shard_map/all_gather | solution.py:824
  166.1 93.5 %collective-permute-start.5 = (bf16[1,512,2048]{2,1,0:T(8,128)(2,1)S(1)}, bf16[1,512,2048]{2,1,0:T(8,128)(2,1)}, u32[]{:S(2)}, u32[]{:S(2)}) collective-permute-start(bf16[1,512,2048]{2,1,0:T(8,128)(2,1)S(1)} %copy-done.10), channel_id=1, source_target_pairs={{0,1},{1,0},{2,3},{3,2},{4,5},{5,4},{6,7},{7,6},{8,9},{9,8},{10,11... | collective-permute-start | bytes 6291464 | tf_op jit(solution)/shard_map/ppermute | solution.py:818
  166.1 93.5 %collective-permute-start.3 = (bf16[256,2816]{1,0:T(8,128)(2,1)}, bf16[256,2816]{1,0:T(8,128)(2,1)}, u32[]{:S(2)}, u32[]{:S(2)}) collective-permute-start(bf16[256,2816]{1,0:T(8,128)(2,1)} %constant_dynamic-update-slice_fusion), channel_id=1, source_target_pairs={{0,2},{1,3},{2,0},{3,1},{4,6},{5,7},{6,4},{7,5},{8,10},{9,11},{10,... | collective-permute-start | bytes 4325384 | tf_op jit(solution)/shard_map/ppermute | solution.py:821
  166.1 93.5 %collective-permute-start.4 = (bf16[256,1408]{1,0:T(8,128)(2,1)S(1)}, bf16[256,1408]{1,0:T(8,128)(2,1)}, u32[]{:S(2)}, u32[]{:S(2)}) collective-permute-start(bf16[256,1408]{1,0:T(8,128)(2,1)S(1)} %copy-done.81), channel_id=1, source_target_pairs={{0,2},{1,3},{2,0},{3,1},{4,6},{5,7},{6,4},{7,5},{8,10},{9,11},{10,... | collective-permute-start | bytes 2162696 | tf_op jit(solution)/shard_map/ppermute | solution.py:821
  259.6 168.2 %all-gather.18.cloned.1.call-start = ((), (), s32[]{:S(2)}) async-start(), calls=%async_computation.12 | async-start | bytes 12976128 | tf_op jit(solution)/shard_map/all_gather | solution.py:824
  260.3 474.6 %reduce-scatter.10.cloned.1.call-start = ((), (), s32[]{:S(2)}) async-start(), calls=%async_computation.15 | async-start | bytes 3604480 | tf_op jit(solution)/shard_map/reduce_scatter | solution.py:835
  268.4 45.8 %collective-permute-start.6 = (bf16[1,512,2048]{2,1,0:T(8,128)(2,1)}, bf16[1,512,2048]{2,1,0:T(8,128)(2,1)S(1)}, u32[]{:S(2)}, u32[]{:S(2)}) collective-permute-start(bf16[1,512,2048]{2,1,0:T(8,128)(2,1)} %rows_matmul.32), channel_id=1, source_target_pairs={{0,1},{1,2},{2,3},{3,0},{4,5},{5,6},{6,7},{7,4},{8,9},{9,10},{10,1... | collective-permute-start | bytes 6291464 | tf_op jit(solution)/shard_map/ppermute | solution.py:818
  410.5 52.6 %collective-permute-start.9 = (bf16[1,512,2048]{2,1,0:T(8,128)(2,1)S(1)}, bf16[1,512,2048]{2,1,0:T(8,128)(2,1)}, u32[]{:S(2)}, u32[]{:S(2)}) collective-permute-start(bf16[1,512,2048]{2,1,0:T(8,128)(2,1)S(1)} %get-tuple-element.245.refs_0_), channel_id=1, source_target_pairs={{0,1},{1,0},{2,3},{3,2},{4,5},{5,4},{6,7},{7,6},{8,9},{9,8},{10,11... | collective-permute-start | bytes 6291464 | tf_op jit(solution)/shard_map/ppermute | solution.py:818
  514.1 46.9 %collective-permute-start.10 = (bf16[1,512,2048]{2,1,0:T(8,128)(2,1)}, bf16[1,512,2048]{2,1,0:T(8,128)(2,1)}, u32[]{:S(2)}, u32[]{:S(2)}) collective-permute-start(bf16[1,512,2048]{2,1,0:T(8,128)(2,1)} %rows_matmul.37), channel_id=1, source_target_pairs={{0,1},{1,0},{2,3},{3,2},{4,5},{5,4},{6,7},{7,6},{8,9},{9,8},{10,11... | collective-permute-start | bytes 6291464 | tf_op jit(solution)/shard_map/ppermute | solution.py:818
  576.3 49.7 %collective-permute-start.11 = (bf16[1,512,2048]{2,1,0:T(8,128)(2,1)}, bf16[1,512,2048]{2,1,0:T(8,128)(2,1)}, u32[]{:S(2)}, u32[]{:S(2)}) collective-permute-start(bf16[1,512,2048]{2,1,0:T(8,128)(2,1)} %get-tuple-element.276.refs_0_), channel_id=1, source_target_pairs={{0,1},{1,2},{2,3},{3,0},{4,5},{5,6},{6,7},{7,4},{8,9},{9,10},{10,1... | collective-permute-start | bytes 6291464 | tf_op jit(solution)/shard_map/ppermute | solution.py:818
  626.0 109.0 %reduce-scatter.8.cloned.1.call-start = ((), (), s32[]{:S(2)}) async-start(), calls=%async_computation.14 | async-start | bytes 7208960 | tf_op jit(solution)/shard_map/reduce_scatter | solution.py:835
  626.7 273.7 %reduce-scatter.12.cloned.1.call-start = ((), (), s32[]{:S(2)}) async-start(), calls=%async_computation.16 | async-start | bytes 3604480 | tf_op jit(solution)/shard_map/reduce_scatter | solution.py:835
  627.3 49.9 %collective-permute-start.14 = (bf16[1,512,2048]{2,1,0:T(8,128)(2,1)}, bf16[1,512,2048]{2,1,0:T(8,128)(2,1)}, u32[]{:S(2)}, u32[]{:S(2)}) collective-permute-start(bf16[1,512,2048]{2,1,0:T(8,128)(2,1)} %collective-permute-done.11.refs_0_.refs_1_), channel_id=1, source_target_pairs={{0,1},{1,2},{2,3},{3,0},{4,5},{5,6},{6,7},{7,4},{8,9},{9,10},{10,1... | collective-permute-start | bytes 6291464 | tf_op jit(solution)/shard_map/ppermute | solution.py:818
  677.2 223.2 %reduce-scatter.14.cloned.1.call-start = ((), (), s32[]{:S(2)}) async-start(), calls=%async_computation.17 | async-start | bytes 7208960 | tf_op jit(solution)/shard_map/reduce_scatter | solution.py:835
  678.0 294.6 %reduce-scatter.16.cloned.1.call-start = ((), (), s32[]{:S(2)}) async-start(), calls=%async_computation.18 | async-start | bytes 5242880 | tf_op jit(solution)/shard_map/reduce_scatter | solution.py:835
  678.0 48.8 %collective-permute-start.17 = (bf16[1,512,2048]{2,1,0:T(8,128)(2,1)}, bf16[1,512,2048]{2,1,0:T(8,128)(2,1)S(1)}, u32[]{:S(2)}, u32[]{:S(2)}) collective-permute-start(bf16[1,512,2048]{2,1,0:T(8,128)(2,1)} %collective-permute-done.14.refs_0_.refs_2_), channel_id=1, source_target_pairs={{0,1},{1,2},{2,3},{3,0},{4,5},{5,6},{6,7},{7,4},{8,9},{9,10},{10,1... | collective-permute-start | bytes 6291464 | tf_op jit(solution)/shard_map/ppermute | solution.py:818
  734.9 96.4 %collective-permute-start.18 = (bf16[1,512,2048]{2,1,0:T(8,128)(2,1)}, bf16[1,512,2048]{2,1,0:T(8,128)(2,1)S(1)}, u32[]{:S(2)}, u32[]{:S(2)}) collective-permute-start(bf16[1,512,2048]{2,1,0:T(8,128)(2,1)} %rows_matmul.39), channel_id=1, source_target_pairs={{0,1},{1,0},{2,3},{3,2},{4,5},{5,4},{6,7},{7,6},{8,9},{9,8},{10,11... | collective-permute-start | bytes 6291464 | tf_op jit(solution)/shard_map/ppermute | solution.py:818
  735.3 96.0 %collective-permute-start.19 = (bf16[256,2816]{1,0:T(8,128)(2,1)}, bf16[256,2816]{1,0:T(8,128)(2,1)S(1)}, u32[]{:S(2)}, u32[]{:S(2)}) collective-permute-start(bf16[256,2816]{1,0:T(8,128)(2,1)} %reduce-scatter.8.cloned.1.call-done), channel_id=1, source_target_pairs={{0,2},{1,3},{2,0},{3,1},{4,6},{5,7},{6,4},{7,5},{8,10},{9,11},{10,... | collective-permute-start | bytes 4325384 | tf_op jit(solution)/shard_map/ppermute | solution.py:821
  737.7 93.6 %collective-permute-start.20 = (bf16[256,1408]{1,0:T(8,128)(2,1)}, bf16[256,1408]{1,0:T(8,128)(2,1)S(1)}, u32[]{:S(2)}, u32[]{:S(2)}) collective-permute-start(bf16[256,1408]{1,0:T(8,128)(2,1)} %reduce-scatter.10.cloned.1.call-done), channel_id=1, source_target_pairs={{0,2},{1,3},{2,0},{3,1},{4,6},{5,7},{6,4},{7,5},{8,10},{9,11},{10,... | collective-permute-start | bytes 2162696 | tf_op jit(solution)/shard_map/ppermute | solution.py:821
  846.9 48.4 %collective-permute-start.21 = (bf16[1,512,2048]{2,1,0:T(8,128)(2,1)}, bf16[1,512,2048]{2,1,0:T(8,128)(2,1)}, u32[]{:S(2)}, u32[]{:S(2)}) collective-permute-start(bf16[1,512,2048]{2,1,0:T(8,128)(2,1)} %get-tuple-element.312), channel_id=1, source_target_pairs={{0,1},{1,2},{2,3},{3,0},{4,5},{5,6},{6,7},{7,4},{8,9},{9,10},{10,1... | collective-permute-start | bytes 6291464 | tf_op jit(solution)/shard_map/ppermute | solution.py:818
  895.3 157.1 %reduce-scatter.20.cloned.1.call-start = ((), (), s32[]{:S(2)}) async-start(), calls=%async_computation.20 | async-start | bytes 2621440 | tf_op jit(solution)/shard_map/reduce_scatter | solution.py:835
  922.1 50.5 %collective-permute-start.26 = (bf16[1,512,2048]{2,1,0:T(8,128)(2,1)}, bf16[1,512,2048]{2,1,0:T(8,128)(2,1)}, u32[]{:S(2)}, u32[]{:S(2)}) collective-permute-start(bf16[1,512,2048]{2,1,0:T(8,128)(2,1)} %add_convert_fusion.1), channel_id=1, source_target_pairs={{0,1},{1,2},{2,3},{3,0},{4,5},{5,6},{6,7},{7,4},{8,9},{9,10},{10,1... | collective-permute-start | bytes 6291464 | tf_op jit(solution)/shard_map/ppermute | solution.py:818
  977.4 50.1 %collective-permute-start.31 = (bf16[1,512,2048]{2,1,0:T(8,128)(2,1)}, bf16[1,512,2048]{2,1,0:T(8,128)(2,1)}, u32[]{:S(2)}, u32[]{:S(2)}) collective-permute-start(bf16[1,512,2048]{2,1,0:T(8,128)(2,1)} %add_convert_fusion), channel_id=1, source_target_pairs={{0,1},{1,2},{2,3},{3,0},{4,5},{5,6},{6,7},{7,4},{8,9},{9,10},{10,1... | collective-permute-start | bytes 6291464 | tf_op jit(solution)/shard_map/ppermute | solution.py:818
  979.6 85.0 %reduce-scatter.18.cloned.1.call-start = ((), (), s32[]{:S(2)}) async-start(), calls=%async_computation.19 | async-start | bytes 2949120 | tf_op jit(solution)/shard_map/reduce_scatter | solution.py:835
  (107 other events, 1367.0 us)
Sparse Core Ops, SparseCore 0:
  11.1 41.6 all-gather.7
  55.2 54.3 all-gather.9
  111.5 36.7 all-gather.11
  164.6 41.2 all-gather.15
  208.3 67.6 all-gather.13
  277.7 43.3 all-gather.19
  323.0 67.6 all-gather.17
  626.1 38.8 reduce-scatter.9
  667.9 65.8 reduce-scatter.7
  736.7 41.7 reduce-scatter.11
  781.4 65.8 reduce-scatter.13
  895.4 52.1 reduce-scatter.15
  979.7 34.4 reduce-scatter.19
  1028.0 36.5 reduce-scatter.17

commit v4 on v3

--- a/solution.py
+++ b/solution.py
@@ -701,7 +701,7 @@
     out[0] = (middle[0] + valid_rows(at) * total).astype(BF)
 
 
-def by_rows(kernel, at, arrays, gain, out_types, with_sum=False):
+def by_rows(kernel, at, arrays, gain, out_types, with_sum=False, limit=SMALL_LIMIT, cost=FREE):
     rows, piece, width = arrays[0].shape
     block = pl.BlockSpec((1, NORM_ROWS, width), lambda r, t, at: (r, t, 0))
     out_shape = [jax.ShapeDtypeStruct((rows, piece, width), x) for x in out_types]
@@ -724,13 +724,33 @@
         ),
         out_shape=out_shape,
         compiler_params=pltpu.CompilerParams(
-            dimension_semantics=("arbitrary", "arbitrary"), vmem_limit_bytes=SMALL_LIMIT
+            dimension_semantics=("arbitrary", "arbitrary"), vmem_limit_bytes=limit
         ),
-        cost_estimate=FREE,
+        cost_estimate=cost,
         name=kernel.__name__,
     )(at, *args)
 
 
+def apart_kernel(lanes, gu, gu_moved, down, down_moved, gate, up, out):
+    out[...] = down[...].astype(F32) + down_moved[...].astype(F32)
+    for at in range(0, gate.shape[1], lanes):
+        for first, half in ((2 * at, gate), (2 * at + lanes, up)):
+            half[:, at : at + lanes] = gu[:, first : first + lanes].astype(F32) + gu_moved[
+                :, first : first + lanes
+            ].astype(F32)
+
+
+def apart(gu, gu_moved, down, down_moved):
+    shape = jax.ShapeDtypeStruct(down.shape, F32)
+    return pl.pallas_call(
+        functools.partial(apart_kernel, lanes_of(down.shape[1])),
+        out_shape=[shape, shape, shape],
+        compiler_params=pltpu.CompilerParams(vmem_limit_bytes=SMALL_LIMIT),
+        cost_estimate=FREE,
+        name="apart",
+    )(gu, gu_moved, down, down_moved)
+
+
 def ring(size, group):
     return [(i, i // group * group + (i + 1) % group) for i in range(size)]
 
@@ -751,8 +771,7 @@
     return lax.dot_general(a, b, NN, preferred_element_type=F32)
 
 
-def sum_over(x, axis, size):
-    bit = 1
+def sum_over(x, axis, size, bit=1):
     while bit < size:
         x = x + lax.ppermute(x, axis, swap(size, bit))
         bit = bit * 2
@@ -764,13 +783,6 @@
     lanes = lanes_of(units)
     parts = [x[:, at : at + lanes] for at in range(0, units, lanes) for x in (gate, up)]
     return jnp.concatenate(parts, axis=1)
-
-
-def apart(both):
-    units = both.shape[1] // 2
-    lanes = lanes_of(units)
-    parts = [both[:, at : at + lanes] for at in range(0, 2 * units, lanes)]
-    return jnp.concatenate(parts[0::2], axis=1), jnp.concatenate(parts[1::2], axis=1)
 
 
 def per_device(
@@ -967,7 +979,7 @@
             own = two_part(s)
             total = (own + moved.astype(F32)).astype(BF)
     grad_middle, grad_attn, dgain_mlp = by_rows(
-        middle_back_kernel, at, [own, moved, middle, cotangent], gain_mlp, [F32, BF], True
+        middle_back_kernel, at, [own, moved, middle, cotangent], gain_mlp, [F32, BF], True, WIDE_LIMIT
     )
 
     pair_gu, pair_down = [None, None], [None, None]
@@ -1004,7 +1016,9 @@
             ]
             item, grad_mixed, *wout_parts = tie(item, grad_mixed, *wout_parts)
         attn_pieces.append(item)
-    grad_mixed = rows_matmul([(item, wo_full)], piece, into=grad_mixed, put=owner(size - 1))
+    grad_mixed = rows_matmul(
+        [(item, wo_full)], piece, into=grad_mixed, put=owner(size - 1), limit=VMEM_LIMIT
+    )
     sums_gu = [None, scatter_weight(pair_gu[1])]
     sums_down = [None, scatter_weight(pair_down[1])]
     sums_gu[0] = scatter_weight(pair_gu[0])
@@ -1037,12 +1051,15 @@
             sums_down[0], sums_gu[0] = last
         total, gqks, gvg = tie(total, gqks, gvg)
         if s == size:
-            total, moved_mlp, *small = tie(
-                total, moved_mlp, dcq, dck, dcv, dsm, dgain, dgain_mlp
+            total, pair_qks, pair_wout = tie(total, pair_qks, pair_wout)
+            pair_last = jnp.concatenate([pair_qks, pair_wout], axis=1)
+            total, moved_mlp, sums_gu[0], sums_down[0], moved_gu, moved_down, *small = tie(
+                total, moved_mlp, sums_gu[0], sums_down[0], moved_gu, moved_down,
+                dcq, dck, dcv, dsm, dgain, dgain_mlp,
             )
         moved = step(total, size)
         if s < size:
-            own, gain_part = one_part(s)
+            own, gain_part = one_part(s, BF)
             gain_sum = gain_sum + gain_part
         if s == 2:
             pair_vg = outer_halves(normed_pieces, [gvg] * size, places, 512, 4)
@@ -1056,7 +1073,7 @@
                 moved, own, pair_qks, pair_wout, scatter_weight(pair_vg)
             )
         if s < size:
-            total = (own + moved.astype(F32)).astype(BF)
+            total = (own.astype(F32) + moved.astype(F32)).astype(BF)
             continue
         own, gain_part = one_part(0)
         small = jnp.concatenate(
@@ -1064,25 +1081,28 @@
             axis=1,
         )
         small = sum_over(small, "dp", data)
-        out_wgate, out_wup = apart(sums_gu[0].astype(F32) + moved_gu.astype(F32))
-        out_wdown = sums_down[0].astype(F32) + moved_down.astype(F32)
+        out_wgate, out_wup, out_wdown = apart(sums_gu[0], moved_gu, sums_down[0], moved_down)
         mixed_rows = by_rows(result_kernel, at, [own_mlp, moved_mlp, middle], None, [BF])[0]
         moved, own, small, out_wgate, out_wup, out_wdown, mixed_rows = tie(
             moved, own, small, out_wgate, out_wup, out_wdown, mixed_rows
         )
+    leave_cost = pl.CostEstimate(flops=0, bytes_accessed=14 * tokens.size, transcendentals=0)
     tokens_grad = by_rows(
-        leave_kernel, at, [own, moved, tokens, grad_middle], gain_attn, [BF]
+        leave_kernel, at, [own, moved, tokens, grad_middle], gain_attn, [BF], False, WIDE_LIMIT,
+        leave_cost,
     )[0]
     out_vg = out_vg.astype(F32)
-    out_wout = scatter_weight(pair_wout).astype(F32)
-    out_qks = scatter_weight(pair_qks).astype(F32)
+    out_last = scatter_weight(pair_last).astype(F32)
+    out_qks, out_wout = out_last[:, : gqks.shape[2]], out_last[:, gqks.shape[2] :]
 
     taps_width = 2 * key_width + value_width
     own_width = taps_width + 128
     spread = lax.dynamic_update_slice_in_dim(
         jnp.zeros((4, size * own_width), F32), small[:, :own_width], me * own_width, 1
     )
-    small = sum_over(jnp.concatenate([spread, small[:, own_width:]], axis=1), "head", size)
+    small = jnp.concatenate([spread, small[:, own_width:]], axis=1)
+    crossed, tokens_grad = tie(lax.ppermute(small, "head", swap(size, 1)), tokens_grad)
+    small = sum_over(small + crossed, "head", size, 2)
     by_head = [small[:, i * own_width : (i + 1) * own_width] for i in range(size)]
     taps = lambda start, stop: jnp.concatenate([x[:, start:stop] for x in by_head], axis=1)
     conv_sums = (

time: 1080 us -> 1060 us (0.981)
  waiting for transfers between devices: 282 us -> 266 us
    ppermute x16, waiting for transfers between devices: 221 us -> 208 us  [step(): return lax.ppermute(x, 'head', ring(size, group))]
    unnamed x217 -> x205, local copies, waits for them, and re-layouts: 95.3 us -> 84.4 us
  transfers between devices with their start and end apart: 51 -> 50, of which waited for: 17 -> 17; matrix products, arithmetic and copies ran while one was open for 6% -> 5% of each run, Pallas kernels for 52% -> 53%
where the time goes in v4:
time: 1060 us; the launch traced here: 1050 us
  Pallas kernels  621 us (59%)
  waiting for transfers between devices  266 us (25%)
  local copies, waits for them, and re-layouts  96.3 us (9%)
  other arithmetic  26.4 us (2%)
  starting transfers between devices  24.3 us (2%)
  between operations  15.6 us (1%)
    pallas_call x24, Pallas kernels, rows_matmul(): pl.pallas_call(functools.partial(rows_kernel, len(pairs), nt, weigh is no...  240 us
    ppermute x16, waiting for transfers between devices, step(): return lax.ppermute(x, 'head', ring(size, group))  208 us
    pallas_call x16, Pallas kernels, outer_sum(): pl.pallas_call(functools.partial(outer_kernel, len(xs), data // 2, [len(x...  159 us
    pallas_call x1, Pallas kernels, mixer_backward(): pl.pallas_call(functools.partial(mixer_backward_kernel, heads), grid=(row...  86 us
    unnamed x205, local copies, waits for them, and re-layouts  84.4 us
    pallas_call x4, Pallas kernels, mlp_block(): pl.pallas_call(functools.partial(kernel, lanes_of(units)), grid=(pl.cdiv(...  63.6 us
    pallas_call x1, Pallas kernels, mixer_forward(): pl.pallas_call(functools.partial(mixer_forward_kernel, heads), grid=(rows...  45.7 us
    ppermute x4, waiting for transfers between devices, opposite(): return lax.ppermute(x, 'head', across(size))  24.7 us
  transfers between devices with their start and end apart: 50, of which 17 were waited for; matrix products, arithmetic and copies ran while one was open for 5% of the time, Pallas kernels for 53%

profile of v4, /device:TPU:0, one launch (start us, length us, event | category | flops | bytes accessed | tf_op | source)
XLA Modules:
  0.0 1049.9 jit_solution(13542278370963676864)
XLA Ops:
  46.2 21.1 %collective-permute-done.refs_0_.refs_4_.refs_1_ = bf16[1,512,2048]{2,1,0:T(8,128)(2,1)} collective-permute-done((bf16[1,512,2048]{2,1,0:T(8,128)(2,1)S(1)}, bf16[1,512,2048]{2,1,0:T(8,128)(2,1)}, u32[]{:S(2)}, u32[]{:S(2)}) %collective-permute-start) | collective-permute-done | bytes 2097184 | tf_op jit(solution)/shard_map/ppermute | solution.py:830
  84.5 31.7 %collective-permute-done.1.refs_0_.refs_4_.refs_2_ = bf16[1,512,2048]{2,1,0:T(8,128)(2,1)S(1)} collective-permute-done((bf16[1,512,2048]{2,1,0:T(8,128)(2,1)}, bf16[1,512,2048]{2,1,0:T(8,128)(2,1)S(1)}, u32[]{:S(2)}, u32[]{:S(2)}) %collective-permute-start.1) | collective-permute-done | bytes 2097184 | tf_op jit(solution)/shard_map/ppermute | solution.py:830
  135.8 10.0 rows_matmul.28.refs_2_
  145.8 10.1 rows_matmul.29.refs_2_
  171.2 9.9 rows_matmul.31.pv.pg.tv
  189.2 45.7 %mixer_forward.1 = (bf16[1,2048,1024]{2,1,0:T(8,128)(2,1)S(1)}, bf16[1,16,4,128,128]{4,3,2,1,0:T(8,128)(2,1)S(1)}, bf16[1,16,4,128,256]{4,3,2,1,0:T(8,128)(2,1)S(1)}, bf16[1,2048,1024]{2,1,0:T(8,128)(2,1)}) custom-call(f32[1,2048,1152]{2,1,0:T(8,128)} %rows_matmul.30.pq.pk.ps.tq.tk, f32[1,2048,1152]{2,1,0:T(8,128)} %rows_matmul.30.pq.pk.ps.tq.tk, ...), custom_call_target="tpu_custom_call" | custom-call | bytes 192500000 | tf_op jit(solution)/shard_map/mixer_forward/pallas_call | solution.py:372
  240.3 19.2 %collective-permute-done.4 = bf16[256,1408]{1,0:T(8,128)(2,1)} collective-permute-done((bf16[256,1408]{1,0:T(8,128)(2,1)S(1)}, bf16[256,1408]{1,0:T(8,128)(2,1)}, u32[]{:S(2)}, u32[]{:S(2)}) %collective-permute-start.4) | collective-permute-done | bytes 720928 | tf_op jit(solution)/shard_map/ppermute | solution.py:833
  274.1 40.0 %collective-permute-done.6 = bf16[1,512,2048]{2,1,0:T(8,128)(2,1)S(1)} collective-permute-done((bf16[1,512,2048]{2,1,0:T(8,128)(2,1)}, bf16[1,512,2048]{2,1,0:T(8,128)(2,1)S(1)}, u32[]{:S(2)}, u32[]{:S(2)}) %collective-permute-start.6) | collective-permute-done | bytes 2097184 | tf_op jit(solution)/shard_map/ppermute | solution.py:830
  320.5 39.4 %collective-permute-done.7 = bf16[1,512,2048]{2,1,0:T(8,128)(2,1)S(1)} collective-permute-done((bf16[1,512,2048]{2,1,0:T(8,128)(2,1)S(1)}, bf16[1,512,2048]{2,1,0:T(8,128)(2,1)S(1)}, u32[]{:S(2)}, u32[]{:S(2)}) %collective-permute-start.7) | collective-permute-done | bytes 2097184 | tf_op jit(solution)/shard_map/ppermute | solution.py:830
  366.4 39.6 %collective-permute-done.8.moved = bf16[1,512,2048]{2,1,0:T(8,128)(2,1)S(1)} collective-permute-done((bf16[1,512,2048]{2,1,0:T(8,128)(2,1)S(1)}, bf16[1,512,2048]{2,1,0:T(8,128)(2,1)S(1)}, u32[]{:S(2)}, u32[]{:S(2)}) %collective-permute-start.8) | collective-permute-done | bytes 2097184 | tf_op jit(solution)/shard_map/ppermute | solution.py:830
  411.8 15.9 %mlp_block.4 = (bf16[512,1408]{1,0:T(8,128)(2,1)}, bf16[512,2816]{1,0:T(8,128)(2,1)}) custom-call(bf16[512,2048]{1,0:T(8,128)(2,1)} %bitcast.50, bf16[2048,2816]{1,0:T(8,128)(2,1)} %all-gather.14.cloned.1.call-done.wgu.refs_1_, bf16[512,2048]{1,0:T(8,128)(2,1)} %bitcast.48, bf16[2048,1408]{1,0:T(8,128)(2,1)} %all-gather.16.cloned.1.call-done.wd.refs_1_), custom_call_target="tpu_custom_call" | custom-call | tf_op jit(solution)/shard_map/mlp_block/pallas_call | solution.py:634
  427.7 15.9 %mlp_block.5 = (bf16[512,1408]{1,0:T(8,128)(2,1)}, bf16[512,2816]{1,0:T(8,128)(2,1)}) custom-call(bf16[512,2048]{1,0:T(8,128)(2,1)} %bitcast.51, bf16[2048,2816]{1,0:T(8,128)(2,1)} %all-gather.18.cloned.1.call-done.wgu.refs_3_, bf16[512,2048]{1,0:T(8,128)(2,1)} %bitcast.49, bf16[2048,1408]{1,0:T(8,128)(2,1)} %all-gather.20.cloned.1.call-done.wd.refs_3_), custom_call_target="tpu_custom_call" | custom-call | tf_op jit(solution)/shard_map/mlp_block/pallas_call | solution.py:634
  444.2 18.9 %rows_matmul.36.own = f32[1,512,2048]{2,1,0:T(8,128)} custom-call(s32[2]{0:T(128)} %broadcast.93.at, bf16[1,512,2816]{2,1,0:T(8,128)(2,1)} %bitcast.52, bf16[2048,2816]{1,0:T(8,128)(2,1)} %all-gather.14.cloned.1.call-done.wgu.refs_1_, bf16[1,512,2816]{2,1,0:T(8,128)(2,1)} %bitcast.58, bf16[2048,2816]{1,0:T(8,128)(2,1)} %all-gather.18.cloned.1.call-done.wgu.refs_3_), custom_call_target="tpu_custom_call" | custom-call | tf_op jit(solution)/shard_map/rows_matmul/pallas_call | solution.py:509
  463.0 15.9 %mlp_block.7 = (bf16[512,1408]{1,0:T(8,128)(2,1)}, bf16[512,2816]{1,0:T(8,128)(2,1)}) custom-call(bf16[512,2048]{1,0:T(8,128)(2,1)} %bitcast.17.x, bf16[2048,2816]{1,0:T(8,128)(2,1)} %all-gather.18.cloned.1.call-done.wgu.refs_3_, bf16[512,2048]{1,0:T(8,128)(2,1)} %bitcast.18.g, bf16[2048,1408]{1,0:T(8,128)(2,1)} %all-gather.20.cloned.1.call-done.wd.refs_3_), custom_call_target="tpu_custom_call" | custom-call | tf_op jit(solution)/shard_map/mlp_block/pallas_call | solution.py:634
  478.9 15.9 %mlp_block.6 = (bf16[512,1408]{1,0:T(8,128)(2,1)}, bf16[512,2816]{1,0:T(8,128)(2,1)}) custom-call(bf16[512,2048]{1,0:T(8,128)(2,1)} %bitcast.17.x, bf16[2048,2816]{1,0:T(8,128)(2,1)} %all-gather.14.cloned.1.call-done.wgu.refs_1_, bf16[512,2048]{1,0:T(8,128)(2,1)} %bitcast.18.g, bf16[2048,1408]{1,0:T(8,128)(2,1)} %all-gather.16.cloned.1.call-done.wd.refs_1_), custom_call_target="tpu_custom_call" | custom-call | tf_op jit(solution)/shard_map/mlp_block/pallas_call | solution.py:634
  494.8 19.0 %rows_matmul.37 = bf16[1,512,2048]{2,1,0:T(8,128)(2,1)} custom-call(s32[2]{0:T(128)} %broadcast.93.at, bf16[1,512,2816]{2,1,0:T(8,128)(2,1)} %bitcast.55, bf16[2048,2816]{1,0:T(8,128)(2,1)} %all-gather.14.cloned.1.call-done.wgu.refs_1_, bf16[1,512,2816]{2,1,0:T(8,128)(2,1)} %bitcast.61, bf16[2048,2816]{1,0:T(8,128)(2,1)} %all-gather.18.cloned.1.call-done.wgu.refs_3_), custom_call_target="tpu_custom_call" | custom-call | tf_op jit(solution)/shard_map/rows_matmul/pallas_call | solution.py:509
  526.7 11.6 %outer_sum.16 = bf16[1024,2816]{1,0:T(8,128)(2,1)} custom-call(s32[3]{0:T(128)S(1)} %stack.57.at, bf16[1,512,2048]{2,1,0:T(8,128)(2,1)S(1)} %copy-done.16, bf16[1,512,2048]{2,1,0:T(8,128)(2,1)} %collective-permute-done.9.refs_1_, bf16[1,512,2816]{2,1,0:T(8,128)(2,1)S(1)} %bitcast.59, bf16[1,512,2816]{2,1,0:T(8,128)(2,1)S(1)} %bitcast.62), custom_call_target="tpu_custom_call" | custom-call | tf_op jit(solution)/shard_map/outer_sum/pallas_call | solution.py:579
  538.3 11.7 %rows_matmul.39 = bf16[1,512,2048]{2,1,0:T(8,128)(2,1)} custom-call(s32[2]{0:T(128)} %broadcast.93.at, bf16[1,512,1408]{2,1,0:T(8,128)(2,1)} %bitcast.64, bf16[2048,1408]{1,0:T(8,128)(2,1)} %all-gather.16.cloned.1.call-done.wd.refs_1_, bf16[1,512,1408]{2,1,0:T(8,128)(2,1)} %bitcast.67, bf16[2048,1408]{1,0:T(8,128)(2,1)} %all-gather.20.cloned.1.call-done.wd.refs_3_), custom_call_target="tpu_custom_call" | custom-call | tf_op jit(solution)/shard_map/rows_matmul/pallas_call | solution.py:509
  550.0 12.1 %rows_matmul.38.own = f32[1,512,2048]{2,1,0:T(8,128)} custom-call(s32[2]{0:T(128)} %broadcast.93.at, bf16[1,512,1408]{2,1,0:T(8,128)(2,1)} %bitcast.70, bf16[2048,1408]{1,0:T(8,128)(2,1)} %all-gather.16.cloned.1.call-done.wd.refs_1_, bf16[1,512,1408]{2,1,0:T(8,128)(2,1)} %bitcast.73, bf16[2048,1408]{1,0:T(8,128)(2,1)} %all-gather.20.cloned.1.call-done.wd.refs_3_), custom_call_target="tpu_custom_call" | custom-call | tf_op jit(solution)/shard_map/rows_matmul/pallas_call | solution.py:509
  585.7 12.0 %outer_sum.20 = bf16[1024,2816]{1,0:T(8,128)(2,1)} custom-call(s32[3]{0:T(128)S(1)} %stack.57.at, bf16[1,512,2048]{2,1,0:T(8,128)(2,1)S(1)} %copy-done.16, bf16[1,512,2048]{2,1,0:T(8,128)(2,1)} %collective-permute-done.9.refs_1_, bf16[1,512,2816]{2,1,0:T(8,128)(2,1)S(1)} %bitcast.53, bf16[1,512,2816]{2,1,0:T(8,128)(2,1)S(1)} %bitcast.56), custom_call_target="tpu_custom_call" | custom-call | tf_op jit(solution)/shard_map/outer_sum/pallas_call | solution.py:579
  612.5 12.4 %outer_sum.18 = bf16[1024,2816]{1,0:T(8,128)(2,1)} custom-call(s32[3]{0:T(128)S(1)} %stack.59.at, bf16[1,512,2048]{2,1,0:T(8,128)(2,1)S(1)} %copy-done.17, bf16[1,512,2048]{2,1,0:T(8,128)(2,1)} %collective-permute-done.9.refs_1_, bf16[1,512,2816]{2,1,0:T(8,128)(2,1)S(1)} %bitcast.60, bf16[1,512,2816]{2,1,0:T(8,128)(2,1)S(1)} %bitcast.63, ...), custom_call_target="tpu_custom_call" | custom-call | tf_op jit(solution)/shard_map/outer_sum/pallas_call | solution.py:579
  626.5 12.7 %collective-permute-done.16.refs_4_ = bf16[1024,1408]{1,0:T(8,128)(2,1)S(1)} collective-permute-done((bf16[1024,1408]{1,0:T(8,128)(2,1)}, bf16[1024,1408]{1,0:T(8,128)(2,1)S(1)}, u32[]{:S(2)}, u32[]{:S(2)}) %collective-permute-start.16) | collective-permute-done | bytes 2883616 | tf_op jit(solution)/shard_map/ppermute | solution.py:839
  657.3 12.6 %outer_sum.22 = bf16[1024,2816]{1,0:T(8,128)(2,1)} custom-call(s32[3]{0:T(128)S(1)} %stack.59.at, bf16[1,512,2048]{2,1,0:T(8,128)(2,1)S(1)} %copy-done.18, bf16[1,512,2048]{2,1,0:T(8,128)(2,1)} %collective-permute-done.9.refs_1_, bf16[1,512,2816]{2,1,0:T(8,128)(2,1)S(1)} %bitcast.54, bf16[1,512,2816]{2,1,0:T(8,128)(2,1)S(1)} %bitcast.57, ...), custom_call_target="tpu_custom_call" | custom-call | tf_op jit(solution)/shard_map/outer_sum/pallas_call | solution.py:579
  740.0 86.0 %mixer_backward.1 = (bf16[1,2048,1152]{2,1,0:T(8,128)(2,1)}, bf16[1,2048,2048]{2,1,0:T(8,128)(2,1)}, f32[8,512]{1,0:T(8,128)S(1)}, f32[8,512]{1,0:T(8,128)S(1)},...) custom-call(f32[1,2048,1024]{2,1,0:T(8,128)} %rows_matmul.43.dm, ...), custom_call_target="tpu_custom_call" | custom-call | bytes 315000000 | tf_op jit(solution)/shard_map/mixer_backward/pallas_call | solution.py:419
  834.8 13.6 %rows_matmul.44 = (bf16[1,512,2048]{2,1,0:T(8,128)(2,1)}, f32[1,8,2048]{2,1,0:T(8,128)}) custom-call(s32[2]{0:T(128)} %pad_add_fusion.3.at, bf16[1,2048,1152]{2,1,0:T(8,128)(2,1)} %get-tuple-element.367.refs_0_.refs_4_.refs_5_.refs_6_.refs_7_, bf16[2048,1152]{1,0:T(8,128)(2,1)} %all-gather.8.cloned.1.call-done.refs_1_, ...), custom_call_target="tpu_custom_call" | custom-call | tf_op jit(solution)/shard_map/rows_matmul/pallas_call | solution.py:509
  848.6 16.0 %outer_sum.26 = (bf16[256,2048]{1,0:T(8,128)(2,1)}, bf16[256,2048]{1,0:T(8,128)(2,1)}, bf16[256,2048]{1,0:T(8,128)(2,1)}, bf16[256,2048]{1,0:T(8,128)(2,1)}) custom-call(s32[5]{0:T(128)S(1)} %stack.63.at, bf16[1,512,2048]{2,1,0:T(8,128)(2,1)S(1)} %copy-done.7, bf16[1,512,2048]{2,1,0:T(8,128)(2,1)} %collective-permute-done.refs_0_.refs_4_.refs_1_, ...), custom_call_target="tpu_custom_call" | custom-call | tf_op jit(solution)/shard_map/outer_sum/pallas_call | solution.py:579
  865.7 13.5 %rows_matmul.45 = (bf16[1,512,2048]{2,1,0:T(8,128)(2,1)}, f32[1,8,2048]{2,1,0:T(8,128)}) custom-call(s32[2]{0:T(128)} %copy-done.73, bf16[1,2048,1152]{2,1,0:T(8,128)(2,1)} %get-tuple-element.367.refs_0_.refs_4_.refs_5_.refs_6_.refs_7_, bf16[2048,1152]{1,0:T(8,128)(2,1)} %all-gather.8.cloned.1.call-done.refs_1_, ...), custom_call_target="tpu_custom_call" | custom-call | tf_op jit(solution)/shard_map/rows_matmul/pallas_call | solution.py:509
  879.2 16.2 %outer_sum.27 = bf16[1024,2048]{1,0:T(8,128)(2,1)} custom-call(s32[5]{0:T(128)S(1)} %stack.62.at, bf16[1,512,2048]{2,1,0:T(8,128)(2,1)S(1)} %copy-done.7, bf16[1,512,2048]{2,1,0:T(8,128)(2,1)} %collective-permute-done.refs_0_.refs_4_.refs_1_, bf16[1,512,2048]{2,1,0:T(8,128)(2,1)} %copy-done.10, ...), custom_call_target="tpu_custom_call" | custom-call | tf_op jit(solution)/shard_map/outer_sum/pallas_call | solution.py:579
  905.7 11.6 %outer_sum.28 = (bf16[512,1152]{1,0:T(8,128)(2,1)}, bf16[512,1152]{1,0:T(8,128)(2,1)}) custom-call(s32[5]{0:T(128)S(1)} %stack.63.at, bf16[1,512,2048]{2,1,0:T(8,128)(2,1)S(1)} %copy-done.8, bf16[1,512,2048]{2,1,0:T(8,128)(2,1)} %collective-permute-done.refs_0_.refs_4_.refs_1_, bf16[1,512,2048]{2,1,0:T(8,128)(2,1)S(1)} %copy-done.11, ...), custom_call_target="tpu_custom_call" | custom-call | tf_op jit(solution)/shard_map/outer_sum/pallas_call | solution.py:579
  924.1 14.3 %rows_matmul.46 = (bf16[1,512,2048]{2,1,0:T(8,128)(2,1)}, f32[1,8,2048]{2,1,0:T(8,128)}) custom-call(s32[2]{0:T(128)} %copy-done.72, bf16[1,2048,1152]{2,1,0:T(8,128)(2,1)} %get-tuple-element.367.refs_0_.refs_4_.refs_5_.refs_6_.refs_7_, bf16[2048,1152]{1,0:T(8,128)(2,1)} %all-gather.8.cloned.1.call-done.refs_1_, ...), custom_call_target="tpu_custom_call" | custom-call | tf_op jit(solution)/shard_map/rows_matmul/pallas_call | solution.py:509
  946.3 11.3 %outer_sum.29 = bf16[1024,1152]{1,0:T(8,128)(2,1)} custom-call(s32[5]{0:T(128)S(1)} %stack.62.at, bf16[1,512,2048]{2,1,0:T(8,128)(2,1)S(1)} %copy-done.9, bf16[1,512,2048]{2,1,0:T(8,128)(2,1)} %collective-permute-done.refs_0_.refs_4_.refs_1_, bf16[1,512,2048]{2,1,0:T(8,128)(2,1)S(1)} %copy-done.12, ...), custom_call_target="tpu_custom_call" | custom-call | tf_op jit(solution)/shard_map/outer_sum/pallas_call | solution.py:579
  966.8 14.2 %rows_matmul.47 = (f32[1,512,2048]{2,1,0:T(8,128)}, f32[1,8,2048]{2,1,0:T(8,128)}) custom-call(s32[2]{0:T(128)} %copy-done.71, bf16[1,2048,1152]{2,1,0:T(8,128)(2,1)} %get-tuple-element.367.refs_0_.refs_4_.refs_5_.refs_6_.refs_7_, bf16[2048,1152]{1,0:T(8,128)(2,1)} %all-gather.8.cloned.1.call-done.refs_1_, ...), custom_call_target="tpu_custom_call" | custom-call | tf_op jit(solution)/shard_map/rows_matmul/pallas_call | solution.py:509
  (397 shorter events, 384.2 us)
Async XLA Ops:
  7.2 61.3 %all-gather.8.cloned.1.call-start = ((), (), s32[]{:S(2)}) async-start(), calls=%async_computation.6 | async-start | bytes 5308416 | tf_op jit(solution)/shard_map/all_gather | solution.py:836
  11.0 114.9 %all-gather.10.cloned.1.call-start = ((), (), s32[]{:S(2)}) async-start(), calls=%async_computation.7 | async-start | bytes 9437184 | tf_op jit(solution)/shard_map/all_gather | solution.py:836
  12.1 248.9 %all-gather.12.cloned.1.call-start = ((), (), s32[]{:S(2)}) async-start(), calls=%async_computation.8 | async-start | bytes 4718592 | tf_op jit(solution)/shard_map/all_gather | solution.py:836
  16.5 50.8 %collective-permute-start = (bf16[1,512,2048]{2,1,0:T(8,128)(2,1)S(1)}, bf16[1,512,2048]{2,1,0:T(8,128)(2,1)}, u32[]{:S(2)}, u32[]{:S(2)}) collective-permute-start(bf16[1,512,2048]{2,1,0:T(8,128)(2,1)S(1)} %enter_kernel.1.refs_0_.refs_4_), channel_id=1, source_target_pairs={{0,1},{1,2},{2,3},{3,0},{4,5},{5,6},{6,7},{7,4},{8,9},{9,10},{10,1... | collective-permute-start | bytes 6291464 | tf_op jit(solution)/shard_map/ppermute | solution.py:830
  19.6 390.9 %all-gather.16.cloned.1.call-start = ((), (), s32[]{:S(2)}) async-start(), calls=%async_computation.10 | async-start | bytes 6488064 | tf_op jit(solution)/shard_map/all_gather | solution.py:836
  67.3 48.8 %collective-permute-start.1 = (bf16[1,512,2048]{2,1,0:T(8,128)(2,1)}, bf16[1,512,2048]{2,1,0:T(8,128)(2,1)S(1)}, u32[]{:S(2)}, u32[]{:S(2)}) collective-permute-start(bf16[1,512,2048]{2,1,0:T(8,128)(2,1)} %collective-permute-done.refs_0_.refs_4_.refs_1_), channel_id=1, source_target_pairs={{0,1},{1,2},{2,3},{3,0},{4,5},{5,6},{6,7},{7,4},{8,9},{9,10},{10,1... | collective-permute-start | bytes 6291464 | tf_op jit(solution)/shard_map/ppermute | solution.py:830
  116.2 48.3 %collective-permute-start.2 = (bf16[1,512,2048]{2,1,0:T(8,128)(2,1)S(1)}, bf16[1,512,2048]{2,1,0:T(8,128)(2,1)}, u32[]{:S(2)}, u32[]{:S(2)}) collective-permute-start(bf16[1,512,2048]{2,1,0:T(8,128)(2,1)S(1)} %collective-permute-done.1.refs_0_.refs_4_.refs_2_), channel_id=1, source_target_pairs={{0,1},{1,2},{2,3},{3,0},{4,5},{5,6},{6,7},{7,4},{8,9},{9,10},{10,1... | collective-permute-start | bytes 6291464 | tf_op jit(solution)/shard_map/ppermute | solution.py:830
  164.5 246.0 %all-gather.14.cloned.1.call-start = ((), (), s32[]{:S(2)}) async-start(), calls=%async_computation.9 | async-start | bytes 12976128 | tf_op jit(solution)/shard_map/all_gather | solution.py:836
  165.1 262.6 %all-gather.20.cloned.1.call-start = ((), (), s32[]{:S(2)}) async-start(), calls=%async_computation.12 | async-start | bytes 6488064 | tf_op jit(solution)/shard_map/all_gather | solution.py:836
  166.1 93.5 %collective-permute-start.5 = (bf16[1,512,2048]{2,1,0:T(8,128)(2,1)S(1)}, bf16[1,512,2048]{2,1,0:T(8,128)(2,1)}, u32[]{:S(2)}, u32[]{:S(2)}) collective-permute-start(bf16[1,512,2048]{2,1,0:T(8,128)(2,1)S(1)} %copy-done.13), channel_id=1, source_target_pairs={{0,1},{1,0},{2,3},{3,2},{4,5},{5,4},{6,7},{7,6},{8,9},{9,8},{10,11... | collective-permute-start | bytes 6291464 | tf_op jit(solution)/shard_map/ppermute | solution.py:830
  166.1 93.5 %collective-permute-start.3 = (bf16[256,2816]{1,0:T(8,128)(2,1)}, bf16[256,2816]{1,0:T(8,128)(2,1)}, u32[]{:S(2)}, u32[]{:S(2)}) collective-permute-start(bf16[256,2816]{1,0:T(8,128)(2,1)} %slice_dynamic-update-slice_fusion), channel_id=1, source_target_pairs={{0,2},{1,3},{2,0},{3,1},{4,6},{5,7},{6,4},{7,5},{8,10},{9,11},{10,... | collective-permute-start | bytes 4325384 | tf_op jit(solution)/shard_map/ppermute | solution.py:833
  166.1 93.5 %collective-permute-start.4 = (bf16[256,1408]{1,0:T(8,128)(2,1)S(1)}, bf16[256,1408]{1,0:T(8,128)(2,1)}, u32[]{:S(2)}, u32[]{:S(2)}) collective-permute-start(bf16[256,1408]{1,0:T(8,128)(2,1)S(1)} %copy-done.81), channel_id=1, source_target_pairs={{0,2},{1,3},{2,0},{3,1},{4,6},{5,7},{6,4},{7,5},{8,10},{9,11},{10,... | collective-permute-start | bytes 2162696 | tf_op jit(solution)/shard_map/ppermute | solution.py:833
  259.6 168.2 %all-gather.18.cloned.1.call-start = ((), (), s32[]{:S(2)}) async-start(), calls=%async_computation.11 | async-start | bytes 12976128 | tf_op jit(solution)/shard_map/all_gather | solution.py:836
  260.3 471.5 %reduce-scatter.9.cloned.1.call-start = ((), (), s32[]{:S(2)}) async-start(), calls=%async_computation.14 | async-start | bytes 3604480 | tf_op jit(solution)/shard_map/reduce_scatter | solution.py:847
  268.4 45.8 %collective-permute-start.6 = (bf16[1,512,2048]{2,1,0:T(8,128)(2,1)}, bf16[1,512,2048]{2,1,0:T(8,128)(2,1)S(1)}, u32[]{:S(2)}, u32[]{:S(2)}) collective-permute-start(bf16[1,512,2048]{2,1,0:T(8,128)(2,1)} %rows_matmul.32), channel_id=1, source_target_pairs={{0,1},{1,2},{2,3},{3,0},{4,5},{5,6},{6,7},{7,4},{8,9},{9,10},{10,1... | collective-permute-start | bytes 6291464 | tf_op jit(solution)/shard_map/ppermute | solution.py:830
  360.6 45.4 %collective-permute-start.8 = (bf16[1,512,2048]{2,1,0:T(8,128)(2,1)S(1)}, bf16[1,512,2048]{2,1,0:T(8,128)(2,1)S(1)}, u32[]{:S(2)}, u32[]{:S(2)}) collective-permute-start(bf16[1,512,2048]{2,1,0:T(8,128)(2,1)S(1)} %add_convert_fusion.2), channel_id=1, source_target_pairs={{0,1},{1,2},{2,3},{3,0},{4,5},{5,6},{6,7},{7,4},{8,9},{9,10},{10,1... | collective-permute-start | bytes 6291464 | tf_op jit(solution)/shard_map/ppermute | solution.py:830
  410.5 52.6 %collective-permute-start.9 = (bf16[1,512,2048]{2,1,0:T(8,128)(2,1)S(1)}, bf16[1,512,2048]{2,1,0:T(8,128)(2,1)}, u32[]{:S(2)}, u32[]{:S(2)}) collective-permute-start(bf16[1,512,2048]{2,1,0:T(8,128)(2,1)S(1)} %get-tuple-element.257.refs_0_), channel_id=1, source_target_pairs={{0,1},{1,0},{2,3},{3,2},{4,5},{5,4},{6,7},{7,6},{8,9},{9,8},{10,11... | collective-permute-start | bytes 6291464 | tf_op jit(solution)/shard_map/ppermute | solution.py:830
  513.8 48.4 %collective-permute-start.10 = (bf16[1,512,2048]{2,1,0:T(8,128)(2,1)}, bf16[1,512,2048]{2,1,0:T(8,128)(2,1)}, u32[]{:S(2)}, u32[]{:S(2)}) collective-permute-start(bf16[1,512,2048]{2,1,0:T(8,128)(2,1)} %rows_matmul.37), channel_id=1, source_target_pairs={{0,1},{1,0},{2,3},{3,2},{4,5},{5,4},{6,7},{7,6},{8,9},{9,8},{10,11... | collective-permute-start | bytes 6291464 | tf_op jit(solution)/shard_map/ppermute | solution.py:830
  572.4 52.6 %collective-permute-start.11 = (bf16[1,512,2048]{2,1,0:T(8,128)(2,1)}, bf16[1,512,2048]{2,1,0:T(8,128)(2,1)}, u32[]{:S(2)}, u32[]{:S(2)}) collective-permute-start(bf16[1,512,2048]{2,1,0:T(8,128)(2,1)} %get-tuple-element.288.refs_0_), channel_id=1, source_target_pairs={{0,1},{1,2},{2,3},{3,0},{4,5},{5,6},{6,7},{7,4},{8,9},{9,10},{10,1... | collective-permute-start | bytes 6291464 | tf_op jit(solution)/shard_map/ppermute | solution.py:830
  625.0 109.0 %reduce-scatter.7.cloned.1.call-start = ((), (), s32[]{:S(2)}) async-start(), calls=%async_computation.13 | async-start | bytes 7208960 | tf_op jit(solution)/shard_map/reduce_scatter | solution.py:847
  625.7 276.6 %reduce-scatter.11.cloned.1.call-start = ((), (), s32[]{:S(2)}) async-start(), calls=%async_computation.15 | async-start | bytes 3604480 | tf_op jit(solution)/shard_map/reduce_scatter | solution.py:847
  626.3 49.9 %collective-permute-start.14 = (bf16[1,512,2048]{2,1,0:T(8,128)(2,1)}, bf16[1,512,2048]{2,1,0:T(8,128)(2,1)}, u32[]{:S(2)}, u32[]{:S(2)}) collective-permute-start(bf16[1,512,2048]{2,1,0:T(8,128)(2,1)} %collective-permute-done.11.refs_0_.refs_1_), channel_id=1, source_target_pairs={{0,1},{1,2},{2,3},{3,0},{4,5},{5,6},{6,7},{7,4},{8,9},{9,10},{10,1... | collective-permute-start | bytes 6291464 | tf_op jit(solution)/shard_map/ppermute | solution.py:830
  676.2 226.1 %reduce-scatter.13.cloned.1.call-start = ((), (), s32[]{:S(2)}) async-start(), calls=%async_computation.16 | async-start | bytes 7208960 | tf_op jit(solution)/shard_map/reduce_scatter | solution.py:847
  677.0 280.7 %reduce-scatter.15.cloned.1.call-start = ((), (), s32[]{:S(2)}) async-start(), calls=%async_computation.17 | async-start | bytes 5242880 | tf_op jit(solution)/shard_map/reduce_scatter | solution.py:847
  677.0 48.9 %collective-permute-start.17 = (bf16[1,512,2048]{2,1,0:T(8,128)(2,1)}, bf16[1,512,2048]{2,1,0:T(8,128)(2,1)}, u32[]{:S(2)}, u32[]{:S(2)}) collective-permute-start(bf16[1,512,2048]{2,1,0:T(8,128)(2,1)} %collective-permute-done.14.refs_0_.refs_2_), channel_id=1, source_target_pairs={{0,1},{1,2},{2,3},{3,0},{4,5},{5,6},{6,7},{7,4},{8,9},{9,10},{10,1... | collective-permute-start | bytes 6291464 | tf_op jit(solution)/shard_map/ppermute | solution.py:830
  734.0 99.4 %collective-permute-start.18 = (bf16[1,512,2048]{2,1,0:T(8,128)(2,1)}, bf16[1,512,2048]{2,1,0:T(8,128)(2,1)S(1)}, u32[]{:S(2)}, u32[]{:S(2)}) collective-permute-start(bf16[1,512,2048]{2,1,0:T(8,128)(2,1)} %rows_matmul.39), channel_id=1, source_target_pairs={{0,1},{1,0},{2,3},{3,2},{4,5},{5,4},{6,7},{7,6},{8,9},{9,8},{10,11... | collective-permute-start | bytes 6291464 | tf_op jit(solution)/shard_map/ppermute | solution.py:830
  735.5 96.9 %collective-permute-start.19 = (bf16[256,2816]{1,0:T(8,128)(2,1)}, bf16[256,2816]{1,0:T(8,128)(2,1)S(1)}, u32[]{:S(2)}, u32[]{:S(2)}) collective-permute-start(bf16[256,2816]{1,0:T(8,128)(2,1)} %reduce-scatter.7.cloned.1.call-done), channel_id=1, source_target_pairs={{0,2},{1,3},{2,0},{3,1},{4,6},{5,7},{6,4},{7,5},{8,10},{9,11},{10,... | collective-permute-start | bytes 4325384 | tf_op jit(solution)/shard_map/ppermute | solution.py:833
  737.9 93.6 %collective-permute-start.20 = (bf16[256,1408]{1,0:T(8,128)(2,1)}, bf16[256,1408]{1,0:T(8,128)(2,1)S(1)}, u32[]{:S(2)}, u32[]{:S(2)}) collective-permute-start(bf16[256,1408]{1,0:T(8,128)(2,1)} %reduce-scatter.9.cloned.1.call-done), channel_id=1, source_target_pairs={{0,2},{1,3},{2,0},{3,1},{4,6},{5,7},{6,4},{7,5},{8,10},{9,11},{10,... | collective-permute-start | bytes 2162696 | tf_op jit(solution)/shard_map/ppermute | solution.py:833
  848.5 48.6 %collective-permute-start.21 = (bf16[1,512,2048]{2,1,0:T(8,128)(2,1)}, bf16[1,512,2048]{2,1,0:T(8,128)(2,1)}, u32[]{:S(2)}, u32[]{:S(2)}) collective-permute-start(bf16[1,512,2048]{2,1,0:T(8,128)(2,1)} %get-tuple-element.324), channel_id=1, source_target_pairs={{0,1},{1,2},{2,3},{3,0},{4,5},{5,6},{6,7},{7,4},{8,9},{9,10},{10,1... | collective-permute-start | bytes 6291464 | tf_op jit(solution)/shard_map/ppermute | solution.py:830
  897.0 140.4 %reduce-scatter.17.cloned.1.call-start = ((), (), s32[]{:S(2)}) async-start(), calls=%async_computation.18 | async-start | bytes 5570560 | tf_op jit(solution)/shard_map/reduce_scatter | solution.py:847
  902.3 55.3 %collective-permute-start.26 = (bf16[1,512,2048]{2,1,0:T(8,128)(2,1)}, bf16[1,512,2048]{2,1,0:T(8,128)(2,1)}, u32[]{:S(2)}, u32[]{:S(2)}) collective-permute-start(bf16[1,512,2048]{2,1,0:T(8,128)(2,1)} %add_convert_fusion.1), channel_id=1, source_target_pairs={{0,1},{1,2},{2,3},{3,0},{4,5},{5,6},{6,7},{7,4},{8,9},{9,10},{10,1... | collective-permute-start | bytes 6291464 | tf_op jit(solution)/shard_map/ppermute | solution.py:830
  962.3 49.8 %collective-permute-start.31 = (bf16[1,512,2048]{2,1,0:T(8,128)(2,1)}, bf16[1,512,2048]{2,1,0:T(8,128)(2,1)}, u32[]{:S(2)}, u32[]{:S(2)}) collective-permute-start(bf16[1,512,2048]{2,1,0:T(8,128)(2,1)} %add_convert_fusion), channel_id=1, source_target_pairs={{0,1},{1,2},{2,3},{3,0},{4,5},{5,6},{6,7},{7,4},{8,9},{9,10},{10,1... | collective-permute-start | bytes 6291464 | tf_op jit(solution)/shard_map/ppermute | solution.py:830
  (105 other events, 1575.5 us)
Sparse Core Ops, SparseCore 0:
  11.1 41.6 all-gather.7
  55.2 54.3 all-gather.9
  111.5 36.7 all-gather.11
  164.6 41.2 all-gather.15
  208.3 67.6 all-gather.13
  277.7 43.3 all-gather.19
  323.0 67.6 all-gather.17
  625.1 40.0 reduce-scatter.8
  668.2 65.8 reduce-scatter.6
  736.9 41.7 reduce-scatter.10
  781.7 65.8 reduce-scatter.12
  897.2 51.5 reduce-scatter.14
  966.9 56.1 reduce-scatter.16

commit v5 on v4

--- a/solution.py
+++ b/solution.py
@@ -601,12 +601,8 @@
     return 128 if units % 128 == 0 else 64
 
 
-def mlp_kernel(lanes, x, wgu, g, wd, hidden, grads):
-    mlp_finish(lanes, lax.dot_general(x[...], wgu[...], NN, preferred_element_type=F32), g, wd, hidden, grads)
-
-
-def mlp_finish(lanes, both, g, wd, hidden, grads):
-    back = lax.dot_general(g[...], wd[...], NN, preferred_element_type=F32)
+def mlp_kernel(lanes, x, wgu, back, hidden, grads):
+    both = lax.dot_general(x[...], wgu[...], NN, preferred_element_type=F32)
     for at in range(0, UNITS, lanes):
         first, second = 2 * at, 2 * at + lanes
         gate = both[:, first : first + lanes]
@@ -620,21 +616,18 @@
         grads[:, second : second + lanes] = (own * act).astype(BF)
 
 
-def mlp_block(g, wd, x=None, wgu=None, both=None):
-    piece, width = g.shape
-    units = wd.shape[1]
-    whole = pl.BlockSpec((piece, width), lambda n: (0, 0))
+def mlp_block(x, wgu, back):
+    piece, width = x.shape
+    units = back.shape[1]
     part = lambda depth, size: pl.BlockSpec((depth, size), lambda n: (0, n))
-    if both is None:
-        kernel, args = mlp_kernel, (x, wgu, g, wd)
-        specs = [whole, part(width, 2 * UNITS), whole, part(width, UNITS)]
-    else:
-        kernel, args = mlp_finish, (both, g, wd)
-        specs = [part(piece, 2 * UNITS), whole, part(width, UNITS)]
     return pl.pallas_call(
-        functools.partial(kernel, lanes_of(units)),
+        functools.partial(mlp_kernel, lanes_of(units)),
         grid=(pl.cdiv(units, UNITS),),
-        in_specs=specs,
+        in_specs=[
+            pl.BlockSpec((piece, width), lambda n: (0, 0)),
+            part(width, 2 * UNITS),
+            part(piece, UNITS),
+        ],
         out_specs=[part(piece, UNITS), part(piece, 2 * UNITS)],
         out_shape=[
             jax.ShapeDtypeStruct((piece, units), BF),
@@ -645,7 +638,7 @@
         ),
         cost_estimate=FREE,
         name="mlp_block",
-    )(*args)
+    )(x, wgu, back)
 
 
 NORM_ROWS = 128
@@ -771,7 +764,8 @@
     return lax.dot_general(a, b, NN, preferred_element_type=F32)
 
 
-def sum_over(x, axis, size, bit=1):
+def sum_over(x, axis, size):
+    bit = 1
     while bit < size:
         x = x + lax.ppermute(x, axis, swap(size, bit))
         bit = bit * 2
@@ -849,6 +843,7 @@
         )
 
     normed = by_rows(enter_kernel, at, [tokens], gain_attn, [BF])[0]
+    normed, w_query = tie(normed, w_query)
     small_pad = jnp.zeros((w_decay.shape[0], 128 - 2 * heads), BF)
     w_qks = gather_weight(jnp.concatenate([w_query, w_key, w_decay, w_beta, small_pad], axis=1))
     w_vg = gather_weight(jnp.concatenate([w_value, w_gate_out], axis=1))
@@ -909,14 +904,27 @@
             [(mixed, wo_full)], piece, nt=True, take=owner(s), dtype=dtype, limit=limit
         )
 
+    def back_parts(b):
+        return [
+            rows_matmul([(g, wdown_full[b])], piece, tile=768, dtype=F32, limit=VMEM_LIMIT)
+            for g in grad_out
+        ]
+
+    back = [None, None]
     total = attn_part(1, BF, WIDE_LIMIT)
     for s in range(2, size + 1):
         moved = step(total, size)
         own = attn_part(s % size)
-        moved, own = tie(moved, own)
+        if s == size - 1:
+            moved, own, wgu_full[0], *back[0] = tie(moved, own, wgu_full[0], *back_parts(0))
+        elif s == size:
+            moved, own, *back[1] = tie(moved, own, *back_parts(1))
+        else:
+            moved, own = tie(moved, own)
         total = (own + moved.astype(F32)).astype(BF)
     middle, normed_two = by_rows(middle_kernel, at, [own, moved, tokens], gain_mlp, [F32, BF])
     flat2 = lambda x: x.reshape(flat_piece, width)
+    flat_units = lambda x: x.reshape(flat_piece, x.shape[2])
     second = [normed_two]
     hidden, grad_gu = [[], []], [[], []]
 
@@ -932,12 +940,12 @@
         pairs = [(grad_gu[b][s], wgu_full[b]) for b in range(2)]
         return rows_matmul(pairs, piece, nt=True, dtype=dtype)
 
-    send, own_x, own_g = tie(normed_two, normed_two, grad_out[0])
+    send, own_x = tie(normed_two, normed_two)
     for s in range(1, group):
         moved = step(send, group)
         if s == 1:
             for b in range(2):
-                keep_block(b, mlp_block(flat2(own_g), wdown_full[b], flat2(own_x), wgu_full[b]))
+                keep_block(b, mlp_block(flat2(own_x), wgu_full[b], flat_units(back[b][0])))
             own_two = two_part(0)
             moved, own_two, *held = tie(moved, own_two, *hidden[0], *hidden[1], *grad_gu[0], *grad_gu[1])
             hidden, grad_gu = [held[:1], held[1:2]], [held[2:3], held[3:]]
@@ -945,9 +953,7 @@
         send = moved
     for s in range(1, group):
         for b in range(2):
-            keep_block(
-                b, mlp_block(flat2(grad_out[s]), wdown_full[b], flat2(second[s]), wgu_full[b])
-            )
+            keep_block(b, mlp_block(flat2(second[s]), wgu_full[b], flat_units(back[b][s])))
     first = [0] * group
     units = hidden[0][0].shape[2]
 
@@ -1097,13 +1103,20 @@
 
     taps_width = 2 * key_width + value_width
     own_width = taps_width + 128
-    spread = lax.dynamic_update_slice_in_dim(
-        jnp.zeros((4, size * own_width), F32), small[:, :own_width], me * own_width, 1
-    )
-    small = jnp.concatenate([spread, small[:, own_width:]], axis=1)
-    crossed, tokens_grad = tie(lax.ppermute(small, "head", swap(size, 1)), tokens_grad)
-    small = sum_over(small + crossed, "head", size, 2)
-    by_head = [small[:, i * own_width : (i + 1) * own_width] for i in range(size)]
+    spread, line = small[:, :own_width], small[0:1, own_width:]
+    bit = 1
+    while bit < size:
+        above = (me // bit) % 2 == 1
+        crossed = lax.ppermute(spread, "head", swap(size, bit))
+        line_crossed = lax.ppermute(line, "head", swap(size, bit))
+        if bit == 1:
+            crossed, line_crossed, tokens_grad = tie(crossed, line_crossed, tokens_grad)
+        low = jnp.where(above, crossed, spread)
+        high = jnp.where(above, spread, crossed)
+        spread = jnp.concatenate([low, high], axis=1)
+        line = line + line_crossed
+        bit = bit * 2
+    by_head = [spread[:, i * own_width : (i + 1) * own_width] for i in range(size)]
     taps = lambda start, stop: jnp.concatenate([x[:, start:stop] for x in by_head], axis=1)
     conv_sums = (
         taps(0, key_width),
@@ -1113,7 +1126,7 @@
     decay_sums = [
         jnp.concatenate([x[i, taps_width : taps_width + heads] for x in by_head]) for i in range(2)
     ]
-    gains = small[0, size * own_width :]
+    gains = line[0]
     gain_head_out = gains[:DV]
     gain_mlp_out = gains[DV : DV + width]
     gain_attn_out = gains[DV + width :] / gain_attn

time: 1060 us -> 1040 us (0.981)
  waiting for transfers between devices: 266 us -> 203 us
  Pallas kernels: 621 us -> 654 us
    ppermute x16, waiting for transfers between devices: 208 us -> 152 us  [step(): return lax.ppermute(x, 'head', ring(size, group))]
    pallas_call x24 -> x28, Pallas kernels: 240 us -> 278 us  [rows_matmul(): pl.pallas_call(functools.partial(rows_kernel, len(pairs), nt, weigh is no...]
    pallas_call x4, Pallas kernels: 63.6 us -> 52 us  [mlp_block(): pl.pallas_call(functools.partial(mlp_kernel, lanes_of(units)), grid=(pl.c...]
    unnamed x205 -> x213, local copies, waits for them, and re-layouts: 84.4 us -> 79.8 us
  transfers between devices with their start and end apart: 50 -> 52, of which waited for: 17 -> 18; matrix products, arithmetic and copies ran while one was open for 5% -> 6% of each run, Pallas kernels for 53% -> 58%
where the time goes in v5:
time: 1040 us; the launch traced here: 1020 us
  Pallas kernels  654 us (63%)
  waiting for transfers between devices  203 us (20%)
  local copies, waits for them, and re-layouts  90.4 us (9%)
  other arithmetic  34.7 us (3%)
  starting transfers between devices  27.2 us (3%)
  between operations  15.6 us (2%)
    pallas_call x28, Pallas kernels, rows_matmul(): pl.pallas_call(functools.partial(rows_kernel, len(pairs), nt, weigh is no...  278 us
    pallas_call x16, Pallas kernels, outer_sum(): pl.pallas_call(functools.partial(outer_kernel, len(xs), data // 2, [len(x...  162 us
    ppermute x16, waiting for transfers between devices, step(): return lax.ppermute(x, 'head', ring(size, group))  152 us
    pallas_call x1, Pallas kernels, mixer_backward(): pl.pallas_call(functools.partial(mixer_backward_kernel, heads), grid=(row...  86 us
    unnamed x213, local copies, waits for them, and re-layouts  79.8 us
    pallas_call x4, Pallas kernels, mlp_block(): pl.pallas_call(functools.partial(mlp_kernel, lanes_of(units)), grid=(pl.c...  52 us
    pallas_call x1, Pallas kernels, mixer_forward(): pl.pallas_call(functools.partial(mixer_forward_kernel, heads), grid=(rows...  45.7 us
    pallas_call x5, Pallas kernels, by_rows(): pl.pallas_call(kernel, grid_spec=pltpu.PrefetchScalarGridSpec(num_scalar_...  27.5 us
  transfers between devices with their start and end apart: 52, of which 18 were waited for; matrix products, arithmetic and copies ran while one was open for 6% of the time, Pallas kernels for 58%

profile of v5, /device:TPU:0, one launch (start us, length us, event | category | flops | bytes accessed | tf_op | source)
XLA Modules:
  0.0 1024.9 jit_solution(14624494930299393297)
XLA Ops:
  45.3 21.1 %collective-permute-done.refs_0_.refs_4_.refs_1_ = bf16[1,512,2048]{2,1,0:T(8,128)(2,1)} collective-permute-done((bf16[1,512,2048]{2,1,0:T(8,128)(2,1)S(1)}, bf16[1,512,2048]{2,1,0:T(8,128)(2,1)}, u32[]{:S(2)}, u32[]{:S(2)}) %collective-permute-start) | collective-permute-done | bytes 2097184 | tf_op jit(solution)/shard_map/ppermute | solution.py:824
  83.6 31.8 %collective-permute-done.1.refs_0_.refs_4_.refs_2_ = bf16[1,512,2048]{2,1,0:T(8,128)(2,1)} collective-permute-done((bf16[1,512,2048]{2,1,0:T(8,128)(2,1)}, bf16[1,512,2048]{2,1,0:T(8,128)(2,1)}, u32[]{:S(2)}, u32[]{:S(2)}) %collective-permute-start.1) | collective-permute-done | bytes 2097184 | tf_op jit(solution)/shard_map/ppermute | solution.py:824
  133.8 10.5 %rows_matmul.32.refs_2_ = f32[1,2048,2048]{2,1,0:T(8,128)} custom-call(s32[2]{0:T(128)} %pad_add_fusion.6.at, bf16[1,512,2048]{2,1,0:T(8,128)(2,1)} %collective-permute-done.refs_0_.refs_4_.refs_1_, bf16[2048,2048]{1,0:T(8,128)(2,1)} %all-gather.10.cloned.1.call-done.refs_1_.refs_3_, ...), custom_call_target="tpu_custom_call", output_to_operand_aliasing={{}: (3, {})} | custom-call | tf_op jit(solution)/shard_map/rows_matmul/pallas_call | solution.py:509
  144.3 10.0 rows_matmul.33.refs_2_
  189.1 45.7 %mixer_forward.1 = (bf16[1,2048,1024]{2,1,0:T(8,128)(2,1)S(1)}, bf16[1,16,4,128,128]{4,3,2,1,0:T(8,128)(2,1)S(1)}, bf16[1,16,4,128,256]{4,3,2,1,0:T(8,128)(2,1)S(1)}, bf16[1,2048,1024]{2,1,0:T(8,128)(2,1)}) custom-call(f32[1,2048,1152]{2,1,0:T(8,128)} %rows_matmul.34.pq.pk.ps.tq.tk, f32[1,2048,1152]{2,1,0:T(8,128)} %rows_matmul.34.pq.pk.ps.tq.tk, ...), custom_call_target="tpu_custom_call" | custom-call | bytes 192500000 | tf_op jit(solution)/shard_map/mixer_forward/pallas_call | solution.py:372
  240.2 18.4 %collective-permute-done.4 = bf16[256,1408]{1,0:T(8,128)(2,1)} collective-permute-done((bf16[256,1408]{1,0:T(8,128)(2,1)S(1)}, bf16[256,1408]{1,0:T(8,128)(2,1)}, u32[]{:S(2)}, u32[]{:S(2)}) %collective-permute-start.4) | collective-permute-done | bytes 720928 | tf_op jit(solution)/shard_map/ppermute | solution.py:827
  267.4 17.4 %rows_matmul.37 = f32[1,512,2048]{2,1,0:T(8,128)S(1)} custom-call(s32[2]{0:T(128)S(1)} %pad_add_fusion.2.at, bf16[1,2048,1024]{2,1,0:T(8,128)(2,1)S(1)} %copy-done.3, bf16[2048,1024]{1,0:T(8,128)(2,1)} %all-gather.12.cloned.1.call-done.refs_1_), custom_call_target="tpu_custom_call" | custom-call | tf_op jit(solution)/shard_map/rows_matmul/pallas_call | solution.py:509
  284.8 26.2 %collective-permute-done.6 = bf16[1,512,2048]{2,1,0:T(8,128)(2,1)S(1)} collective-permute-done((bf16[1,512,2048]{2,1,0:T(8,128)(2,1)}, bf16[1,512,2048]{2,1,0:T(8,128)(2,1)S(1)}, u32[]{:S(2)}, u32[]{:S(2)}) %collective-permute-start.6) | collective-permute-done | bytes 2097184 | tf_op jit(solution)/shard_map/ppermute | solution.py:824
  337.7 16.5 %collective-permute-done.7 = bf16[1,512,2048]{2,1,0:T(8,128)(2,1)} collective-permute-done((bf16[1,512,2048]{2,1,0:T(8,128)(2,1)}, bf16[1,512,2048]{2,1,0:T(8,128)(2,1)}, u32[]{:S(2)}, u32[]{:S(2)}) %collective-permute-start.7) | collective-permute-done | bytes 2097184 | tf_op jit(solution)/shard_map/ppermute | solution.py:824
  385.7 13.9 %collective-permute-done.8.moved = bf16[1,512,2048]{2,1,0:T(8,128)(2,1)} collective-permute-done((bf16[1,512,2048]{2,1,0:T(8,128)(2,1)}, bf16[1,512,2048]{2,1,0:T(8,128)(2,1)}, u32[]{:S(2)}, u32[]{:S(2)}) %collective-permute-start.8) | collective-permute-done | bytes 2097184 | tf_op jit(solution)/shard_map/ppermute | solution.py:824
  406.9 13.0 %mlp_block.4 = (bf16[512,1408]{1,0:T(8,128)(2,1)}, bf16[512,2816]{1,0:T(8,128)(2,1)}) custom-call(bf16[512,2048]{1,0:T(8,128)(2,1)} %bitcast.11.x, bf16[2048,2816]{1,0:T(8,128)(2,1)} %all-gather.14.cloned.1.call-done.wgu.refs_1_, f32[512,1408]{1,0:T(8,128)} %bitcast.75), custom_call_target="tpu_custom_call" | custom-call | tf_op jit(solution)/shard_map/mlp_block/pallas_call | solution.py:623
  419.9 13.0 %mlp_block.5 = (bf16[512,1408]{1,0:T(8,128)(2,1)}, bf16[512,2816]{1,0:T(8,128)(2,1)}) custom-call(bf16[512,2048]{1,0:T(8,128)(2,1)} %bitcast.11.x, bf16[2048,2816]{1,0:T(8,128)(2,1)} %all-gather.20.cloned.1.call-done.wgu.refs_3_, f32[512,1408]{1,0:T(8,128)} %bitcast.77), custom_call_target="tpu_custom_call" | custom-call | tf_op jit(solution)/shard_map/mlp_block/pallas_call | solution.py:623
  432.9 18.9 %rows_matmul.44.own = f32[1,512,2048]{2,1,0:T(8,128)} custom-call(s32[2]{0:T(128)} %copy-done.66, bf16[1,512,2816]{2,1,0:T(8,128)(2,1)} %bitcast.50, bf16[2048,2816]{1,0:T(8,128)(2,1)} %all-gather.14.cloned.1.call-done.wgu.refs_1_, bf16[1,512,2816]{2,1,0:T(8,128)(2,1)} %bitcast.56, bf16[2048,2816]{1,0:T(8,128)(2,1)} %all-gather.20.cloned.1.call-done.wgu.refs_3_), custom_call_target="tpu_custom_call" | custom-call | tf_op jit(solution)/shard_map/rows_matmul/pallas_call | solution.py:509
  451.7 13.0 %mlp_block.6 = (bf16[512,1408]{1,0:T(8,128)(2,1)}, bf16[512,2816]{1,0:T(8,128)(2,1)}) custom-call(bf16[512,2048]{1,0:T(8,128)(2,1)} %bitcast.18.x, bf16[2048,2816]{1,0:T(8,128)(2,1)} %all-gather.14.cloned.1.call-done.wgu.refs_1_, f32[512,1408]{1,0:T(8,128)} %bitcast.74), custom_call_target="tpu_custom_call" | custom-call | tf_op jit(solution)/shard_map/mlp_block/pallas_call | solution.py:623
  464.7 13.1 %mlp_block.7 = (bf16[512,1408]{1,0:T(8,128)(2,1)}, bf16[512,2816]{1,0:T(8,128)(2,1)}) custom-call(bf16[512,2048]{1,0:T(8,128)(2,1)} %bitcast.18.x, bf16[2048,2816]{1,0:T(8,128)(2,1)} %all-gather.20.cloned.1.call-done.wgu.refs_3_, f32[512,1408]{1,0:T(8,128)} %bitcast.76), custom_call_target="tpu_custom_call" | custom-call | tf_op jit(solution)/shard_map/mlp_block/pallas_call | solution.py:623
  477.8 19.1 %rows_matmul.45 = bf16[1,512,2048]{2,1,0:T(8,128)(2,1)} custom-call(s32[2]{0:T(128)} %copy-done.66, bf16[1,512,2816]{2,1,0:T(8,128)(2,1)} %bitcast.53, bf16[2048,2816]{1,0:T(8,128)(2,1)} %all-gather.14.cloned.1.call-done.wgu.refs_1_, bf16[1,512,2816]{2,1,0:T(8,128)(2,1)} %bitcast.59, bf16[2048,2816]{1,0:T(8,128)(2,1)} %all-gather.20.cloned.1.call-done.wgu.refs_3_), custom_call_target="tpu_custom_call" | custom-call | tf_op jit(solution)/shard_map/rows_matmul/pallas_call | solution.py:509
  509.1 12.2 %outer_sum.16 = bf16[1024,2816]{1,0:T(8,128)(2,1)} custom-call(s32[3]{0:T(128)S(1)} %stack.57.at, bf16[1,512,2048]{2,1,0:T(8,128)(2,1)} %get-tuple-element.268.refs_0_, bf16[1,512,2048]{2,1,0:T(8,128)(2,1)} %collective-permute-done.9.refs_1_, bf16[1,512,2816]{2,1,0:T(8,128)(2,1)S(1)} %bitcast.57, bf16[1,512,2816]{2,1,0:T(8,128)(2,1)S(1)} %bitcast.60), custom_call_target="tpu_custom_call" | custom-call | tf_op jit(solution)/shard_map/outer_sum/pallas_call | solution.py:579
  521.3 11.7 %rows_matmul.47 = bf16[1,512,2048]{2,1,0:T(8,128)(2,1)} custom-call(s32[2]{0:T(128)} %copy-done.66, bf16[1,512,1408]{2,1,0:T(8,128)(2,1)} %bitcast.62, bf16[2048,1408]{1,0:T(8,128)(2,1)} %all-gather.16.cloned.1.call-done.refs_1_, bf16[1,512,1408]{2,1,0:T(8,128)(2,1)} %bitcast.65, bf16[2048,1408]{1,0:T(8,128)(2,1)} %all-gather.18.cloned.1.call-done.refs_1_.refs_3_), custom_call_target="tpu_custom_call" | custom-call | tf_op jit(solution)/shard_map/rows_matmul/pallas_call | solution.py:509
  533.0 12.1 %rows_matmul.46.own = f32[1,512,2048]{2,1,0:T(8,128)} custom-call(s32[2]{0:T(128)} %copy-done.66, bf16[1,512,1408]{2,1,0:T(8,128)(2,1)} %bitcast.68, bf16[2048,1408]{1,0:T(8,128)(2,1)} %all-gather.16.cloned.1.call-done.refs_1_, bf16[1,512,1408]{2,1,0:T(8,128)(2,1)} %bitcast.71, bf16[2048,1408]{1,0:T(8,128)(2,1)} %all-gather.18.cloned.1.call-done.refs_1_.refs_3_), custom_call_target="tpu_custom_call" | custom-call | tf_op jit(solution)/shard_map/rows_matmul/pallas_call | solution.py:509
  564.5 12.4 %outer_sum.20 = bf16[1024,2816]{1,0:T(8,128)(2,1)} custom-call(s32[3]{0:T(128)S(1)} %stack.57.at, bf16[1,512,2048]{2,1,0:T(8,128)(2,1)} %get-tuple-element.268.refs_0_, bf16[1,512,2048]{2,1,0:T(8,128)(2,1)} %collective-permute-done.9.refs_1_, bf16[1,512,2816]{2,1,0:T(8,128)(2,1)S(1)} %bitcast.51, bf16[1,512,2816]{2,1,0:T(8,128)(2,1)S(1)} %bitcast.54), custom_call_target="tpu_custom_call" | custom-call | tf_op jit(solution)/shard_map/outer_sum/pallas_call | solution.py:579
  588.5 13.2 %outer_sum.18 = bf16[1024,2816]{1,0:T(8,128)(2,1)} custom-call(s32[3]{0:T(128)S(1)} %stack.59.at, bf16[1,512,2048]{2,1,0:T(8,128)(2,1)} %get-tuple-element.268.refs_0_, bf16[1,512,2048]{2,1,0:T(8,128)(2,1)} %collective-permute-done.9.refs_1_, bf16[1,512,2816]{2,1,0:T(8,128)(2,1)S(1)} %bitcast.58, bf16[1,512,2816]{2,1,0:T(8,128)(2,1)S(1)} %bitcast.61, ...), custom_call_target="tpu_custom_call" | custom-call | tf_op jit(solution)/shard_map/outer_sum/pallas_call | solution.py:579
  606.8 12.7 %collective-permute-done.16.refs_4_ = bf16[1024,1408]{1,0:T(8,128)(2,1)S(1)} collective-permute-done((bf16[1024,1408]{1,0:T(8,128)(2,1)}, bf16[1024,1408]{1,0:T(8,128)(2,1)S(1)}, u32[]{:S(2)}, u32[]{:S(2)}) %collective-permute-start.16) | collective-permute-done | bytes 2883616 | tf_op jit(solution)/shard_map/ppermute | solution.py:833
  636.0 13.1 %outer_sum.22 = bf16[1024,2816]{1,0:T(8,128)(2,1)} custom-call(s32[3]{0:T(128)S(1)} %stack.59.at, bf16[1,512,2048]{2,1,0:T(8,128)(2,1)} %get-tuple-element.268.refs_0_, bf16[1,512,2048]{2,1,0:T(8,128)(2,1)} %collective-permute-done.9.refs_1_, bf16[1,512,2816]{2,1,0:T(8,128)(2,1)S(1)} %bitcast.52, bf16[1,512,2816]{2,1,0:T(8,128)(2,1)S(1)} %bitcast.55, ...), custom_call_target="tpu_custom_call" | custom-call | tf_op jit(solution)/shard_map/outer_sum/pallas_call | solution.py:579
  720.5 86.0 %mixer_backward.1 = (bf16[1,2048,1152]{2,1,0:T(8,128)(2,1)}, bf16[1,2048,2048]{2,1,0:T(8,128)(2,1)}, f32[8,512]{1,0:T(8,128)S(1)}, f32[8,512]{1,0:T(8,128)S(1)},...) custom-call(f32[1,2048,1024]{2,1,0:T(8,128)} %rows_matmul.51.dm, ...), custom_call_target="tpu_custom_call" | custom-call | bytes 315000000 | tf_op jit(solution)/shard_map/mixer_backward/pallas_call | solution.py:419
  815.2 13.6 %rows_matmul.52 = (bf16[1,512,2048]{2,1,0:T(8,128)(2,1)}, f32[1,8,2048]{2,1,0:T(8,128)}) custom-call(s32[2]{0:T(128)} %pad_add_fusion.3.at, bf16[1,2048,1152]{2,1,0:T(8,128)(2,1)} %get-tuple-element.380.refs_0_.refs_4_.refs_5_.refs_6_.refs_7_, bf16[2048,1152]{1,0:T(8,128)(2,1)} %all-gather.8.cloned.1.call-done.refs_1_, ...), custom_call_target="tpu_custom_call" | custom-call | tf_op jit(solution)/shard_map/rows_matmul/pallas_call | solution.py:509
  829.0 16.0 %outer_sum.26 = (bf16[256,2048]{1,0:T(8,128)(2,1)}, bf16[256,2048]{1,0:T(8,128)(2,1)}, bf16[256,2048]{1,0:T(8,128)(2,1)}, bf16[256,2048]{1,0:T(8,128)(2,1)}) custom-call(s32[5]{0:T(128)S(1)} %stack.63.at, bf16[1,512,2048]{2,1,0:T(8,128)(2,1)S(1)} %copy-done.8, bf16[1,512,2048]{2,1,0:T(8,128)(2,1)} %collective-permute-done.refs_0_.refs_4_.refs_1_, ...), custom_call_target="tpu_custom_call" | custom-call | tf_op jit(solution)/shard_map/outer_sum/pallas_call | solution.py:579
  846.1 13.5 %rows_matmul.53 = (bf16[1,512,2048]{2,1,0:T(8,128)(2,1)}, f32[1,8,2048]{2,1,0:T(8,128)}) custom-call(s32[2]{0:T(128)} %copy-done.75, bf16[1,2048,1152]{2,1,0:T(8,128)(2,1)} %get-tuple-element.380.refs_0_.refs_4_.refs_5_.refs_6_.refs_7_, bf16[2048,1152]{1,0:T(8,128)(2,1)} %all-gather.8.cloned.1.call-done.refs_1_, ...), custom_call_target="tpu_custom_call" | custom-call | tf_op jit(solution)/shard_map/rows_matmul/pallas_call | solution.py:509
  859.6 16.2 %outer_sum.27 = bf16[1024,2048]{1,0:T(8,128)(2,1)} custom-call(s32[5]{0:T(128)S(1)} %stack.62.at, bf16[1,512,2048]{2,1,0:T(8,128)(2,1)S(1)} %copy-done.8, bf16[1,512,2048]{2,1,0:T(8,128)(2,1)} %collective-permute-done.refs_0_.refs_4_.refs_1_, bf16[1,512,2048]{2,1,0:T(8,128)(2,1)} %collective-permute-done.1.refs_0_.refs_4_.refs_2_, ...), custom_call_target="tpu_custom_call" | custom-call | tf_op jit(solution)/shard_map/outer_sum/pallas_call | solution.py:579
  884.5 11.9 %outer_sum.28 = (bf16[512,1152]{1,0:T(8,128)(2,1)}, bf16[512,1152]{1,0:T(8,128)(2,1)}) custom-call(s32[5]{0:T(128)S(1)} %stack.63.at, bf16[1,512,2048]{2,1,0:T(8,128)(2,1)S(1)} %copy-done.9, bf16[1,512,2048]{2,1,0:T(8,128)(2,1)} %collective-permute-done.refs_0_.refs_4_.refs_1_, bf16[1,512,2048]{2,1,0:T(8,128)(2,1)} %collective-permute-done.1.refs_0_.refs_4_.refs_2_, ...), custom_call_target="tpu_custom_call" | custom-call | tf_op jit(solution)/shard_map/outer_sum/pallas_call | solution.py:579
  903.2 13.5 %rows_matmul.54 = (bf16[1,512,2048]{2,1,0:T(8,128)(2,1)}, f32[1,8,2048]{2,1,0:T(8,128)}) custom-call(s32[2]{0:T(128)} %copy-done.74, bf16[1,2048,1152]{2,1,0:T(8,128)(2,1)} %get-tuple-element.380.refs_0_.refs_4_.refs_5_.refs_6_.refs_7_, bf16[2048,1152]{1,0:T(8,128)(2,1)} %all-gather.8.cloned.1.call-done.refs_1_, ...), custom_call_target="tpu_custom_call" | custom-call | tf_op jit(solution)/shard_map/rows_matmul/pallas_call | solution.py:509
  924.0 11.8 %outer_sum.29 = bf16[1024,1152]{1,0:T(8,128)(2,1)} custom-call(s32[5]{0:T(128)S(1)} %stack.62.at, bf16[1,512,2048]{2,1,0:T(8,128)(2,1)S(1)} %copy-done.10, bf16[1,512,2048]{2,1,0:T(8,128)(2,1)} %collective-permute-done.refs_0_.refs_4_.refs_1_, bf16[1,512,2048]{2,1,0:T(8,128)(2,1)} %collective-permute-done.1.refs_0_.refs_4_.refs_2_, ...), custom_call_target="tpu_custom_call" | custom-call | tf_op jit(solution)/shard_map/outer_sum/pallas_call | solution.py:579
  945.1 14.3 %rows_matmul.55 = (f32[1,512,2048]{2,1,0:T(8,128)}, f32[1,8,2048]{2,1,0:T(8,128)}) custom-call(s32[2]{0:T(128)} %copy-done.73, bf16[1,2048,1152]{2,1,0:T(8,128)(2,1)} %get-tuple-element.380.refs_0_.refs_4_.refs_5_.refs_6_.refs_7_, bf16[2048,1152]{1,0:T(8,128)(2,1)} %all-gather.8.cloned.1.call-done.refs_1_, ...), custom_call_target="tpu_custom_call" | custom-call | tf_op jit(solution)/shard_map/rows_matmul/pallas_call | solution.py:509
  (418 shorter events, 423.4 us)
Async XLA Ops:
  7.2 60.4 %all-gather.8.cloned.1.call-start = ((), (), s32[]{:S(2)}) async-start(), calls=%async_computation.6 | async-start | bytes 5308416 | tf_op jit(solution)/shard_map/all_gather | solution.py:830
  13.3 110.6 %all-gather.10.cloned.1.call-start = ((), (), s32[]{:S(2)}) async-start(), calls=%async_computation.7 | async-start | bytes 9437184 | tf_op jit(solution)/shard_map/all_gather | solution.py:830
  15.6 244.4 %all-gather.12.cloned.1.call-start = ((), (), s32[]{:S(2)}) async-start(), calls=%async_computation.8 | async-start | bytes 4718592 | tf_op jit(solution)/shard_map/all_gather | solution.py:830
  15.6 50.8 %collective-permute-start = (bf16[1,512,2048]{2,1,0:T(8,128)(2,1)S(1)}, bf16[1,512,2048]{2,1,0:T(8,128)(2,1)}, u32[]{:S(2)}, u32[]{:S(2)}) collective-permute-start(bf16[1,512,2048]{2,1,0:T(8,128)(2,1)S(1)} %enter_kernel.1.refs_0_.refs_4_), channel_id=1, source_target_pairs={{0,1},{1,2},{2,3},{3,0},{4,5},{5,6},{6,7},{7,4},{8,9},{9,10},{10,1... | collective-permute-start | bytes 6291464 | tf_op jit(solution)/shard_map/ppermute | solution.py:824
  18.7 302.1 %all-gather.16.cloned.1.call-start = ((), (), s32[]{:S(2)}) async-start(), calls=%async_computation.10 | async-start | bytes 6488064 | tf_op jit(solution)/shard_map/all_gather | solution.py:830
  66.5 48.9 %collective-permute-start.1 = (bf16[1,512,2048]{2,1,0:T(8,128)(2,1)}, bf16[1,512,2048]{2,1,0:T(8,128)(2,1)}, u32[]{:S(2)}, u32[]{:S(2)}) collective-permute-start(bf16[1,512,2048]{2,1,0:T(8,128)(2,1)} %collective-permute-done.refs_0_.refs_4_.refs_1_), channel_id=1, source_target_pairs={{0,1},{1,2},{2,3},{3,0},{4,5},{5,6},{6,7},{7,4},{8,9},{9,10},{10,1... | collective-permute-start | bytes 6291464 | tf_op jit(solution)/shard_map/ppermute | solution.py:824
  115.4 48.9 %collective-permute-start.2 = (bf16[1,512,2048]{2,1,0:T(8,128)(2,1)}, bf16[1,512,2048]{2,1,0:T(8,128)(2,1)}, u32[]{:S(2)}, u32[]{:S(2)}) collective-permute-start(bf16[1,512,2048]{2,1,0:T(8,128)(2,1)} %collective-permute-done.1.refs_0_.refs_4_.refs_2_), channel_id=1, source_target_pairs={{0,1},{1,2},{2,3},{3,0},{4,5},{5,6},{6,7},{7,4},{8,9},{9,10},{10,1... | collective-permute-start | bytes 6291464 | tf_op jit(solution)/shard_map/ppermute | solution.py:824
  164.3 189.9 %all-gather.14.cloned.1.call-start = ((), (), s32[]{:S(2)}) async-start(), calls=%async_computation.9 | async-start | bytes 12976128 | tf_op jit(solution)/shard_map/all_gather | solution.py:830
  164.9 204.0 %all-gather.18.cloned.1.call-start = ((), (), s32[]{:S(2)}) async-start(), calls=%async_computation.11 | async-start | bytes 6488064 | tf_op jit(solution)/shard_map/all_gather | solution.py:830
  165.3 93.3 %collective-permute-start.5 = (bf16[1,512,2048]{2,1,0:T(8,128)(2,1)S(1)}, bf16[1,512,2048]{2,1,0:T(8,128)(2,1)}, u32[]{:S(2)}, u32[]{:S(2)}) collective-permute-start(bf16[1,512,2048]{2,1,0:T(8,128)(2,1)S(1)} %copy-done.11), channel_id=1, source_target_pairs={{0,1},{1,0},{2,3},{3,2},{4,5},{5,4},{6,7},{7,6},{8,9},{9,8},{10,11... | collective-permute-start | bytes 6291464 | tf_op jit(solution)/shard_map/ppermute | solution.py:824
  165.4 93.2 %collective-permute-start.3 = (bf16[256,2816]{1,0:T(8,128)(2,1)}, bf16[256,2816]{1,0:T(8,128)(2,1)}, u32[]{:S(2)}, u32[]{:S(2)}) collective-permute-start(bf16[256,2816]{1,0:T(8,128)(2,1)} %slice_dynamic-update-slice_fusion), channel_id=1, source_target_pairs={{0,2},{1,3},{2,0},{3,1},{4,6},{5,7},{6,4},{7,5},{8,10},{9,11},{10,... | collective-permute-start | bytes 4325384 | tf_op jit(solution)/shard_map/ppermute | solution.py:827
  165.5 93.1 %collective-permute-start.4 = (bf16[256,1408]{1,0:T(8,128)(2,1)S(1)}, bf16[256,1408]{1,0:T(8,128)(2,1)}, u32[]{:S(2)}, u32[]{:S(2)}) collective-permute-start(bf16[256,1408]{1,0:T(8,128)(2,1)S(1)} %copy-done.82), channel_id=1, source_target_pairs={{0,2},{1,3},{2,0},{3,1},{4,6},{5,7},{6,4},{7,5},{8,10},{9,11},{10,... | collective-permute-start | bytes 2162696 | tf_op jit(solution)/shard_map/ppermute | solution.py:827
  258.6 161.3 %all-gather.20.cloned.1.call-start = ((), (), s32[]{:S(2)}) async-start(), calls=%async_computation.12 | async-start | bytes 12976128 | tf_op jit(solution)/shard_map/all_gather | solution.py:830
  259.4 452.8 %reduce-scatter.9.cloned.1.call-start = ((), (), s32[]{:S(2)}) async-start(), calls=%async_computation.14 | async-start | bytes 3604480 | tf_op jit(solution)/shard_map/reduce_scatter | solution.py:841
  267.3 43.7 %collective-permute-start.6 = (bf16[1,512,2048]{2,1,0:T(8,128)(2,1)}, bf16[1,512,2048]{2,1,0:T(8,128)(2,1)S(1)}, u32[]{:S(2)}, u32[]{:S(2)}) collective-permute-start(bf16[1,512,2048]{2,1,0:T(8,128)(2,1)} %rows_matmul.36), channel_id=1, source_target_pairs={{0,1},{1,2},{2,3},{3,0},{4,5},{5,6},{6,7},{7,4},{8,9},{9,10},{10,1... | collective-permute-start | bytes 6291464 | tf_op jit(solution)/shard_map/ppermute | solution.py:824
  313.0 41.2 %collective-permute-start.7 = (bf16[1,512,2048]{2,1,0:T(8,128)(2,1)}, bf16[1,512,2048]{2,1,0:T(8,128)(2,1)}, u32[]{:S(2)}, u32[]{:S(2)}) collective-permute-start(bf16[1,512,2048]{2,1,0:T(8,128)(2,1)} %add_convert_fusion.3), channel_id=1, source_target_pairs={{0,1},{1,2},{2,3},{3,0},{4,5},{5,6},{6,7},{7,4},{8,9},{9,10},{10,1... | collective-permute-start | bytes 6291464 | tf_op jit(solution)/shard_map/ppermute | solution.py:824
  406.9 44.8 %collective-permute-start.9 = (bf16[1,512,2048]{2,1,0:T(8,128)(2,1)}, bf16[1,512,2048]{2,1,0:T(8,128)(2,1)}, u32[]{:S(2)}, u32[]{:S(2)}) collective-permute-start(bf16[1,512,2048]{2,1,0:T(8,128)(2,1)} %get-tuple-element.268.refs_0_), channel_id=1, source_target_pairs={{0,1},{1,0},{2,3},{3,2},{4,5},{5,4},{6,7},{7,6},{8,9},{9,8},{10,11... | collective-permute-start | bytes 6291464 | tf_op jit(solution)/shard_map/ppermute | solution.py:824
  496.9 48.3 %collective-permute-start.10 = (bf16[1,512,2048]{2,1,0:T(8,128)(2,1)}, bf16[1,512,2048]{2,1,0:T(8,128)(2,1)}, u32[]{:S(2)}, u32[]{:S(2)}) collective-permute-start(bf16[1,512,2048]{2,1,0:T(8,128)(2,1)} %rows_matmul.45), channel_id=1, source_target_pairs={{0,1},{1,0},{2,3},{3,2},{4,5},{5,4},{6,7},{7,6},{8,9},{9,8},{10,11... | collective-permute-start | bytes 6291464 | tf_op jit(solution)/shard_map/ppermute | solution.py:824
  555.5 49.7 %collective-permute-start.11 = (bf16[1,512,2048]{2,1,0:T(8,128)(2,1)}, bf16[1,512,2048]{2,1,0:T(8,128)(2,1)}, u32[]{:S(2)}, u32[]{:S(2)}) collective-permute-start(bf16[1,512,2048]{2,1,0:T(8,128)(2,1)} %get-tuple-element.301.refs_0_), channel_id=1, source_target_pairs={{0,1},{1,2},{2,3},{3,0},{4,5},{5,6},{6,7},{7,4},{8,9},{9,10},{10,1... | collective-permute-start | bytes 6291464 | tf_op jit(solution)/shard_map/ppermute | solution.py:824
  605.3 109.2 %reduce-scatter.7.cloned.1.call-start = ((), (), s32[]{:S(2)}) async-start(), calls=%async_computation.13 | async-start | bytes 7208960 | tf_op jit(solution)/shard_map/reduce_scatter | solution.py:841
  606.0 276.7 %reduce-scatter.11.cloned.1.call-start = ((), (), s32[]{:S(2)}) async-start(), calls=%async_computation.15 | async-start | bytes 3604480 | tf_op jit(solution)/shard_map/reduce_scatter | solution.py:841
  606.6 49.9 %collective-permute-start.14 = (bf16[1,512,2048]{2,1,0:T(8,128)(2,1)}, bf16[1,512,2048]{2,1,0:T(8,128)(2,1)}, u32[]{:S(2)}, u32[]{:S(2)}) collective-permute-start(bf16[1,512,2048]{2,1,0:T(8,128)(2,1)} %collective-permute-done.11.refs_0_.refs_1_), channel_id=1, source_target_pairs={{0,1},{1,2},{2,3},{3,0},{4,5},{5,6},{6,7},{7,4},{8,9},{9,10},{10,1... | collective-permute-start | bytes 6291464 | tf_op jit(solution)/shard_map/ppermute | solution.py:824
  656.6 226.1 %reduce-scatter.13.cloned.1.call-start = ((), (), s32[]{:S(2)}) async-start(), calls=%async_computation.16 | async-start | bytes 7208960 | tf_op jit(solution)/shard_map/reduce_scatter | solution.py:841
  657.3 278.5 %reduce-scatter.15.cloned.1.call-start = ((), (), s32[]{:S(2)}) async-start(), calls=%async_computation.17 | async-start | bytes 5242880 | tf_op jit(solution)/shard_map/reduce_scatter | solution.py:841
  657.4 48.9 %collective-permute-start.17 = (bf16[1,512,2048]{2,1,0:T(8,128)(2,1)}, bf16[1,512,2048]{2,1,0:T(8,128)(2,1)}, u32[]{:S(2)}, u32[]{:S(2)}) collective-permute-start(bf16[1,512,2048]{2,1,0:T(8,128)(2,1)} %collective-permute-done.14.refs_0_.refs_2_), channel_id=1, source_target_pairs={{0,1},{1,2},{2,3},{3,0},{4,5},{5,6},{6,7},{7,4},{8,9},{9,10},{10,1... | collective-permute-start | bytes 6291464 | tf_op jit(solution)/shard_map/ppermute | solution.py:824
  714.5 99.5 %collective-permute-start.18 = (bf16[1,512,2048]{2,1,0:T(8,128)(2,1)}, bf16[1,512,2048]{2,1,0:T(8,128)(2,1)S(1)}, u32[]{:S(2)}, u32[]{:S(2)}) collective-permute-start(bf16[1,512,2048]{2,1,0:T(8,128)(2,1)} %rows_matmul.47), channel_id=1, source_target_pairs={{0,1},{1,0},{2,3},{3,2},{4,5},{5,4},{6,7},{7,6},{8,9},{9,8},{10,11... | collective-permute-start | bytes 6291464 | tf_op jit(solution)/shard_map/ppermute | solution.py:824
  715.9 96.9 %collective-permute-start.19 = (bf16[256,2816]{1,0:T(8,128)(2,1)}, bf16[256,2816]{1,0:T(8,128)(2,1)S(1)}, u32[]{:S(2)}, u32[]{:S(2)}) collective-permute-start(bf16[256,2816]{1,0:T(8,128)(2,1)} %reduce-scatter.7.cloned.1.call-done), channel_id=1, source_target_pairs={{0,2},{1,3},{2,0},{3,1},{4,6},{5,7},{6,4},{7,5},{8,10},{9,11},{10,... | collective-permute-start | bytes 4325384 | tf_op jit(solution)/shard_map/ppermute | solution.py:827
  718.4 93.6 %collective-permute-start.20 = (bf16[256,1408]{1,0:T(8,128)(2,1)}, bf16[256,1408]{1,0:T(8,128)(2,1)S(1)}, u32[]{:S(2)}, u32[]{:S(2)}) collective-permute-start(bf16[256,1408]{1,0:T(8,128)(2,1)} %reduce-scatter.9.cloned.1.call-done), channel_id=1, source_target_pairs={{0,2},{1,3},{2,0},{3,1},{4,6},{5,7},{6,4},{7,5},{8,10},{9,11},{10,... | collective-permute-start | bytes 2162696 | tf_op jit(solution)/shard_map/ppermute | solution.py:827
  828.9 48.6 %collective-permute-start.21 = (bf16[1,512,2048]{2,1,0:T(8,128)(2,1)}, bf16[1,512,2048]{2,1,0:T(8,128)(2,1)}, u32[]{:S(2)}, u32[]{:S(2)}) collective-permute-start(bf16[1,512,2048]{2,1,0:T(8,128)(2,1)} %get-tuple-element.337), channel_id=1, source_target_pairs={{0,1},{1,2},{2,3},{3,0},{4,5},{5,6},{6,7},{7,4},{8,9},{9,10},{10,1... | collective-permute-start | bytes 6291464 | tf_op jit(solution)/shard_map/ppermute | solution.py:824
  877.4 135.0 %reduce-scatter.17.cloned.1.call-start = ((), (), s32[]{:S(2)}) async-start(), calls=%async_computation.18 | async-start | bytes 5570560 | tf_op jit(solution)/shard_map/reduce_scatter | solution.py:841
  882.7 53.1 %collective-permute-start.26 = (bf16[1,512,2048]{2,1,0:T(8,128)(2,1)}, bf16[1,512,2048]{2,1,0:T(8,128)(2,1)}, u32[]{:S(2)}, u32[]{:S(2)}) collective-permute-start(bf16[1,512,2048]{2,1,0:T(8,128)(2,1)} %add_convert_fusion.1), channel_id=1, source_target_pairs={{0,1},{1,2},{2,3},{3,0},{4,5},{5,6},{6,7},{7,4},{8,9},{9,10},{10,1... | collective-permute-start | bytes 6291464 | tf_op jit(solution)/shard_map/ppermute | solution.py:824
  940.5 49.9 %collective-permute-start.31 = (bf16[1,512,2048]{2,1,0:T(8,128)(2,1)}, bf16[1,512,2048]{2,1,0:T(8,128)(2,1)}, u32[]{:S(2)}, u32[]{:S(2)}) collective-permute-start(bf16[1,512,2048]{2,1,0:T(8,128)(2,1)} %add_convert_fusion), channel_id=1, source_target_pairs={{0,1},{1,2},{2,3},{3,0},{4,5},{5,6},{6,7},{7,4},{8,9},{9,10},{10,1... | collective-permute-start | bytes 6291464 | tf_op jit(solution)/shard_map/ppermute | solution.py:824
  (111 other events, 1601.6 us)
Sparse Core Ops, SparseCore 0:
  13.4 41.6 all-gather.7
  57.6 54.3 all-gather.9
  113.9 36.7 all-gather.11
  164.4 41.2 all-gather.15
  208.0 67.6 all-gather.13
  277.5 43.3 all-gather.17
  322.8 67.6 all-gather.19
  605.4 40.1 reduce-scatter.8
  648.6 65.8 reduce-scatter.6
  717.4 41.7 reduce-scatter.10
  762.1 65.8 reduce-scatter.12
  877.6 51.5 reduce-scatter.14
  945.1 56.5 reduce-scatter.16

commit v6 on v5

--- a/solution.py
+++ b/solution.py
@@ -594,7 +594,7 @@
     )(at, *args)
 
 
-UNITS = 256
+UNITS = 512
 
 
 def lanes_of(units):

time: 1040 us -> 1030 us (level)
  no operation moved by 1% of the time
where the time goes in v6:
time: 1030 us; the launch traced here: 1020 us
  Pallas kernels  652 us (63%)
  waiting for transfers between devices  203 us (20%)
  local copies, waits for them, and re-layouts  90.5 us (9%)
  other arithmetic  34.7 us (3%)
  starting transfers between devices  27.4 us (3%)
  between operations  15.6 us (2%)
    pallas_call x28, Pallas kernels, rows_matmul(): pl.pallas_call(functools.partial(rows_kernel, len(pairs), nt, weigh is no...  278 us
    pallas_call x16, Pallas kernels, outer_sum(): pl.pallas_call(functools.partial(outer_kernel, len(xs), data // 2, [len(x...  163 us
    ppermute x16, waiting for transfers between devices, step(): return lax.ppermute(x, 'head', ring(size, group))  152 us
    pallas_call x1, Pallas kernels, mixer_backward(): pl.pallas_call(functools.partial(mixer_backward_kernel, heads), grid=(row...  85.7 us
    unnamed x213, local copies, waits for them, and re-layouts  79.9 us
    pallas_call x4, Pallas kernels, mlp_block(): pl.pallas_call(functools.partial(mlp_kernel, lanes_of(units)), grid=(pl.c...  49.7 us
    pallas_call x1, Pallas kernels, mixer_forward(): pl.pallas_call(functools.partial(mixer_forward_kernel, heads), grid=(rows...  45.7 us
    pallas_call x5, Pallas kernels, by_rows(): pl.pallas_call(kernel, grid_spec=pltpu.PrefetchScalarGridSpec(num_scalar_...  27.7 us
  transfers between devices with their start and end apart: 52, of which 18 were waited for; matrix products, arithmetic and copies ran while one was open for 6% of the time, Pallas kernels for 58%

profile of v6, /device:TPU:0, one launch (start us, length us, event | category | flops | bytes accessed | tf_op | source)
XLA Modules:
  0.0 1022.4 jit_solution(16367857092687683462)
XLA Ops:
  45.3 21.1 %collective-permute-done.refs_0_.refs_4_.refs_1_ = bf16[1,512,2048]{2,1,0:T(8,128)(2,1)} collective-permute-done((bf16[1,512,2048]{2,1,0:T(8,128)(2,1)S(1)}, bf16[1,512,2048]{2,1,0:T(8,128)(2,1)}, u32[]{:S(2)}, u32[]{:S(2)}) %collective-permute-start) | collective-permute-done | bytes 2097184 | tf_op jit(solution)/shard_map/ppermute | solution.py:824
  83.6 31.8 %collective-permute-done.1.refs_0_.refs_4_.refs_2_ = bf16[1,512,2048]{2,1,0:T(8,128)(2,1)} collective-permute-done((bf16[1,512,2048]{2,1,0:T(8,128)(2,1)}, bf16[1,512,2048]{2,1,0:T(8,128)(2,1)}, u32[]{:S(2)}, u32[]{:S(2)}) %collective-permute-start.1) | collective-permute-done | bytes 2097184 | tf_op jit(solution)/shard_map/ppermute | solution.py:824
  133.8 10.5 %rows_matmul.32.refs_2_ = f32[1,2048,2048]{2,1,0:T(8,128)} custom-call(s32[2]{0:T(128)} %pad_add_fusion.6.at, bf16[1,512,2048]{2,1,0:T(8,128)(2,1)} %collective-permute-done.refs_0_.refs_4_.refs_1_, bf16[2048,2048]{1,0:T(8,128)(2,1)} %all-gather.10.cloned.1.call-done.refs_1_.refs_3_, ...), custom_call_target="tpu_custom_call", output_to_operand_aliasing={{}: (3, {})} | custom-call | tf_op jit(solution)/shard_map/rows_matmul/pallas_call | solution.py:509
  189.1 45.7 %mixer_forward.1 = (bf16[1,2048,1024]{2,1,0:T(8,128)(2,1)S(1)}, bf16[1,16,4,128,128]{4,3,2,1,0:T(8,128)(2,1)S(1)}, bf16[1,16,4,128,256]{4,3,2,1,0:T(8,128)(2,1)S(1)}, bf16[1,2048,1024]{2,1,0:T(8,128)(2,1)}) custom-call(f32[1,2048,1152]{2,1,0:T(8,128)} %rows_matmul.34.pq.pk.ps.tq.tk, f32[1,2048,1152]{2,1,0:T(8,128)} %rows_matmul.34.pq.pk.ps.tq.tk, ...), custom_call_target="tpu_custom_call" | custom-call | bytes 192500000 | tf_op jit(solution)/shard_map/mixer_forward/pallas_call | solution.py:372
  240.2 18.4 %collective-permute-done.4 = bf16[256,1408]{1,0:T(8,128)(2,1)} collective-permute-done((bf16[256,1408]{1,0:T(8,128)(2,1)S(1)}, bf16[256,1408]{1,0:T(8,128)(2,1)}, u32[]{:S(2)}, u32[]{:S(2)}) %collective-permute-start.4) | collective-permute-done | bytes 720928 | tf_op jit(solution)/shard_map/ppermute | solution.py:827
  267.4 17.9 %rows_matmul.37 = f32[1,512,2048]{2,1,0:T(8,128)S(1)} custom-call(s32[2]{0:T(128)S(1)} %pad_add_fusion.2.at, bf16[1,2048,1024]{2,1,0:T(8,128)(2,1)S(1)} %copy-done.3, bf16[2048,1024]{1,0:T(8,128)(2,1)} %all-gather.12.cloned.1.call-done.refs_1_), custom_call_target="tpu_custom_call" | custom-call | tf_op jit(solution)/shard_map/rows_matmul/pallas_call | solution.py:509
  285.3 25.7 %collective-permute-done.6 = bf16[1,512,2048]{2,1,0:T(8,128)(2,1)S(1)} collective-permute-done((bf16[1,512,2048]{2,1,0:T(8,128)(2,1)}, bf16[1,512,2048]{2,1,0:T(8,128)(2,1)S(1)}, u32[]{:S(2)}, u32[]{:S(2)}) %collective-permute-start.6) | collective-permute-done | bytes 2097184 | tf_op jit(solution)/shard_map/ppermute | solution.py:824
  337.7 16.5 %collective-permute-done.7 = bf16[1,512,2048]{2,1,0:T(8,128)(2,1)} collective-permute-done((bf16[1,512,2048]{2,1,0:T(8,128)(2,1)}, bf16[1,512,2048]{2,1,0:T(8,128)(2,1)}, u32[]{:S(2)}, u32[]{:S(2)}) %collective-permute-start.7) | collective-permute-done | bytes 2097184 | tf_op jit(solution)/shard_map/ppermute | solution.py:824
  385.7 13.9 %collective-permute-done.8.moved = bf16[1,512,2048]{2,1,0:T(8,128)(2,1)} collective-permute-done((bf16[1,512,2048]{2,1,0:T(8,128)(2,1)}, bf16[1,512,2048]{2,1,0:T(8,128)(2,1)}, u32[]{:S(2)}, u32[]{:S(2)}) %collective-permute-start.8) | collective-permute-done | bytes 2097184 | tf_op jit(solution)/shard_map/ppermute | solution.py:824
  406.9 12.3 %mlp_block.4 = (bf16[512,1408]{1,0:T(8,128)(2,1)}, bf16[512,2816]{1,0:T(8,128)(2,1)}) custom-call(bf16[512,2048]{1,0:T(8,128)(2,1)} %bitcast.11.x, bf16[2048,2816]{1,0:T(8,128)(2,1)} %all-gather.14.cloned.1.call-done.wgu.refs_1_, f32[512,1408]{1,0:T(8,128)} %bitcast.75), custom_call_target="tpu_custom_call" | custom-call | tf_op jit(solution)/shard_map/mlp_block/pallas_call | solution.py:623
  419.2 12.3 %mlp_block.5 = (bf16[512,1408]{1,0:T(8,128)(2,1)}, bf16[512,2816]{1,0:T(8,128)(2,1)}) custom-call(bf16[512,2048]{1,0:T(8,128)(2,1)} %bitcast.11.x, bf16[2048,2816]{1,0:T(8,128)(2,1)} %all-gather.20.cloned.1.call-done.wgu.refs_3_, f32[512,1408]{1,0:T(8,128)} %bitcast.77), custom_call_target="tpu_custom_call" | custom-call | tf_op jit(solution)/shard_map/mlp_block/pallas_call | solution.py:623
  431.5 18.8 %rows_matmul.44.own = f32[1,512,2048]{2,1,0:T(8,128)} custom-call(s32[2]{0:T(128)} %copy-done.66, bf16[1,512,2816]{2,1,0:T(8,128)(2,1)} %bitcast.50, bf16[2048,2816]{1,0:T(8,128)(2,1)} %all-gather.14.cloned.1.call-done.wgu.refs_1_, bf16[1,512,2816]{2,1,0:T(8,128)(2,1)} %bitcast.56, bf16[2048,2816]{1,0:T(8,128)(2,1)} %all-gather.20.cloned.1.call-done.wgu.refs_3_), custom_call_target="tpu_custom_call" | custom-call | tf_op jit(solution)/shard_map/rows_matmul/pallas_call | solution.py:509
  450.4 12.3 %mlp_block.6 = (bf16[512,1408]{1,0:T(8,128)(2,1)}, bf16[512,2816]{1,0:T(8,128)(2,1)}) custom-call(bf16[512,2048]{1,0:T(8,128)(2,1)} %bitcast.18.x, bf16[2048,2816]{1,0:T(8,128)(2,1)} %all-gather.14.cloned.1.call-done.wgu.refs_1_, f32[512,1408]{1,0:T(8,128)} %bitcast.74), custom_call_target="tpu_custom_call" | custom-call | tf_op jit(solution)/shard_map/mlp_block/pallas_call | solution.py:623
  462.7 12.7 %mlp_block.7 = (bf16[512,1408]{1,0:T(8,128)(2,1)}, bf16[512,2816]{1,0:T(8,128)(2,1)}) custom-call(bf16[512,2048]{1,0:T(8,128)(2,1)} %bitcast.18.x, bf16[2048,2816]{1,0:T(8,128)(2,1)} %all-gather.20.cloned.1.call-done.wgu.refs_3_, f32[512,1408]{1,0:T(8,128)} %bitcast.76), custom_call_target="tpu_custom_call" | custom-call | tf_op jit(solution)/shard_map/mlp_block/pallas_call | solution.py:623
  475.4 18.7 %rows_matmul.45 = bf16[1,512,2048]{2,1,0:T(8,128)(2,1)} custom-call(s32[2]{0:T(128)} %copy-done.66, bf16[1,512,2816]{2,1,0:T(8,128)(2,1)} %bitcast.53, bf16[2048,2816]{1,0:T(8,128)(2,1)} %all-gather.14.cloned.1.call-done.wgu.refs_1_, bf16[1,512,2816]{2,1,0:T(8,128)(2,1)} %bitcast.59, bf16[2048,2816]{1,0:T(8,128)(2,1)} %all-gather.20.cloned.1.call-done.wgu.refs_3_), custom_call_target="tpu_custom_call" | custom-call | tf_op jit(solution)/shard_map/rows_matmul/pallas_call | solution.py:509
  506.3 12.2 %outer_sum.16 = bf16[1024,2816]{1,0:T(8,128)(2,1)} custom-call(s32[3]{0:T(128)S(1)} %stack.57.at, bf16[1,512,2048]{2,1,0:T(8,128)(2,1)} %get-tuple-element.268.refs_0_, bf16[1,512,2048]{2,1,0:T(8,128)(2,1)} %collective-permute-done.9.refs_1_, bf16[1,512,2816]{2,1,0:T(8,128)(2,1)S(1)} %bitcast.57, bf16[1,512,2816]{2,1,0:T(8,128)(2,1)S(1)} %bitcast.60), custom_call_target="tpu_custom_call" | custom-call | tf_op jit(solution)/shard_map/outer_sum/pallas_call | solution.py:579
  518.5 11.7 %rows_matmul.47 = bf16[1,512,2048]{2,1,0:T(8,128)(2,1)} custom-call(s32[2]{0:T(128)} %copy-done.66, bf16[1,512,1408]{2,1,0:T(8,128)(2,1)} %bitcast.62, bf16[2048,1408]{1,0:T(8,128)(2,1)} %all-gather.16.cloned.1.call-done.refs_1_, bf16[1,512,1408]{2,1,0:T(8,128)(2,1)} %bitcast.65, bf16[2048,1408]{1,0:T(8,128)(2,1)} %all-gather.18.cloned.1.call-done.refs_1_.refs_3_), custom_call_target="tpu_custom_call" | custom-call | tf_op jit(solution)/shard_map/rows_matmul/pallas_call | solution.py:509
  530.2 12.1 %rows_matmul.46.own = f32[1,512,2048]{2,1,0:T(8,128)} custom-call(s32[2]{0:T(128)} %copy-done.66, bf16[1,512,1408]{2,1,0:T(8,128)(2,1)} %bitcast.68, bf16[2048,1408]{1,0:T(8,128)(2,1)} %all-gather.16.cloned.1.call-done.refs_1_, bf16[1,512,1408]{2,1,0:T(8,128)(2,1)} %bitcast.71, bf16[2048,1408]{1,0:T(8,128)(2,1)} %all-gather.18.cloned.1.call-done.refs_1_.refs_3_), custom_call_target="tpu_custom_call" | custom-call | tf_op jit(solution)/shard_map/rows_matmul/pallas_call | solution.py:509
  542.3 10.1 middle_back_kernel.1
  561.9 12.2 %outer_sum.20 = bf16[1024,2816]{1,0:T(8,128)(2,1)} custom-call(s32[3]{0:T(128)S(1)} %stack.57.at, bf16[1,512,2048]{2,1,0:T(8,128)(2,1)} %get-tuple-element.268.refs_0_, bf16[1,512,2048]{2,1,0:T(8,128)(2,1)} %collective-permute-done.9.refs_1_, bf16[1,512,2816]{2,1,0:T(8,128)(2,1)S(1)} %bitcast.51, bf16[1,512,2816]{2,1,0:T(8,128)(2,1)S(1)} %bitcast.54), custom_call_target="tpu_custom_call" | custom-call | tf_op jit(solution)/shard_map/outer_sum/pallas_call | solution.py:579
  585.8 13.2 %outer_sum.18 = bf16[1024,2816]{1,0:T(8,128)(2,1)} custom-call(s32[3]{0:T(128)S(1)} %stack.59.at, bf16[1,512,2048]{2,1,0:T(8,128)(2,1)} %get-tuple-element.268.refs_0_, bf16[1,512,2048]{2,1,0:T(8,128)(2,1)} %collective-permute-done.9.refs_1_, bf16[1,512,2816]{2,1,0:T(8,128)(2,1)S(1)} %bitcast.58, bf16[1,512,2816]{2,1,0:T(8,128)(2,1)S(1)} %bitcast.61, ...), custom_call_target="tpu_custom_call" | custom-call | tf_op jit(solution)/shard_map/outer_sum/pallas_call | solution.py:579
  604.4 12.5 %collective-permute-done.16.refs_4_ = bf16[1024,1408]{1,0:T(8,128)(2,1)S(1)} collective-permute-done((bf16[1024,1408]{1,0:T(8,128)(2,1)}, bf16[1024,1408]{1,0:T(8,128)(2,1)S(1)}, u32[]{:S(2)}, u32[]{:S(2)}) %collective-permute-start.16) | collective-permute-done | bytes 2883616 | tf_op jit(solution)/shard_map/ppermute | solution.py:833
  633.4 13.1 %outer_sum.22 = bf16[1024,2816]{1,0:T(8,128)(2,1)} custom-call(s32[3]{0:T(128)S(1)} %stack.59.at, bf16[1,512,2048]{2,1,0:T(8,128)(2,1)} %get-tuple-element.268.refs_0_, bf16[1,512,2048]{2,1,0:T(8,128)(2,1)} %collective-permute-done.9.refs_1_, bf16[1,512,2816]{2,1,0:T(8,128)(2,1)S(1)} %bitcast.52, bf16[1,512,2816]{2,1,0:T(8,128)(2,1)S(1)} %bitcast.55, ...), custom_call_target="tpu_custom_call" | custom-call | tf_op jit(solution)/shard_map/outer_sum/pallas_call | solution.py:579
  717.9 85.7 %mixer_backward.1 = (bf16[1,2048,1152]{2,1,0:T(8,128)(2,1)}, bf16[1,2048,2048]{2,1,0:T(8,128)(2,1)}, f32[8,512]{1,0:T(8,128)S(1)}, f32[8,512]{1,0:T(8,128)S(1)},...) custom-call(f32[1,2048,1024]{2,1,0:T(8,128)} %rows_matmul.51.dm, ...), custom_call_target="tpu_custom_call" | custom-call | bytes 315000000 | tf_op jit(solution)/shard_map/mixer_backward/pallas_call | solution.py:419
  812.6 13.6 %rows_matmul.52 = (bf16[1,512,2048]{2,1,0:T(8,128)(2,1)}, f32[1,8,2048]{2,1,0:T(8,128)}) custom-call(s32[2]{0:T(128)} %pad_add_fusion.3.at, bf16[1,2048,1152]{2,1,0:T(8,128)(2,1)} %get-tuple-element.380.refs_0_.refs_4_.refs_5_.refs_6_.refs_7_, bf16[2048,1152]{1,0:T(8,128)(2,1)} %all-gather.8.cloned.1.call-done.refs_1_, ...), custom_call_target="tpu_custom_call" | custom-call | tf_op jit(solution)/shard_map/rows_matmul/pallas_call | solution.py:509
  826.3 16.0 %outer_sum.26 = (bf16[256,2048]{1,0:T(8,128)(2,1)}, bf16[256,2048]{1,0:T(8,128)(2,1)}, bf16[256,2048]{1,0:T(8,128)(2,1)}, bf16[256,2048]{1,0:T(8,128)(2,1)}) custom-call(s32[5]{0:T(128)S(1)} %stack.63.at, bf16[1,512,2048]{2,1,0:T(8,128)(2,1)S(1)} %copy-done.8, bf16[1,512,2048]{2,1,0:T(8,128)(2,1)} %collective-permute-done.refs_0_.refs_4_.refs_1_, ...), custom_call_target="tpu_custom_call" | custom-call | tf_op jit(solution)/shard_map/outer_sum/pallas_call | solution.py:579
  843.5 13.5 %rows_matmul.53 = (bf16[1,512,2048]{2,1,0:T(8,128)(2,1)}, f32[1,8,2048]{2,1,0:T(8,128)}) custom-call(s32[2]{0:T(128)} %copy-done.75, bf16[1,2048,1152]{2,1,0:T(8,128)(2,1)} %get-tuple-element.380.refs_0_.refs_4_.refs_5_.refs_6_.refs_7_, bf16[2048,1152]{1,0:T(8,128)(2,1)} %all-gather.8.cloned.1.call-done.refs_1_, ...), custom_call_target="tpu_custom_call" | custom-call | tf_op jit(solution)/shard_map/rows_matmul/pallas_call | solution.py:509
  857.0 16.2 %outer_sum.27 = bf16[1024,2048]{1,0:T(8,128)(2,1)} custom-call(s32[5]{0:T(128)S(1)} %stack.62.at, bf16[1,512,2048]{2,1,0:T(8,128)(2,1)S(1)} %copy-done.8, bf16[1,512,2048]{2,1,0:T(8,128)(2,1)} %collective-permute-done.refs_0_.refs_4_.refs_1_, bf16[1,512,2048]{2,1,0:T(8,128)(2,1)} %collective-permute-done.1.refs_0_.refs_4_.refs_2_, ...), custom_call_target="tpu_custom_call" | custom-call | tf_op jit(solution)/shard_map/outer_sum/pallas_call | solution.py:579
  882.0 11.9 %outer_sum.28 = (bf16[512,1152]{1,0:T(8,128)(2,1)}, bf16[512,1152]{1,0:T(8,128)(2,1)}) custom-call(s32[5]{0:T(128)S(1)} %stack.63.at, bf16[1,512,2048]{2,1,0:T(8,128)(2,1)S(1)} %copy-done.9, bf16[1,512,2048]{2,1,0:T(8,128)(2,1)} %collective-permute-done.refs_0_.refs_4_.refs_1_, bf16[1,512,2048]{2,1,0:T(8,128)(2,1)} %collective-permute-done.1.refs_0_.refs_4_.refs_2_, ...), custom_call_target="tpu_custom_call" | custom-call | tf_op jit(solution)/shard_map/outer_sum/pallas_call | solution.py:579
  900.7 13.5 %rows_matmul.54 = (bf16[1,512,2048]{2,1,0:T(8,128)(2,1)}, f32[1,8,2048]{2,1,0:T(8,128)}) custom-call(s32[2]{0:T(128)} %copy-done.74, bf16[1,2048,1152]{2,1,0:T(8,128)(2,1)} %get-tuple-element.380.refs_0_.refs_4_.refs_5_.refs_6_.refs_7_, bf16[2048,1152]{1,0:T(8,128)(2,1)} %all-gather.8.cloned.1.call-done.refs_1_, ...), custom_call_target="tpu_custom_call" | custom-call | tf_op jit(solution)/shard_map/rows_matmul/pallas_call | solution.py:509
  921.6 11.8 %outer_sum.29 = bf16[1024,1152]{1,0:T(8,128)(2,1)} custom-call(s32[5]{0:T(128)S(1)} %stack.62.at, bf16[1,512,2048]{2,1,0:T(8,128)(2,1)S(1)} %copy-done.10, bf16[1,512,2048]{2,1,0:T(8,128)(2,1)} %collective-permute-done.refs_0_.refs_4_.refs_1_, bf16[1,512,2048]{2,1,0:T(8,128)(2,1)} %collective-permute-done.1.refs_0_.refs_4_.refs_2_, ...), custom_call_target="tpu_custom_call" | custom-call | tf_op jit(solution)/shard_map/outer_sum/pallas_call | solution.py:579
  942.7 14.2 %rows_matmul.55 = (f32[1,512,2048]{2,1,0:T(8,128)}, f32[1,8,2048]{2,1,0:T(8,128)}) custom-call(s32[2]{0:T(128)} %copy-done.73, bf16[1,2048,1152]{2,1,0:T(8,128)(2,1)} %get-tuple-element.380.refs_0_.refs_4_.refs_5_.refs_6_.refs_7_, bf16[2048,1152]{1,0:T(8,128)(2,1)} %all-gather.8.cloned.1.call-done.refs_1_, ...), custom_call_target="tpu_custom_call" | custom-call | tf_op jit(solution)/shard_map/rows_matmul/pallas_call | solution.py:509
  (418 shorter events, 424.3 us)
Async XLA Ops:
  7.2 60.4 %all-gather.8.cloned.1.call-start = ((), (), s32[]{:S(2)}) async-start(), calls=%async_computation.6 | async-start | bytes 5308416 | tf_op jit(solution)/shard_map/all_gather | solution.py:830
  13.3 110.6 %all-gather.10.cloned.1.call-start = ((), (), s32[]{:S(2)}) async-start(), calls=%async_computation.7 | async-start | bytes 9437184 | tf_op jit(solution)/shard_map/all_gather | solution.py:830
  15.6 244.4 %all-gather.12.cloned.1.call-start = ((), (), s32[]{:S(2)}) async-start(), calls=%async_computation.8 | async-start | bytes 4718592 | tf_op jit(solution)/shard_map/all_gather | solution.py:830
  15.6 50.8 %collective-permute-start = (bf16[1,512,2048]{2,1,0:T(8,128)(2,1)S(1)}, bf16[1,512,2048]{2,1,0:T(8,128)(2,1)}, u32[]{:S(2)}, u32[]{:S(2)}) collective-permute-start(bf16[1,512,2048]{2,1,0:T(8,128)(2,1)S(1)} %enter_kernel.1.refs_0_.refs_4_), channel_id=1, source_target_pairs={{0,1},{1,2},{2,3},{3,0},{4,5},{5,6},{6,7},{7,4},{8,9},{9,10},{10,1... | collective-permute-start | bytes 6291464 | tf_op jit(solution)/shard_map/ppermute | solution.py:824
  18.7 302.1 %all-gather.16.cloned.1.call-start = ((), (), s32[]{:S(2)}) async-start(), calls=%async_computation.10 | async-start | bytes 6488064 | tf_op jit(solution)/shard_map/all_gather | solution.py:830
  66.5 48.9 %collective-permute-start.1 = (bf16[1,512,2048]{2,1,0:T(8,128)(2,1)}, bf16[1,512,2048]{2,1,0:T(8,128)(2,1)}, u32[]{:S(2)}, u32[]{:S(2)}) collective-permute-start(bf16[1,512,2048]{2,1,0:T(8,128)(2,1)} %collective-permute-done.refs_0_.refs_4_.refs_1_), channel_id=1, source_target_pairs={{0,1},{1,2},{2,3},{3,0},{4,5},{5,6},{6,7},{7,4},{8,9},{9,10},{10,1... | collective-permute-start | bytes 6291464 | tf_op jit(solution)/shard_map/ppermute | solution.py:824
  115.4 48.9 %collective-permute-start.2 = (bf16[1,512,2048]{2,1,0:T(8,128)(2,1)}, bf16[1,512,2048]{2,1,0:T(8,128)(2,1)}, u32[]{:S(2)}, u32[]{:S(2)}) collective-permute-start(bf16[1,512,2048]{2,1,0:T(8,128)(2,1)} %collective-permute-done.1.refs_0_.refs_4_.refs_2_), channel_id=1, source_target_pairs={{0,1},{1,2},{2,3},{3,0},{4,5},{5,6},{6,7},{7,4},{8,9},{9,10},{10,1... | collective-permute-start | bytes 6291464 | tf_op jit(solution)/shard_map/ppermute | solution.py:824
  164.3 189.9 %all-gather.14.cloned.1.call-start = ((), (), s32[]{:S(2)}) async-start(), calls=%async_computation.9 | async-start | bytes 12976128 | tf_op jit(solution)/shard_map/all_gather | solution.py:830
  164.9 204.0 %all-gather.18.cloned.1.call-start = ((), (), s32[]{:S(2)}) async-start(), calls=%async_computation.11 | async-start | bytes 6488064 | tf_op jit(solution)/shard_map/all_gather | solution.py:830
  165.3 93.3 %collective-permute-start.5 = (bf16[1,512,2048]{2,1,0:T(8,128)(2,1)S(1)}, bf16[1,512,2048]{2,1,0:T(8,128)(2,1)}, u32[]{:S(2)}, u32[]{:S(2)}) collective-permute-start(bf16[1,512,2048]{2,1,0:T(8,128)(2,1)S(1)} %copy-done.11), channel_id=1, source_target_pairs={{0,1},{1,0},{2,3},{3,2},{4,5},{5,4},{6,7},{7,6},{8,9},{9,8},{10,11... | collective-permute-start | bytes 6291464 | tf_op jit(solution)/shard_map/ppermute | solution.py:824
  165.4 93.2 %collective-permute-start.3 = (bf16[256,2816]{1,0:T(8,128)(2,1)}, bf16[256,2816]{1,0:T(8,128)(2,1)}, u32[]{:S(2)}, u32[]{:S(2)}) collective-permute-start(bf16[256,2816]{1,0:T(8,128)(2,1)} %slice_dynamic-update-slice_fusion), channel_id=1, source_target_pairs={{0,2},{1,3},{2,0},{3,1},{4,6},{5,7},{6,4},{7,5},{8,10},{9,11},{10,... | collective-permute-start | bytes 4325384 | tf_op jit(solution)/shard_map/ppermute | solution.py:827
  165.5 93.1 %collective-permute-start.4 = (bf16[256,1408]{1,0:T(8,128)(2,1)S(1)}, bf16[256,1408]{1,0:T(8,128)(2,1)}, u32[]{:S(2)}, u32[]{:S(2)}) collective-permute-start(bf16[256,1408]{1,0:T(8,128)(2,1)S(1)} %copy-done.82), channel_id=1, source_target_pairs={{0,2},{1,3},{2,0},{3,1},{4,6},{5,7},{6,4},{7,5},{8,10},{9,11},{10,... | collective-permute-start | bytes 2162696 | tf_op jit(solution)/shard_map/ppermute | solution.py:827
  258.6 160.6 %all-gather.20.cloned.1.call-start = ((), (), s32[]{:S(2)}) async-start(), calls=%async_computation.12 | async-start | bytes 12976128 | tf_op jit(solution)/shard_map/all_gather | solution.py:830
  259.4 450.3 %reduce-scatter.9.cloned.1.call-start = ((), (), s32[]{:S(2)}) async-start(), calls=%async_computation.14 | async-start | bytes 3604480 | tf_op jit(solution)/shard_map/reduce_scatter | solution.py:841
  267.3 43.7 %collective-permute-start.6 = (bf16[1,512,2048]{2,1,0:T(8,128)(2,1)}, bf16[1,512,2048]{2,1,0:T(8,128)(2,1)S(1)}, u32[]{:S(2)}, u32[]{:S(2)}) collective-permute-start(bf16[1,512,2048]{2,1,0:T(8,128)(2,1)} %rows_matmul.36), channel_id=1, source_target_pairs={{0,1},{1,2},{2,3},{3,0},{4,5},{5,6},{6,7},{7,4},{8,9},{9,10},{10,1... | collective-permute-start | bytes 6291464 | tf_op jit(solution)/shard_map/ppermute | solution.py:824
  313.0 41.2 %collective-permute-start.7 = (bf16[1,512,2048]{2,1,0:T(8,128)(2,1)}, bf16[1,512,2048]{2,1,0:T(8,128)(2,1)}, u32[]{:S(2)}, u32[]{:S(2)}) collective-permute-start(bf16[1,512,2048]{2,1,0:T(8,128)(2,1)} %add_convert_fusion.3), channel_id=1, source_target_pairs={{0,1},{1,2},{2,3},{3,0},{4,5},{5,6},{6,7},{7,4},{8,9},{9,10},{10,1... | collective-permute-start | bytes 6291464 | tf_op jit(solution)/shard_map/ppermute | solution.py:824
  406.9 43.5 %collective-permute-start.9 = (bf16[1,512,2048]{2,1,0:T(8,128)(2,1)}, bf16[1,512,2048]{2,1,0:T(8,128)(2,1)}, u32[]{:S(2)}, u32[]{:S(2)}) collective-permute-start(bf16[1,512,2048]{2,1,0:T(8,128)(2,1)} %get-tuple-element.268.refs_0_), channel_id=1, source_target_pairs={{0,1},{1,0},{2,3},{3,2},{4,5},{5,4},{6,7},{7,6},{8,9},{9,8},{10,11... | collective-permute-start | bytes 6291464 | tf_op jit(solution)/shard_map/ppermute | solution.py:824
  494.1 48.2 %collective-permute-start.10 = (bf16[1,512,2048]{2,1,0:T(8,128)(2,1)}, bf16[1,512,2048]{2,1,0:T(8,128)(2,1)}, u32[]{:S(2)}, u32[]{:S(2)}) collective-permute-start(bf16[1,512,2048]{2,1,0:T(8,128)(2,1)} %rows_matmul.45), channel_id=1, source_target_pairs={{0,1},{1,0},{2,3},{3,2},{4,5},{5,4},{6,7},{7,6},{8,9},{9,8},{10,11... | collective-permute-start | bytes 6291464 | tf_op jit(solution)/shard_map/ppermute | solution.py:824
  552.9 49.7 %collective-permute-start.11 = (bf16[1,512,2048]{2,1,0:T(8,128)(2,1)}, bf16[1,512,2048]{2,1,0:T(8,128)(2,1)}, u32[]{:S(2)}, u32[]{:S(2)}) collective-permute-start(bf16[1,512,2048]{2,1,0:T(8,128)(2,1)} %get-tuple-element.301.refs_0_), channel_id=1, source_target_pairs={{0,1},{1,2},{2,3},{3,0},{4,5},{5,6},{6,7},{7,4},{8,9},{9,10},{10,1... | collective-permute-start | bytes 6291464 | tf_op jit(solution)/shard_map/ppermute | solution.py:824
  602.7 109.2 %reduce-scatter.7.cloned.1.call-start = ((), (), s32[]{:S(2)}) async-start(), calls=%async_computation.13 | async-start | bytes 7208960 | tf_op jit(solution)/shard_map/reduce_scatter | solution.py:841
  603.4 276.7 %reduce-scatter.11.cloned.1.call-start = ((), (), s32[]{:S(2)}) async-start(), calls=%async_computation.15 | async-start | bytes 3604480 | tf_op jit(solution)/shard_map/reduce_scatter | solution.py:841
  604.0 50.1 %collective-permute-start.14 = (bf16[1,512,2048]{2,1,0:T(8,128)(2,1)}, bf16[1,512,2048]{2,1,0:T(8,128)(2,1)}, u32[]{:S(2)}, u32[]{:S(2)}) collective-permute-start(bf16[1,512,2048]{2,1,0:T(8,128)(2,1)} %collective-permute-done.11.refs_0_.refs_1_), channel_id=1, source_target_pairs={{0,1},{1,2},{2,3},{3,0},{4,5},{5,6},{6,7},{7,4},{8,9},{9,10},{10,1... | collective-permute-start | bytes 6291464 | tf_op jit(solution)/shard_map/ppermute | solution.py:824
  654.2 225.9 %reduce-scatter.13.cloned.1.call-start = ((), (), s32[]{:S(2)}) async-start(), calls=%async_computation.16 | async-start | bytes 7208960 | tf_op jit(solution)/shard_map/reduce_scatter | solution.py:841
  654.9 278.5 %reduce-scatter.15.cloned.1.call-start = ((), (), s32[]{:S(2)}) async-start(), calls=%async_computation.17 | async-start | bytes 5242880 | tf_op jit(solution)/shard_map/reduce_scatter | solution.py:841
  654.9 48.9 %collective-permute-start.17 = (bf16[1,512,2048]{2,1,0:T(8,128)(2,1)}, bf16[1,512,2048]{2,1,0:T(8,128)(2,1)}, u32[]{:S(2)}, u32[]{:S(2)}) collective-permute-start(bf16[1,512,2048]{2,1,0:T(8,128)(2,1)} %collective-permute-done.14.refs_0_.refs_2_), channel_id=1, source_target_pairs={{0,1},{1,2},{2,3},{3,0},{4,5},{5,6},{6,7},{7,4},{8,9},{9,10},{10,1... | collective-permute-start | bytes 6291464 | tf_op jit(solution)/shard_map/ppermute | solution.py:824
  711.9 99.4 %collective-permute-start.18 = (bf16[1,512,2048]{2,1,0:T(8,128)(2,1)}, bf16[1,512,2048]{2,1,0:T(8,128)(2,1)S(1)}, u32[]{:S(2)}, u32[]{:S(2)}) collective-permute-start(bf16[1,512,2048]{2,1,0:T(8,128)(2,1)} %rows_matmul.47), channel_id=1, source_target_pairs={{0,1},{1,0},{2,3},{3,2},{4,5},{5,4},{6,7},{7,6},{8,9},{9,8},{10,11... | collective-permute-start | bytes 6291464 | tf_op jit(solution)/shard_map/ppermute | solution.py:824
  713.3 96.9 %collective-permute-start.19 = (bf16[256,2816]{1,0:T(8,128)(2,1)}, bf16[256,2816]{1,0:T(8,128)(2,1)S(1)}, u32[]{:S(2)}, u32[]{:S(2)}) collective-permute-start(bf16[256,2816]{1,0:T(8,128)(2,1)} %reduce-scatter.7.cloned.1.call-done), channel_id=1, source_target_pairs={{0,2},{1,3},{2,0},{3,1},{4,6},{5,7},{6,4},{7,5},{8,10},{9,11},{10,... | collective-permute-start | bytes 4325384 | tf_op jit(solution)/shard_map/ppermute | solution.py:827
  715.7 93.6 %collective-permute-start.20 = (bf16[256,1408]{1,0:T(8,128)(2,1)}, bf16[256,1408]{1,0:T(8,128)(2,1)S(1)}, u32[]{:S(2)}, u32[]{:S(2)}) collective-permute-start(bf16[256,1408]{1,0:T(8,128)(2,1)} %reduce-scatter.9.cloned.1.call-done), channel_id=1, source_target_pairs={{0,2},{1,3},{2,0},{3,1},{4,6},{5,7},{6,4},{7,5},{8,10},{9,11},{10,... | collective-permute-start | bytes 2162696 | tf_op jit(solution)/shard_map/ppermute | solution.py:827
  826.2 48.5 %collective-permute-start.21 = (bf16[1,512,2048]{2,1,0:T(8,128)(2,1)}, bf16[1,512,2048]{2,1,0:T(8,128)(2,1)}, u32[]{:S(2)}, u32[]{:S(2)}) collective-permute-start(bf16[1,512,2048]{2,1,0:T(8,128)(2,1)} %get-tuple-element.337), channel_id=1, source_target_pairs={{0,1},{1,2},{2,3},{3,0},{4,5},{5,6},{6,7},{7,4},{8,9},{9,10},{10,1... | collective-permute-start | bytes 6291464 | tf_op jit(solution)/shard_map/ppermute | solution.py:824
  874.8 135.3 %reduce-scatter.17.cloned.1.call-start = ((), (), s32[]{:S(2)}) async-start(), calls=%async_computation.18 | async-start | bytes 5570560 | tf_op jit(solution)/shard_map/reduce_scatter | solution.py:841
  880.1 53.3 %collective-permute-start.26 = (bf16[1,512,2048]{2,1,0:T(8,128)(2,1)}, bf16[1,512,2048]{2,1,0:T(8,128)(2,1)}, u32[]{:S(2)}, u32[]{:S(2)}) collective-permute-start(bf16[1,512,2048]{2,1,0:T(8,128)(2,1)} %add_convert_fusion.1), channel_id=1, source_target_pairs={{0,1},{1,2},{2,3},{3,0},{4,5},{5,6},{6,7},{7,4},{8,9},{9,10},{10,1... | collective-permute-start | bytes 6291464 | tf_op jit(solution)/shard_map/ppermute | solution.py:824
  938.0 50.0 %collective-permute-start.31 = (bf16[1,512,2048]{2,1,0:T(8,128)(2,1)}, bf16[1,512,2048]{2,1,0:T(8,128)(2,1)}, u32[]{:S(2)}, u32[]{:S(2)}) collective-permute-start(bf16[1,512,2048]{2,1,0:T(8,128)(2,1)} %add_convert_fusion), channel_id=1, source_target_pairs={{0,1},{1,2},{2,3},{3,0},{4,5},{5,6},{6,7},{7,4},{8,9},{9,10},{10,1... | collective-permute-start | bytes 6291464 | tf_op jit(solution)/shard_map/ppermute | solution.py:824
  (111 other events, 1601.0 us)
Sparse Core Ops, SparseCore 0:
  13.4 41.6 all-gather.7
  57.6 54.3 all-gather.9
  113.9 36.7 all-gather.11
  164.4 41.2 all-gather.15
  208.0 67.6 all-gather.13
  277.5 43.3 all-gather.17
  322.8 67.6 all-gather.19
  602.8 40.1 reduce-scatter.8
  646.0 65.8 reduce-scatter.6
  714.8 41.7 reduce-scatter.10
  759.5 65.7 reduce-scatter.12
  874.9 51.6 reduce-scatter.14
  942.8 56.4 reduce-scatter.16
